TPU v7x, 256 devices: a whole 4x4x8 slice. The times are simulated.
256 devices in a mesh: band: 16 (over z, core), lev: 16 (over y, x).
Axes of the slice: x: 4, y: 4, z: 8, core: 2. Of those that a mesh axis runs over, the one named last changes fastest.
Arguments:
- spectral: bfloat16 [256, 2, 320, 641], P('lev', None, 'band'), may hold values from -0.29882812 to 0.29882812
- legendre: bfloat16 [320, 128, 641], P('band'), may hold values from -0.3125 to 0.3125
- weights: float32 [128], replicated, may hold values from 2 to 40
- vertical: bfloat16 [256, 256], replicated, may hold values from -0.375 to 0.375
- grid_factor: bfloat16 [256, 2688], P('band'), may hold values from 0.29882812 to 3
- points: int32 [128], replicated, may hold values from 20 to 2576, as said below
- cutoffs: int32 [128], replicated, may hold values from 6 to 639, as said below
- row_latitude: int32 [256], replicated, may hold values from 0 to 255, each once
- slot_pair: int32 [320], replicated, may hold values from 0 to 319, each once
Outputs:
- grid_field: bfloat16 [256, 256, 2688], P('band', 'lev')
- round_trip: float32 [256, 2, 320, 641], P('lev', None, 'band')
Inputs may be any that keep to these rules, and one draw needn't show every extreme that they name: points: 4 r + 16 for a cycle number r of 1 to 640; some latitude has 2576 points. cutoffs: at most min(639, (points - 1) // 2) of the same latitude; some latitude keeps 639. `row_latitude`: a permutation; latitudes below 128 are northern, latitude 128 + j mirrors j. `slot_pair`: a permutation; pair k joins wavenumbers k and 639 - k.
All inputs are finite; a program needn't handle non-finite values.
Results may differ from a plain program's by a relative error of at most 0.008.
Values may be sent and summed in bfloat16 or wider, within the bound.
No kernel may reach another device: no remote copies, remote signals or barrier semaphores. Data moves between devices by JAX's collectives and lax.ppermute only.
A program may use at most 128 MiB of HBM per device.

v0:
```python
from functools import partial
import math

import jax
import jax.numpy as jnp
from jax import lax
from jax.sharding import PartitionSpec as P


def class_masks(pair_ids, truncation, width):
    column = jnp.arange(width, dtype=jnp.int32)[None, :]
    split_at = (truncation + 1 - pair_ids)[:, None]
    first_part = column < split_at
    parity = jnp.where(first_part, column, column - split_at) % 2
    category = jnp.where(first_part, 0, 2) + parity
    return (category[None] == jnp.arange(4, dtype=jnp.int32)[:, None, None]).astype(jnp.float32)


def mirror_fold(legendre_sums):
    north_rows = jnp.stack(
        [legendre_sums[0] + legendre_sums[1], legendre_sums[2] + legendre_sums[3]], 3
    )
    south_rows = jnp.stack(
        [legendre_sums[0] - legendre_sums[1], legendre_sums[2] - legendre_sums[3]], 3
    )
    return jnp.concatenate([north_rows, south_rows], 0)


def paired_classes(placed, weights):
    half_count = weights.shape[0]
    north_rows = placed[:half_count].astype(jnp.float32)
    south_rows = placed[half_count:].astype(jnp.float32)
    weighting = weights[:, None, None, None, None]
    even_part = (north_rows + south_rows) * weighting
    odd_part = (north_rows - south_rows) * weighting
    return jnp.stack(
        [even_part[:, :, :, 0], odd_part[:, :, :, 0], even_part[:, :, :, 1], odd_part[:, :, :, 1]],
        0,
    )


def phase_tables(wavenumbers, row_points, outer_count):
    inner_index = jnp.arange(128, dtype=jnp.int32)
    outer_index = jnp.arange(outer_count, dtype=jnp.int32)
    unit_angle = 2.0 * math.pi / row_points.astype(jnp.float32)
    inner_angle = (wavenumbers[:, None] * inner_index[None, :] % row_points).astype(
        jnp.float32
    ) * unit_angle
    outer_angle = (wavenumbers[:, None] * (128 * outer_index)[None, :] % row_points).astype(
        jnp.float32
    ) * unit_angle
    inner_cos = jnp.cos(inner_angle).astype(jnp.bfloat16)
    inner_sin = jnp.sin(inner_angle).astype(jnp.bfloat16)
    return (inner_cos, inner_sin, jnp.cos(outer_angle).T, jnp.sin(outer_angle).T)


def inverse_row(
    fourier_row,
    row_points,
    row_cutoff,
    inner_cos,
    inner_sin,
    outer_cos,
    outer_sin,
    wavenumbers,
    row_width,
):
    doubling = jnp.where(wavenumbers == 0, jnp.float32(1.0), jnp.float32(2.0))
    values = fourier_row.astype(jnp.float32) * (
        doubling * (wavenumbers <= row_cutoff).astype(jnp.float32)
    )
    real_part = values[:, 0, None, :] * outer_cos[None] - values[:, 1, None, :] * outer_sin[None]
    imag_part = values[:, 0, None, :] * outer_sin[None] + values[:, 1, None, :] * outer_cos[None]
    twisted = jnp.concatenate([real_part, -imag_part], 2).astype(jnp.bfloat16)
    table = jnp.concatenate([inner_cos, inner_sin], 0)
    samples = jnp.einsum("lqm,mp->lqp", twisted, table, preferred_element_type=jnp.float32)
    samples = samples.reshape(samples.shape[0], row_width)
    inside = jnp.arange(row_width, dtype=jnp.int32) < row_points
    return jnp.where(inside[None, :], samples, jnp.float32(0.0)).astype(jnp.bfloat16)


def direct_row(
    samples, row_points, row_cutoff, inner_cos, inner_sin, outer_cos, outer_sin, wavenumbers
):
    level_total, row_width = samples.shape
    outer_count = row_width // 128
    table = jnp.concatenate([inner_cos, -inner_sin], 0)
    blocks = samples.reshape(level_total, outer_count, 128)
    partial_sums = jnp.einsum("lqp,mp->lqm", blocks, table, preferred_element_type=jnp.float32)
    wave_total = wavenumbers.shape[0]
    cos_part = partial_sums[:, :, :wave_total]
    sin_part = partial_sums[:, :, wave_total:]
    real_sum = jnp.sum(cos_part * outer_cos[None] + sin_part * outer_sin[None], 1)
    imag_sum = jnp.sum(sin_part * outer_cos[None] - cos_part * outer_sin[None], 1)
    factor = (wavenumbers <= row_cutoff).astype(jnp.float32) / row_points.astype(jnp.float32)
    return (jnp.stack([real_sum, imag_sum], 1) * factor[None, None, :]).astype(jnp.bfloat16)


def rowwise(function, inputs):
    row_total = inputs[0].shape[0]
    block_rows = math.gcd(row_total, 8)

    def reshaped(array):
        return array.reshape((row_total // block_rows, block_rows) + array.shape[1:])

    def one_block(block_inputs):
        return jax.vmap(function)(*block_inputs)

    result = lax.map(one_block, tuple((reshaped(item) for item in inputs)))
    return result.reshape((row_total,) + result.shape[2:])


def per_device(
    spectral, legendre, weights, vertical, grid_factor, points, cutoffs, row_latitude, slot_pair
):
    band_index = lax.axis_index("band")
    band_count = lax.axis_size("band")
    level_index = lax.axis_index("lev")
    slot_count = spectral.shape[2]
    level_count = spectral.shape[0]
    north_count = points.shape[0]
    row_count = grid_factor.shape[0]
    row_width = grid_factor.shape[1]
    truncation = 2 * slot_pair.shape[0] - 1
    own_pairs = lax.dynamic_slice_in_dim(slot_pair, band_index * slot_count, slot_count)
    selectors = class_masks(own_pairs, truncation, spectral.shape[3])
    masked = spectral[None] * selectors[:, None, None].astype(jnp.bfloat16)
    legendre_sums = jnp.einsum(
        "qlrsc,sjc->qjlrs", masked, legendre, preferred_element_type=jnp.float32
    )
    by_latitude = mirror_fold(legendre_sums).astype(jnp.bfloat16)
    by_row = jnp.take(by_latitude, row_latitude, axis=0)
    received = lax.all_to_all(
        by_row.reshape(by_row.shape[0], 1, -1), "band", split_axis=0, concat_axis=1, tiled=True
    )
    received = received.reshape(row_count, band_count, level_count, 2, 2, slot_count)
    fourier = received.transpose(0, 2, 3, 1, 4, 5).reshape(row_count, level_count, 2, -1)
    pair_table = slot_pair.reshape(band_count, slot_count)
    wavenumbers = jnp.stack([pair_table, truncation - pair_table], 1).reshape(-1)
    own_rows = (
        lax.dynamic_slice_in_dim(row_latitude, band_index * row_count, row_count) % north_count
    )
    one_hot = (own_rows[:, None] == jnp.arange(north_count, dtype=jnp.int32)[None, :]).astype(
        jnp.int32
    )
    points_row = jnp.sum(one_hot * points[None, :], 1)
    cutoff_row = jnp.sum(one_hot * cutoffs[None, :], 1)
    inner_cos, inner_sin, outer_cos, outer_sin = jax.vmap(phase_tables, in_axes=(None, 0, None))(
        wavenumbers, points_row, row_width // 128
    )
    grid_field = rowwise(
        partial(inverse_row, wavenumbers=wavenumbers, row_width=row_width),
        (fourier, points_row, cutoff_row, inner_cos, inner_sin, outer_cos, outer_sin),
    )
    columns = lax.all_to_all(grid_field, "lev", split_axis=2, concat_axis=1, tiled=True)
    mixture = jnp.einsum("ak,bkp->bap", vertical, columns, preferred_element_type=jnp.float32)
    column_count = columns.shape[2]
    factor_columns = lax.dynamic_slice_in_dim(
        grid_factor, level_index * column_count, column_count, 1
    )
    product = (factor_columns[:, None, :].astype(jnp.float32) * mixture).astype(jnp.bfloat16)
    samples = lax.all_to_all(product, "lev", split_axis=1, concat_axis=2, tiled=True)
    harmonic = rowwise(
        partial(direct_row, wavenumbers=wavenumbers),
        (samples, points_row, cutoff_row, inner_cos, inner_sin, outer_cos, outer_sin),
    )
    outgoing = harmonic.reshape(row_count, level_count, 2, band_count, 2, slot_count)
    outgoing = outgoing.transpose(0, 3, 1, 2, 4, 5).reshape(row_count, band_count, -1)
    returned = lax.all_to_all(outgoing, "band", split_axis=1, concat_axis=0, tiled=True)
    returned = returned.reshape(returned.shape[0], level_count, 2, 2, slot_count)
    row_total = row_latitude.shape[0]
    inverse_order = (
        jnp.zeros((row_total,), jnp.int32)
        .at[row_latitude]
        .set(jnp.arange(row_total, dtype=jnp.int32))
    )
    placed = jnp.take(returned, inverse_order, axis=0)
    parts = paired_classes(placed, weights).astype(jnp.bfloat16)
    projected = jnp.einsum("qjlrs,sjc->qlrsc", parts, legendre, preferred_element_type=jnp.float32)
    round_trip = jnp.sum(selectors[:, None, None] * projected, 0)
    return (grid_field, round_trip)


def solution(mesh):
    in_specs = (
        P("lev", None, "band", None),
        P("band", None, None),
        P(),
        P(),
        P("band", None),
        P(),
        P(),
        P(),
        P(),
    )
    out_specs = (P("band", "lev", None), P("lev", None, "band", None))
    return jax.shard_map(
        per_device, mesh=mesh, in_specs=in_specs, out_specs=out_specs, check_vma=False
    )
```

profile of v0, /device:TPU:1, one launch (start us, length us, event | category | flops | bytes accessed | tf_op | source)
XLA Modules:
  0.0 485.3 jit_solution(14778868581855503409)
XLA Ops:
  6.3 7.8 %copy.97 = bf16[256,16,2,2,20]{4,1,3,2,0:T(8,128)(2,1)} copy(bf16[256,16,2,2,20]{0,1,2,4,3:T(8,128)(2,1)} %maximum_maximum_fusion) | data formatting | bytes 1310720 | tf_op jit(solution)/shard_map/concatenate | solution.py:26
  14.1 5.3 %gather_fusion = bf16[256,16,2,2,20]{4,1,3,2,0:T(8,128)(2,1)} fusion(bf16[256,16,2,2,20]{4,1,3,2,0:T(8,128)(2,1)} %copy.97, s32[1024]{0:T(1024)S(1)} %pad_clamp_fusion.1), kind=kCustom, calls=%fused_computation.clone | custom fusion | bytes 1311744 | tf_op jit(solution)/shard_map/jit(_take)/gather | solution.py:132
  19.4 4.1 broadcast_select_fusion
  23.4 6.4 %copy.98 = bf16[256,16,2,2,20]{0,4,3,2,1:T(8,128)(2,1)} copy(bf16[256,16,2,2,20]{4,1,3,2,0:T(8,128)(2,1)} %broadcast_select_fusion) | data formatting | bytes 1310720 | tf_op jit(solution)/shard_map/jit(_take)/select_n | solution.py:132
  32.4 2.8 reduce
  37.4 2.7 reshape.530
  40.1 10.6 %all-to-all-start = ((bf16[16,2,10240]{2,1,0:T(2,128)(2,1)}), bf16[16,2,10240]{2,1,0:T(2,128)(2,1)}, u32[]{:S(2)}, u32[]{:S(2)}) async-start(bf16[16,2,10240]{2,1,0:T(2,128)(2,1)} %reshape.530), calls=%async_computation | async-start | bytes 1310720 | tf_op jit(solution)/shard_map/all_to_all | solution.py:133
  51.9 14.5 %fusion.45 = (f32[2,8,21,640]{3,2,1,0:T(8,128)}, f32[2,8,21,640]{3,2,1,0:T(8,128)}) fusion(f32[2,8]{1,0:T(2,128)S(1)} %convert_divide_fusion.1, s32[2,8]{1,0:T(2,128)S(1)} %compare_select_fusion.4, s32[21,640]{1,0:T(8,128)S(1)} %broadcast_multiply_fusion, pred[2,8]{1,0:T(4,128)(4,1)S(1)} %broadcast_compare_fusion), kind=kLoop, calls=%fused_computation.85 | loop fusion | flops 1935360 | bytes 1774224 | tf_op jit(solution)/shard_map/vmap()/sin | solution.py:54
  66.4 69.9 %fusion.25 = (bf16[2,8,640,128]{3,2,1,0:T(8,128)(2,1)}, bf16[2,8,640,128]{3,2,1,0:T(8,128)(2,1)}) fusion(f32[2,8]{1,0:T(2,128)S(1)} %convert_divide_fusion.1, s32[2,8]{1,0:T(2,128)S(1)} %compare_select_fusion.4, s32[640,128]{1,0:T(8,128)S(1)} %iota_multiply_fusion, pred[2,8]{1,0:T(4,128)(4,1)S(1)} %broadcast_compare_fusion), kind=kLoop, calls=%fused_computation.63 | loop fusion | flops 14417920 | bytes 5570704 | tf_op jit(solution)/shard_map/vmap()/convert_element_type | solution.py:53
  136.3 5.0 %reshape.531 = bf16[256,1,1280]{2,1,0:T(2,128)(2,1)} reshape(bf16[16,2,10240]{2,1,0:T(2,128)(2,1)} %all-to-all-done) | data formatting | bytes 1310720
  143.5 14.7 %reshape.486 = bf16[16,16,16,2,2,20]{5,4,3,2,0,1:T(2,128)(2,1)} reshape(bf16[16,16,1,1280]{3,0,1,2:T(8,128)(2,1)} %bitcast.199) | data formatting | bytes 1310720 | tf_op jit(solution)/shard_map/reshape | solution.py:136
  158.2 8.0 %copy.134 = bf16[16,16,16,2,2,20]{5,4,1,2,3,0:T(2,128)(2,1)} copy(bf16[16,16,16,2,2,20]{5,4,3,2,0,1:T(2,128)(2,1)} %reshape.486) | data formatting | bytes 1310720 | tf_op jit(solution)/shard_map/reshape | solution.py:136
  166.2 10.9 %reshape_reshape.6 = bf16[2,8,16,2,640]{4,2,3,1,0:T(8,128)(2,1)} reshape(bf16[16,16,2,16,2,20]{5,4,3,1,2,0:T(2,128)(2,1)} %bitcast.196) | data formatting | bytes 1310720 | tf_op jit(solution)/shard_map/reshape;reshape | solution.py:104
  177.2 31.8 %while.22 = (s32[]{:T(128)}, bf16[2,8,16,2688]{3,2,1,0:T(8,128)(2,1)}, s32[2,8]{1,0:T(2,128)S(1)}, bf16[2,8,16,2,640]{4,2,3,1,0:T(8,128)(2,1)}, s32[16,2,20]{2,1...) while((s32[]{:T(128)}, ...), condition=%wide.wide.region_3.5_spmd, body=%wide.wide.region_2.4_spmd.sunk | while | flops 915996928 | bytes 51664256 | solution.py:109
  179.8 3.1 subtract_convert_fusion.5
  184.2 4.6 fusion.94
  195.6 3.1 subtract_convert_fusion.5
  200.0 4.6 fusion.94
  209.0 11.2 %copy.102 = bf16[2,8,16,2688]{2,1,0,3:T(8,128)(2,1)} copy(bf16[2,8,16,2688]{3,2,1,0:T(8,128)(2,1)} %get-tuple-element.112) | data formatting | bytes 2752512 | tf_op jit(solution)/shard_map/while | solution.py:109
  220.1 10.7 %bitcast_bitcast_fusion = bf16[2688,16,16]{2,1,0:T(8,128)(2,1)} fusion(bf16[2,8,16,2688]{2,1,0,3:T(8,128)(2,1)} %copy.102), kind=kLoop, calls=%fused_computation.155 | loop fusion | bytes 2752512
  230.9 13.4 %reshape.532 = bf16[16,2,21504]{2,1,0:T(2,128)(2,1)} reshape(bf16[2688,16,16]{2,1,0:T(8,128)(2,1)} %bitcast_bitcast_fusion) | data formatting | bytes 2752512
  244.3 6.8 %all-to-all-start.1 = ((bf16[16,2,21504]{2,1,0:T(2,128)(2,1)}), bf16[16,2,21504]{2,1,0:T(2,128)(2,1)}, u32[]{:S(2)}, u32[]{:S(2)}) async-start(bf16[16,2,21504]{2,1,0:T(2,128)(2,1)} %reshape.532), calls=%async_computation.1 | async-start | bytes 2752512 | tf_op jit(solution)/shard_map/all_to_all | solution.py:155
  251.9 21.9 %all-to-all-done.1 = bf16[16,2,21504]{2,1,0:T(2,128)(2,1)} async-done(((bf16[16,2,21504]{2,1,0:T(2,128)(2,1)}), bf16[16,2,21504]{2,1,0:T(2,128)(2,1)}, u32[]{:S(2)}, u32[]{:S(2)}) %all-to-all-start.1) | async-done | bytes 1376288 | tf_op jit(solution)/shard_map/all_to_all | solution.py:155
  273.8 10.3 %reshape.533 = bf16[2688,16,16]{2,1,0:T(8,128)(2,1)} reshape(bf16[16,2,21504]{2,1,0:T(2,128)(2,1)} %all-to-all-done.1) | data formatting | bytes 2752512
  284.2 12.5 %copy.103 = bf16[16,16,16,168]{3,1,2,0:T(8,128)(2,1)} copy(bf16[16,16,16,168]{1,0,3,2:T(8,128)(2,1)} %bitcast.195) | data formatting | bytes 2752512 | tf_op jit(solution)/shard_map/all_to_all | solution.py:155
  296.6 3.6 fusion.37
  300.3 4.4 copy.105
  304.7 4.8 all-to-all-start.2
  309.7 30.0 %all-to-all-done.2 = bf16[16,256,168]{2,0,1:T(8,128)(2,1)} async-done(((bf16[16,256,168]{2,0,1:T(8,128)(2,1)}), bf16[16,256,168]{2,0,1:T(8,128)(2,1)}, u32[]{:S(2)}, u32[]{:S(2)}) %all-to-all-start.2) | async-done | bytes 1376288 | tf_op jit(solution)/shard_map/all_to_all | solution.py:162
  339.7 4.1 copy.107
  343.7 5.0 %reshape.489 = bf16[2,8,16,2688]{3,2,1,0:T(8,128)(2,1)} reshape(bf16[16,16,16,168]{3,2,1,0:T(8,128)(2,1)} %copy.107) | data formatting | bytes 2752512 | tf_op jit(solution)/shard_map/reshape | solution.py:104
  348.7 34.7 %while.23 = (s32[]{:T(128)}, bf16[2,8,16,2,640]{4,3,2,1,0:T(2,128)(2,1)}, bf16[2,8,16,2688]{3,2,1,0:T(8,128)(2,1)}, bf16[2,8,640,128]{3,2,1,0:T(8,128)(2,1)}, bf...) while((s32[]{:T(128)}, ...), condition=%wide.wide.region_7.9_spmd, body=%wide.wide.region_4.8_spmd.sunk | while | flops 900807680 | bytes 56790424 | solution.py:109
  348.7 3.6 negate_bitcast_fusion.3
  355.5 4.3 fusion.97
  359.9 4.2 add_reduce_fusion.3
  366.1 3.6 negate_bitcast_fusion.3
  372.8 4.3 fusion.97
  377.3 4.2 add_reduce_fusion.3
  383.4 15.4 %reshape_reshape.7 = bf16[16,16,2,16,2,20]{5,4,3,2,1,0:T(2,128)(2,1)} reshape(bf16[2,8,16,2,640]{4,3,2,1,0:T(2,128)(2,1)} %get-tuple-element.113) | data formatting | bytes 1310720 | tf_op jit(solution)/shard_map/reshape;reshape | solution.py:167
  398.8 8.7 %copy.133 = bf16[16,16,2,16,2,20]{5,4,2,1,3,0:T(2,128)(2,1)} copy(bf16[16,16,2,16,2,20]{5,4,3,2,1,0:T(2,128)(2,1)} %reshape_reshape.7) | data formatting | bytes 1310720 | tf_op jit(solution)/shard_map/reshape;reshape | solution.py:167
  407.6 11.0 %reshape.490 = bf16[16,16,1280]{2,1,0:T(8,128)(2,1)} reshape(bf16[16,16,16,2,2,20]{5,4,3,2,1,0:T(2,128)(2,1)} %bitcast.197) | data formatting | bytes 1310720 | tf_op jit(solution)/shard_map/reshape | solution.py:168
  420.7 6.8 %all-to-all-start.3 = ((bf16[16,16,1280]{2,0,1:T(8,128)(2,1)}), bf16[16,16,1280]{2,0,1:T(8,128)(2,1)}, u32[]{:S(2)}, u32[]{:S(2)}) async-start(bf16[16,16,1280]{2,0,1:T(8,128)(2,1)} %copy.109), calls=%async_computation.3 | async-start | bytes 1310720 | tf_op jit(solution)/shard_map/all_to_all | solution.py:169
  429.1 18.6 %all-to-all-done.3 = bf16[16,16,1280]{2,0,1:T(8,128)(2,1)} async-done(((bf16[16,16,1280]{2,0,1:T(8,128)(2,1)}), bf16[16,16,1280]{2,0,1:T(8,128)(2,1)}, u32[]{:S(2)}, u32[]{:S(2)}) %all-to-all-start.3) | async-done | bytes 655392 | tf_op jit(solution)/shard_map/all_to_all | solution.py:169
  447.7 14.7 %reshape.491 = bf16[256,16,2,2,20]{4,3,2,1,0:T(2,128)(2,1)} reshape(bf16[16,16,1,1280]{3,1,0,2:T(8,128)(2,1)} %bitcast.42) | data formatting | bytes 1310720 | tf_op jit(solution)/shard_map/reshape | solution.py:170
  462.4 5.2 %copy.110 = bf16[256,16,2,2,20]{4,1,3,2,0:T(8,128)(2,1)} copy(bf16[256,16,2,2,20]{4,3,2,1,0:T(2,128)(2,1)} %reshape.491) | data formatting | bytes 1310720 | tf_op jit(solution)/shard_map/reshape | solution.py:170
  467.7 5.2 %gather_fusion.1 = bf16[256,16,2,2,20]{4,1,3,2,0:T(8,128)(2,1)} fusion(bf16[256,16,2,2,20]{4,1,3,2,0:T(8,128)(2,1)} %copy.110, s32[1024]{0:T(1024)S(1)} %pad_clamp_fusion), kind=kCustom, calls=%fused_computation.1.clone | custom fusion | bytes 1311744 | tf_op jit(solution)/shard_map/jit(_take)/gather | solution.py:177
  472.9 6.6 %copy.111 = bf16[256,16,2,2,20]{0,1,2,4,3:T(8,128)(2,1)} copy(bf16[256,16,2,2,20]{4,1,3,2,0:T(8,128)(2,1)} %gather_fusion.1) | data formatting | bytes 1310720 | tf_op jit(solution)/shard_map/jit(_take)/gather | solution.py:177
  482.3 2.8 copy.116
  (123 shorter events, 47.5 us)
Async XLA Ops:
  0.6 3.2 copy-start
  3.8 1.4 copy-start.12
  5.3 14.1 %copy-start.10 = (s32[256]{0:T(256)}, s32[256]{0:T(256)S(1)}, u32[]{:S(2)}) copy-start(s32[256]{0:T(256)S(1)} %compare_select_fusion.3) | copy-start | bytes 3076
  29.8 21.1 %copy-start.14 = (s32[128]{0:T(128)S(1)}, s32[128]{0:T(128)}, u32[]{:S(2)}) copy-start(s32[128]{0:T(128)} %param.21) | copy-start | bytes 1540
  29.8 21.1 %copy-start.15 = (s32[128]{0:T(128)S(1)}, s32[128]{0:T(128)}, u32[]{:S(2)}) copy-start(s32[128]{0:T(128)} %param.20) | copy-start | bytes 1540
  29.8 21.3 %copy-start.11 = (s32[320]{0:T(512)S(1)}, s32[320]{0:T(512)}, u32[]{:S(2)}) copy-start(s32[320]{0:T(512)} %param.23) | copy-start | bytes 3844
  40.1 96.2 %all-to-all-start = ((bf16[16,2,10240]{2,1,0:T(2,128)(2,1)}), bf16[16,2,10240]{2,1,0:T(2,128)(2,1)}, u32[]{:S(2)}, u32[]{:S(2)}) async-start(bf16[16,2,10240]{2,1,0:T(2,128)(2,1)} %reshape.530), calls=%async_computation | async-start | bytes 1310720 | tf_op jit(solution)/shard_map/all_to_all | solution.py:133
  51.3 85.0 %copy-start.6 = (s32[16,2,20]{2,1,0:T(2,128)}, s32[16,2,20]{2,1,0:T(2,128)S(1)}, u32[]{:S(2)}) copy-start(s32[16,2,20]{2,1,0:T(2,128)S(1)} %pad_add_fusion) | copy-start | bytes 7684
  179.8 3.1 copy-start.1
  179.8 3.1 copy-start.2
  195.6 3.1 copy-start.1
  195.6 3.1 copy-start.2
  244.3 29.5 %all-to-all-start.1 = ((bf16[16,2,21504]{2,1,0:T(2,128)(2,1)}), bf16[16,2,21504]{2,1,0:T(2,128)(2,1)}, u32[]{:S(2)}, u32[]{:S(2)}) async-start(bf16[16,2,21504]{2,1,0:T(2,128)(2,1)} %reshape.532), calls=%async_computation.1 | async-start | bytes 2752512 | tf_op jit(solution)/shard_map/all_to_all | solution.py:155
  284.2 12.5 %copy-start.9 = (bf16[256,256]{1,0:T(8,128)(2,1)S(1)}, bf16[256,256]{1,0:T(8,128)(2,1)}, u32[]{:S(2)}) copy-start(bf16[256,256]{1,0:T(8,128)(2,1)} %param.18) | copy-start | bytes 393220
  300.3 9.3 %copy-start.7 = (s32[16,2,20]{2,1,0:T(2,128)S(1)}, s32[16,2,20]{2,1,0:T(2,128)}, u32[]{:S(2)}) copy-start(s32[16,2,20]{2,1,0:T(2,128)} %get-tuple-element.606) | copy-start | bytes 7684
  304.7 35.0 %all-to-all-start.2 = ((bf16[16,256,168]{2,0,1:T(8,128)(2,1)}), bf16[16,256,168]{2,0,1:T(8,128)(2,1)}, u32[]{:S(2)}, u32[]{:S(2)}) async-start(bf16[16,256,168]{2,0,1:T(8,128)(2,1)} %copy.105), calls=%async_computation.2 | async-start | bytes 4194304 | tf_op jit(solution)/shard_map/all_to_all | solution.py:162
  348.7 3.6 copy-start.5
  355.5 4.3 copy-start.3
  355.5 4.4 copy-start.4
  366.0 3.6 copy-start.5
  372.8 4.3 copy-start.3
  372.8 4.4 copy-start.4
  420.7 27.0 %all-to-all-start.3 = ((bf16[16,16,1280]{2,0,1:T(8,128)(2,1)}), bf16[16,16,1280]{2,0,1:T(8,128)(2,1)}, u32[]{:S(2)}, u32[]{:S(2)}) async-start(bf16[16,16,1280]{2,0,1:T(8,128)(2,1)} %copy.109), calls=%async_computation.3 | async-start | bytes 1310720 | tf_op jit(solution)/shard_map/all_to_all | solution.py:169
  472.9 7.8 %copy-start.13 = (f32[128]{0:T(128)S(1)}, f32[128]{0:T(128)}, u32[]{:S(2)}) copy-start(f32[128]{0:T(128)} %param.17) | copy-start | bytes 1540
  479.6 1.5 copy-start.8
where the time goes:
time: 494 us; the launch traced here: 485 us
  local copies, waits for them, and re-layouts  232 us (47%)
  other arithmetic  128 us (26%)
  waiting for transfers between devices  70.5 us (14%)
  starting transfers between devices  29.1 us (6%)
  matrix products  23.9 us (5%)
    convert_element_type x1, other arithmetic, phase_tables(): inner_sin = jnp.sin(inner_angle).astype(jnp.bfloat16)  69.9 us
    unnamed x31, local copies, waits for them, and re-layouts  50.8 us
    all_to_all x1, waiting for transfers between devices, per_device(): lax.all_to_all(product, 'lev', split_axis=1, concat_axis=2, tiled=True)  30 us
    another operation x2, local copies, waits for them, and re-layouts, per_device(): harmonic.reshape(row_count, level_count, 2, band_count, 2, slot_count)  24.1 us
    reshape x2, local copies, waits for them, and re-layouts, per_device(): received.reshape(row_count, band_count, level_count, 2, 2, slot_count)  22.7 us
    all_to_all x1, waiting for transfers between devices, per_device(): lax.all_to_all(grid_field, 'lev', split_axis=2, concat_axis=1, tiled=True)  21.9 us
    reshape x2, local copies, waits for them, and re-layouts, per_device(): returned.reshape(returned.shape[0], level_count, 2, 2, slot_count)  20 us
    all_to_all x1, waiting for transfers between devices, per_device(): lax.all_to_all(outgoing, 'band', split_axis=1, concat_axis=0, tiled=True)  18.6 us
  transfers between devices with their start and end apart: 4, of which 3 were waited for; matrix products, arithmetic and copies ran while one was open for 18% of the time, Pallas kernels for 0%

commit v1 on v0

v1 whole, which is shorter than its diff:
```python
import math

import jax
import jax.numpy as jnp
from jax import lax
from jax.experimental import pallas as pl
from jax.experimental.pallas import tpu as pltpu
from jax.sharding import PartitionSpec as P

F32, BF16 = jnp.float32, jnp.bfloat16
NB = 16
GROUPS = 5
WAVES = 1280
COS = (1.0, -19.739208221435547, 64.93938446044922, -85.45658111572266,
       60.241241455078125, -26.39919662475586, 7.783571243286133, -1.4335278272628784)
SIN = (6.2831854820251465, -41.34170150756836, 81.6052474975586, -76.70577239990234,
       42.05741882324219, -15.084507942199707, 3.775092124938965, -0.6134149432182312)
NT = (((1,), (1,)), ((), ()))


def params(limit=40):
    return pltpu.CompilerParams(vmem_limit_bytes=limit * 1024 * 1024)


def dot(a, b, dims=(((1,), (0,)), ((), ()))):
    return lax.dot_general(a, b, dims, preferred_element_type=F32)


def exchange_chunks(items, width):
    items = list(items)
    lane = lax.broadcasted_iota(jnp.int32, items[0][0].shape, 1)
    for level in range(4):
        step = 1 << level
        shift = width * step
        for low in range(16):
            if low & step:
                continue
            a, b = items[low], items[low + step]
            if shift == 128:
                items[low], items[low + step] = (a[0], b[0]), (a[1], b[1])
                continue
            keep = (lane & shift) == 0
            items[low] = tuple(jnp.where(keep, a[h], pltpu.roll(b[h], shift, 1)) for h in (0, 1))
            items[low + step] = tuple(
                jnp.where(keep, pltpu.roll(a[h], 128 - shift, 1), b[h]) for h in (0, 1)
            )
    return items


def swap_parts(x):
    lane = lax.broadcasted_iota(jnp.int32, (x.shape[0], 128), 1)
    even = (lane & 1) == 0
    pieces = []
    for t in range(x.shape[1] // 128):
        piece = x[:, 128 * t : 128 * (t + 1)]
        pieces.append(jnp.where(even, pltpu.roll(piece, 127, 1), pltpu.roll(piece, 1, 1)))
    return jnp.concatenate(pieces, 1)


def slot_columns(pair, width, truncation):
    column = lax.broadcasted_iota(jnp.int32, (1, width), 1)
    split = truncation + 1 - pair
    first = column < split
    odd = jnp.where(first, column, column - split) & 1
    return first, odd


def table_kernel(rows_per_step, band, row_latitude, points, waves, table, outer_cos, outer_sin, seeds):
    step = pl.program_id(0)
    wave = waves[...]
    imag = (lax.broadcasted_iota(jnp.int32, (1, WAVES), 1) & 1) == 1
    index = lax.broadcasted_iota(jnp.int32, (16, WAVES), 0).astype(F32)
    for r in range(rows_per_step):
        lat = row_latitude[band[0] * NB + step * rows_per_step + r] & (points.shape[0] - 1)
        count = jnp.full((1, WAVES), points[lat].astype(F32))
        inverse = 1.0 / count

        def circle(stride):
            product = (wave * stride) * index
            turns = jnp.floor(product * inverse + 0.5)
            y = (product - turns * count) * inverse
            z = y * y
            c = jnp.full_like(z, COS[-1])
            s = jnp.full_like(z, SIN[-1])
            for k in range(6, -1, -1):
                c = c * z + COS[k]
                s = s * z + SIN[k]
            return c, s * y

        c1, s1 = circle(1.0)
        c2, s2 = circle(16.0)
        seeds[0] = jnp.where(imag, s2, c2)
        seeds[1] = jnp.where(imag, -c2, s2)
        seeds[2] = c1
        seeds[3] = s1
        c3, s3 = circle(256.0)
        outer_cos[r] = c3
        outer_sin[r] = s3
        for t in range(5):
            lanes = slice(256 * t, 256 * (t + 1))
            c1, s1 = seeds[2, :, lanes], seeds[3, :, lanes]
            for a in range(16):
                value = seeds[0, a : a + 1, lanes] * c1 - seeds[1, a : a + 1, lanes] * s1
                table[r, 16 * a : 16 * (a + 1), lanes] = value.astype(BF16)


def send_kernel(truncation, band, slot_pair, lane_latitude, spectral, legendre, out, sums):
    group = pl.program_id(0)
    width = spectral.shape[-1]
    place = (
        lax.broadcasted_iota(jnp.int32, (256, 256), 0) == lane_latitude[...]
    ).astype(F32).astype(BF16)
    for s in range(4):
        first, odd = slot_columns(slot_pair[band[0] * 20 + group * 4 + s], width, truncation)
        one = first.astype(F32)
        sign = 1.0 - 2.0 * odd.astype(F32)
        x = spectral[s].reshape(32, width)
        picks = [one, 1.0 - one, one * sign, (1.0 - one) * sign]
        left = jnp.concatenate([x * p.astype(BF16) for p in picks], 0)
        values = dot(left, legendre[s]).astype(BF16)
        sums[64 * s : 64 * (s + 1), :128] = values[:64]
        sums[64 * s : 64 * (s + 1), 128:] = values[64:]
    placed = dot(sums[...], place)
    items = [
        (placed[16 * u : 16 * (u + 1), :128], placed[16 * u : 16 * (u + 1), 128:])
        for u in range(16)
    ]
    for b, (lo, hi) in enumerate(exchange_chunks(items, 1)):
        out[b, 0, :, :128] = lo.astype(BF16)
        out[b, 0, :, 128:] = hi.astype(BF16)


def rows_kernel(
    rows_per_step, band, row_latitude, points, cutoffs, received, waves, table, outer_cos,
    outer_sin, factor, grid_field, out, fourier, twisted, samples
):
    step = pl.program_id(0)

    @pl.when(step == 0)
    def _():
        for g in range(GROUPS):
            items = []
            for src in range(NB):
                block = received[src, g].astype(F32)
                items.append((block[:, :128], block[:, 128:]))
            for row, (lo, hi) in enumerate(exchange_chunks(items, 16)):
                fourier[row, :, 256 * g : 256 * g + 128] = lo
                fourier[row, :, 256 * g + 128 : 256 * g + 256] = hi

    wave = waves[...]
    imag = (lax.broadcasted_iota(jnp.int32, (1, WAVES), 1) & 1) == 1
    sign = jnp.where(imag, F32(-1.0), F32(1.0))
    lane = lax.broadcasted_iota(jnp.int32, (1, 256), 1)
    for r in range(rows_per_step):
        row = step * rows_per_step + r
        lat = row_latitude[band[0] * NB + row] & (points.shape[0] - 1)
        count = points[lat]
        kept = (wave <= cutoffs[lat].astype(F32)).astype(F32)
        weight = kept * jnp.where(wave == 0.0, F32(1.0), F32(2.0))
        x = fourier[row]
        crossed = swap_parts(x) * -weight
        x = x * (weight * sign)
        for b in range(11):
            value = x * outer_cos[r, b : b + 1, :] + crossed * outer_sin[r, b : b + 1, :]
            twisted[r, 16 * b : 16 * (b + 1), :] = value.astype(BF16)
        field = dot(twisted[r], table[r], NT)
        for b in range(11):
            value = jnp.where(lane + 256 * b < count, field[16 * b : 16 * (b + 1), :], 0.0)
            value = value.astype(BF16)
            if b < 10:
                grid_field[r, :, 256 * b : 256 * (b + 1)] = value
                scaled = value.astype(F32) * factor[r, :, 256 * b : 256 * (b + 1)]
                samples[r, 16 * b : 16 * (b + 1), :] = scaled.astype(BF16)
            else:
                value = value[:, :128]
                grid_field[r, :, 2560:2688] = value
                scaled = value.astype(F32) * factor[r, :, 2560:2688]
                samples[r, 160:176, :128] = scaled.astype(BF16)
                samples[r, 160:176, 128:] = jnp.zeros((16, 128), BF16)
        scale = kept / jnp.full((1, WAVES), count.astype(F32))
        for t in range(5):
            lanes = slice(256 * t, 256 * (t + 1))
            part = dot(samples[r], table[r, :, lanes])
            total_cos = jnp.zeros((16, 256), F32)
            total_sin = jnp.zeros((16, 256), F32)
            for b in range(11):
                block = part[16 * b : 16 * (b + 1), :]
                total_cos = total_cos + block * outer_cos[r, b : b + 1, lanes]
                total_sin = total_sin + block * outer_sin[r, b : b + 1, lanes]
            value = sign[:, lanes] * total_cos - swap_parts(total_sin)
            fourier[row, :, lanes] = value * scale[:, lanes]

    @pl.when(step == pl.num_programs(0) - 1)
    def _():
        for g in range(GROUPS):
            items = [
                (fourier[row, :, 256 * g : 256 * g + 128],
                 fourier[row, :, 256 * g + 128 : 256 * g + 256])
                for row in range(NB)
            ]
            for b, (lo, hi) in enumerate(exchange_chunks(items, 16)):
                out[b, g, :, :128] = lo.astype(BF16)
                out[b, g, :, 128:] = hi.astype(BF16)


def mix_kernel(vertical, received, out):
    matrix = vertical[...]
    devices, chunks = received.shape[:2]
    for chunk in range(chunks):
        for g in range(GROUPS):
            block = received[:, chunk, g].reshape(devices * 16, 256)
            value = dot(matrix, block).astype(BF16)
            out[:, chunk, g] = value.reshape(devices, 16, 256)


def final_kernel(truncation, band, slot_pair, lane_latitude, weights, received, legendre, out, sums):
    group = pl.program_id(0)
    width = legendre.shape[1]
    items = []
    for src in range(NB):
        block = received[src, 0].astype(F32)
        items.append((block[:, :128], block[:, 128:]))
    for u, (lo, hi) in enumerate(exchange_chunks(items, 1)):
        sums[16 * u : 16 * (u + 1), :128] = lo.astype(BF16)
        sums[16 * u : 16 * (u + 1), 128:] = hi.astype(BF16)
    target = lax.broadcasted_iota(jnp.int32, (256, 256), 0)
    source = lane_latitude[...]
    value = jnp.where((target >= 128) & (source >= 128), F32(-1.0), F32(1.0))
    fold = jnp.where((target & 127) == (source & 127), value, 0.0).astype(BF16)
    parts = (dot(sums[...], fold, NT) * weights[...]).astype(BF16)
    for s in range(4):
        first, odd = slot_columns(slot_pair[band[0] * 20 + group * 4 + s], width, truncation)
        own = parts[64 * s : 64 * (s + 1)]
        left = jnp.concatenate([own[:, :128], own[:, 128:]], 0)
        full = dot(left, legendre[s], NT)
        even_part = jnp.where(first, full[0:32], full[32:64])
        odd_part = jnp.where(first, full[64:96], full[96:128])
        chosen = jnp.where(odd == 0, even_part, odd_part)
        out[s, 0] = chosen[:16]
        out[s, 1] = chosen[16:]


def whole(shape):
    return pl.BlockSpec(shape, lambda i: (0,) * len(shape))


SMEM = pl.BlockSpec(memory_space=pltpu.SMEM)


def cost(flops, size):
    return pl.CostEstimate(flops=flops, bytes_accessed=size, transcendentals=0)


def per_device(
    spectral, legendre, weights, vertical, grid_factor, points, cutoffs, row_latitude, slot_pair
):
    band = lax.axis_index("band").astype(jnp.int32).reshape(1)
    lev_count = lax.axis_size("lev")
    truncation = 2 * slot_pair.shape[0] - 1
    width = spectral.shape[3]
    row_width = grid_factor.shape[1]
    by_slot = spectral.transpose(2, 1, 0, 3)
    legendre = legendre.transpose(0, 2, 1)
    lane_latitude = row_latitude.reshape(NB, NB).T.reshape(1, 256)
    pairs = slot_pair.reshape(NB, GROUPS, 4).transpose(1, 0, 2)
    waves = jnp.stack([pairs, truncation - pairs], -1)
    waves = jnp.broadcast_to(waves[..., None], waves.shape + (2,)).reshape(1, WAVES).astype(F32)

    message = pl.pallas_call(
        lambda *refs: send_kernel(truncation, *refs),
        grid=(GROUPS,),
        in_specs=[
            SMEM, SMEM, whole((1, 256)),
            pl.BlockSpec((4, 2, 16, width), lambda i: (i, 0, 0, 0)),
            pl.BlockSpec((4, width, 128), lambda i: (i, 0, 0)),
        ],
        out_specs=pl.BlockSpec((NB, 1, 16, 256), lambda i: (0, i, 0, 0)),
        out_shape=jax.ShapeDtypeStruct((NB, GROUPS, 16, 256), BF16),
        scratch_shapes=[pltpu.VMEM((256, 256), BF16)],
        compiler_params=params(),
        cost_estimate=cost(2 * 20 * 128 * 768 * 128, 5_000_000),
        name="legendre_send",
    )(band, slot_pair, lane_latitude, by_slot, legendre)
    received = lax.all_to_all(message, "band", split_axis=0, concat_axis=0, tiled=True)

    per_step = 2
    table, outer_cos, outer_sin = pl.pallas_call(
        lambda *refs: table_kernel(per_step, *refs),
        grid=(NB // per_step,),
        in_specs=[SMEM, SMEM, SMEM, whole((1, WAVES))],
        out_specs=[
            pl.BlockSpec((per_step, 256, WAVES), lambda i: (i, 0, 0)),
            pl.BlockSpec((per_step, 16, WAVES), lambda i: (i, 0, 0)),
            pl.BlockSpec((per_step, 16, WAVES), lambda i: (i, 0, 0)),
        ],
        out_shape=[
            jax.ShapeDtypeStruct((NB, 256, WAVES), BF16),
            jax.ShapeDtypeStruct((NB, 16, WAVES), F32),
            jax.ShapeDtypeStruct((NB, 16, WAVES), F32),
        ],
        scratch_shapes=[pltpu.VMEM((4, 16, WAVES), F32)],
        compiler_params=params(),
        cost_estimate=cost(16 * 256 * 1280 * 20, 14_000_000),
        name="phase_tables",
    )(band, row_latitude, points, waves)

    factor = grid_factor.astype(F32).reshape(NB, 1, row_width)
    grid_field, harmonic = pl.pallas_call(
        lambda *refs: rows_kernel(per_step, *refs),
        grid=(NB // per_step,),
        in_specs=[
            SMEM, SMEM, SMEM, SMEM,
            whole((NB, GROUPS, 16, 256)),
            whole((1, WAVES)),
            pl.BlockSpec((per_step, 256, WAVES), lambda i: (i, 0, 0)),
            pl.BlockSpec((per_step, 16, WAVES), lambda i: (i, 0, 0)),
            pl.BlockSpec((per_step, 16, WAVES), lambda i: (i, 0, 0)),
            pl.BlockSpec((per_step, 1, row_width), lambda i: (i, 0, 0)),
        ],
        out_specs=[
            pl.BlockSpec((per_step, 16, row_width), lambda i: (i, 0, 0)),
            whole((NB, GROUPS, 16, 256)),
        ],
        out_shape=[
            jax.ShapeDtypeStruct((NB, 16, row_width), BF16),
            jax.ShapeDtypeStruct((NB, GROUPS, 16, 256), BF16),
        ],
        scratch_shapes=[
            pltpu.VMEM((NB, 16, WAVES), F32),
            pltpu.VMEM((per_step, 176, WAVES), BF16),
            pltpu.VMEM((per_step, 176, 256), BF16),
        ],
        compiler_params=params(),
        cost_estimate=cost(4 * 16 * 176 * 1280 * 256, 17_000_000),
        name="grid_rows",
    )(band, row_latitude, points, cutoffs, received, waves, table, outer_cos, outer_sin, factor)

    levels_in = lax.all_to_all(harmonic, "lev", split_axis=0, concat_axis=0, tiled=True)
    shape = (lev_count, NB // lev_count, GROUPS, 16, 256)
    mixed = pl.pallas_call(
        mix_kernel,
        grid=(1,),
        in_specs=[whole(vertical.shape), whole(shape)],
        out_specs=whole(shape),
        out_shape=jax.ShapeDtypeStruct(shape, BF16),
        compiler_params=params(),
        cost_estimate=cost(2 * 256 * 256 * 1280, 1_400_000),
        name="vertical_mix",
    )(vertical, levels_in.reshape(shape))
    outgoing = lax.all_to_all(
        mixed.reshape(NB, GROUPS, 16, 256), "lev", split_axis=0, concat_axis=0, tiled=True
    )
    returned = lax.all_to_all(outgoing, "band", split_axis=0, concat_axis=0, tiled=True)

    round_trip = pl.pallas_call(
        lambda *refs: final_kernel(truncation, *refs),
        grid=(GROUPS,),
        in_specs=[
            SMEM, SMEM, whole((1, 256)), whole((1, 256)),
            pl.BlockSpec((NB, 1, 16, 256), lambda i: (0, i, 0, 0)),
            pl.BlockSpec((4, width, 128), lambda i: (i, 0, 0)),
        ],
        out_specs=pl.BlockSpec((4, 2, 16, width), lambda i: (i, 0, 0, 0)),
        out_shape=jax.ShapeDtypeStruct((20, 2, 16, width), F32),
        scratch_shapes=[pltpu.VMEM((256, 256), BF16)],
        compiler_params=params(),
        cost_estimate=cost(2 * 20 * 128 * 768 * 128, 6_000_000),
        name="legendre_return",
    )(
        band, slot_pair, lane_latitude, jnp.concatenate([weights, weights]).reshape(1, 256),
        returned, legendre,
    )
    return (grid_field, round_trip.transpose(2, 1, 0, 3))


def solution(mesh):
    in_specs = (
        P("lev", None, "band", None),
        P("band", None, None),
        P(),
        P(),
        P("band", None),
        P(),
        P(),
        P(),
        P(),
    )
    out_specs = (P("band", "lev", None), P("lev", None, "band", None))
    return jax.shard_map(
        per_device, mesh=mesh, in_specs=in_specs, out_specs=out_specs, check_vma=False
    )
```

time: 494 us -> 130 us (0.26); the launches traced: 485 us -> 129 us
  local copies, waits for them, and re-layouts: 232 us -> 16.3 us
  other arithmetic: 128 us -> 0.02 us
  waiting for transfers between devices: 70.5 us -> 26.3 us
  Pallas kernels: 0 us -> 35.7 us
  blocking collectives: 0 us -> 35.3 us
  matrix products: 23.9 us -> 0 us
  starting transfers between devices: 29.1 us -> 15.1 us
    reshape x15 -> x5, local copies, waits for them, and re-layouts: 72.6 us -> 1.14 us  [the longest x2 0.84 us: per_device(): lane_latitude = row_latitude.reshape(NB, NB).T.reshape(1, 256)]
    convert_element_type x3 -> x1, other arithmetic: 71.4 us -> 0.01 us  [per_device(): jnp.broadcast_to(waves[..., None], waves.shape + (2,)).reshape(1, WAVES)]
    all_to_all x4 -> x2, waiting for transfers between devices: 70.5 us -> 26.3 us  [the longest x1 20.1 us: per_device(): lax.all_to_all(outgoing, 'band', split_axis=0, concat_axis=0, tiled=True)]
    unnamed x31 -> x24, local copies, waits for them, and re-layouts: 50.8 us -> 14.1 us
    another operation x9 -> x0, local copies, waits for them, and re-layouts: 36.1 us -> none  [the longest x2 24.1 us: per_device(): harmonic.reshape(row_count, level_count, 2, band_count, 2, slot_count)]
    pallas_call x0 -> x5, Pallas kernels: none -> 35.7 us  [the longest x1 16.2 us: per_device(): pl.pallas_call(lambda *refs: rows_kernel(per_step, *refs), grid=(NB // pe...]
    all_to_all x0 -> x2, blocking collectives: none -> 35.3 us  [the longest x1 18.9 us: per_device(): lax.all_to_all(harmonic, 'lev', split_axis=0, concat_axis=0, tiled=True)]
    dot_general x7 -> x0, matrix products: 23.9 us -> none  [the longest x2 9.14 us: inverse_row(): jnp.einsum('lqm,mp->lqp', twisted, table, preferred_element_type=jnp.floa...]
  transfers between devices with their start and end apart: 4 -> 2, of which waited for: 3 -> 2; matrix products, arithmetic and copies ran while one was open for 18% -> 1% of each run, Pallas kernels for 0% -> 7%
where the time goes in v1:
time: 130 us; the launch traced here: 129 us
  Pallas kernels  35.7 us (27%)
  blocking collectives  35.3 us (27%)
  waiting for transfers between devices  26.3 us (20%)
  local copies, waits for them, and re-layouts  16.3 us (13%)
  starting transfers between devices  15.1 us (12%)
    all_to_all x1, waiting for transfers between devices, per_device(): lax.all_to_all(outgoing, 'band', split_axis=0, concat_axis=0, tiled=True)  20.1 us
    all_to_all x1, blocking collectives, per_device(): lax.all_to_all(harmonic, 'lev', split_axis=0, concat_axis=0, tiled=True)  18.9 us
    all_to_all x1, blocking collectives, per_device(): lax.all_to_all(mixed.reshape(NB, GROUPS, 16, 256), 'lev', split_axis=0, c...  16.4 us
    pallas_call x1, Pallas kernels, per_device(): pl.pallas_call(lambda *refs: rows_kernel(per_step, *refs), grid=(NB // pe...  16.2 us
    unnamed x24, local copies, waits for them, and re-layouts  14.1 us
    all_to_all x1, starting transfers between devices, per_device(): lax.all_to_all(message, 'band', split_axis=0, concat_axis=0, tiled=True)  10.1 us
    pallas_call x1, Pallas kernels, per_device(): pl.pallas_call(lambda *refs: table_kernel(per_step, *refs), grid=(NB // p...  8.43 us
    all_to_all x1, waiting for transfers between devices, per_device(): lax.all_to_all(message, 'band', split_axis=0, concat_axis=0, tiled=True)  6.2 us
  transfers between devices with their start and end apart: 2, of which 2 were waited for; matrix products, arithmetic and copies ran while one was open for 1% of the time, Pallas kernels for 7%

profile of v1, /device:TPU:1, one launch (start us, length us, event | category | flops | bytes accessed | tf_op | source)
XLA Modules:
  0.0 129.5 jit_solution(18183092297599202948)
XLA Ops:
  0.6 0.0 copy-start.5
  0.6 0.8 reshape.46
  1.4 0.1 copy.27
  1.5 0.1 reshape.47.refs_2_
  1.6 1.4 %copy.35 = bf16[16,2,20,641]{3,0,1,2:T(8,128)(2,1)S(1)} copy(bf16[16,2,20,641]{3,1,2,0:T(2,128)(2,1)} %param.9) | data formatting | bytes 1640960 | tf_op args[0]
  2.9 0.0 copy-done.5
  3.0 0.0 copy-start
  3.0 1.9 %copy-done = bf16[20,128,641]{1,2,0:T(8,128)(2,1)S(1)} copy-done((bf16[20,128,641]{1,2,0:T(8,128)(2,1)S(1)}, bf16[20,128,641]{1,2,0:T(8,128)(2,1)}, u32[]{:S(2)}) %copy-start) | copy-done | bytes 3281944
  4.9 5.6 %legendre_send.1 = bf16[16,5,16,256]{3,2,1,0:T(8,128)(2,1)} custom-call(s32[1]{0:T(128)} %bitcast.refs_0_, s32[320]{0:T(512)S(1)} %copy-done.5, s32[1,256]{1,0:T(1,128)S(1)} %reshape.47.refs_2_, bf16[20,2,16,641]{3,2,1,0:T(8,128)(2,1)S(1)} %bitcast.25, bf16[20,641,128]{2,1,0:T(8,128)(2,1)S(1)} %bitcast.22), custom_call_target="tpu_custom_call" | custom-call | flops 503316480 | bytes 5000000 | tf_op jit(solution)/shard_map/legendre_send/pallas_call | solution.py:269
  10.5 0.0 copy-start.9
  10.5 0.0 copy-start.6
  10.5 0.0 copy-start.7
  10.5 0.0 copy-start.8
  10.5 10.1 %all-to-all-start = ((bf16[16,5,16,256]{3,2,1,0:T(8,128)(2,1)}), bf16[16,5,16,256]{3,2,1,0:T(8,128)(2,1)S(1)}, u32[]{:S(2)}, u32[]{:S(2)}) async-start(bf16[16,5,16,256]{3,2,1,0:T(8,128)(2,1)} %legendre_send.1), calls=%async_computation | async-start | bytes 1310720 | tf_op jit(solution)/shard_map/all_to_all | solution.py:284
  20.6 0.1 reshape.48
  20.7 0.1 copy.29
  20.8 0.2 copy.32
  21.1 0.4 broadcast_in_dim.2
  21.5 0.4 convert_element_type.7.refs_3_.refs_5_
  21.9 0.0 copy-done.9
  21.9 0.1 reshape.55.refs_9_
  22.0 0.0 copy-done.6
  22.0 0.0 copy-done.7
  22.0 8.4 %phase_tables.1 = (bf16[16,256,1280]{2,1,0:T(8,128)(2,1)S(1)}, f32[16,16,1280]{2,1,0:T(8,128)S(1)}, f32[16,16,1280]{2,1,0:T(8,128)S(1)}) custom-call(s32[1]{0:T(128)} %bitcast.refs_0_, s32[256]{0:T(256)S(1)} %copy-done.6, s32[128]{0:T(128)S(1)} %copy-done.7, f32[1,1280]{1,0:T(1,128)S(1)} %convert_element_type.7.refs_3_.refs_5_), custom_call_target="tpu_custom_call" | custom-call | flops 104857600 | bytes 14000000 | tf_op jit(solution)/shard_map/phase_tables/pallas_call | solution.py:287
  30.5 0.0 copy-start.2
  30.5 4.0 %copy-done.2 = bf16[16,256,1280]{2,1,0:T(8,128)(2,1)} copy-done((bf16[16,256,1280]{2,1,0:T(8,128)(2,1)}, bf16[16,256,1280]{2,1,0:T(8,128)(2,1)S(1)}, u32[]{:S(2)}) %copy-start.2) | copy-done | bytes 10485784
  34.4 6.2 %all-to-all-done.refs_4_ = bf16[16,5,16,256]{3,2,1,0:T(8,128)(2,1)S(1)} async-done(((bf16[16,5,16,256]{3,2,1,0:T(8,128)(2,1)}), bf16[16,5,16,256]{3,2,1,0:T(8,128)(2,1)S(1)}, u32[]{:S(2)}, u32[]{:S(2)}) %all-to-all-start) | async-done | bytes 655392 | tf_op jit(solution)/shard_map/all_to_all | solution.py:284
  40.6 0.0 copy-done.8
  40.6 0.0 copy-start.3
  40.6 4.0 %copy-done.3 = bf16[16,256,1280]{2,1,0:T(8,128)(2,1)S(1)} copy-done((bf16[16,256,1280]{2,1,0:T(8,128)(2,1)S(1)}, bf16[16,256,1280]{2,1,0:T(8,128)(2,1)}, u32[]{:S(2)}) %copy-start.3) | copy-done | bytes 10485784
  44.6 0.0 copy-start.4
  44.6 16.2 %grid_rows.1 = (bf16[16,16,2688]{2,1,0:T(8,128)(2,1)}, bf16[16,5,16,256]{3,2,1,0:T(8,128)(2,1)S(1)}) custom-call(s32[1]{0:T(128)} %bitcast.refs_0_, s32[256]{0:T(256)S(1)} %copy-done.6, s32[128]{0:T(128)S(1)} %copy-done.7, s32[128]{0:T(128)S(1)} %copy-done.8, bf16[16,5,16,256]{3,2,1,0:T(8,128)(2,1)S(1)} %all-to-all-done.refs_4_, ...), custom_call_target="tpu_custom_call" | custom-call | flops 3690987520 | bytes 17000000 | tf_op jit(solution)/shard_map/grid_rows/pallas_call | solution.py:308
  60.8 18.9 %all_to_all.20 = bf16[16,5,16,256]{3,2,1,0:T(8,128)(2,1)S(1)} all-to-all(bf16[16,5,16,256]{3,2,1,0:T(8,128)(2,1)S(1)} %get-tuple-element.11), channel_id=1, replica_groups=mesh['band'=16,'lev'=16] {'lev'}, dimensions={0} | all-to-all | bytes 1310720 | tf_op jit(solution)/shard_map/all_to_all | solution.py:338
  79.7 0.0 copy-done.4
  79.7 0.0 copy-start.10
  79.7 0.0 copy-start.1
  79.7 0.3 vertical_mix.1
  80.0 16.4 %all_to_all.21 = bf16[16,5,16,256]{3,2,1,0:T(8,128)(2,1)} all-to-all(bf16[16,5,16,256]{3,2,1,0:T(8,128)(2,1)S(1)} %bitcast.27), channel_id=1, replica_groups=mesh['band'=16,'lev'=16] {'lev'}, dimensions={0} | all-to-all | bytes 1310720 | tf_op jit(solution)/shard_map/all_to_all | solution.py:350
  96.4 4.9 %all-to-all-start.3 = ((bf16[16,5,16,256]{3,2,1,0:T(8,128)(2,1)}), bf16[16,5,16,256]{3,2,1,0:T(8,128)(2,1)}, u32[]{:S(2)}, u32[]{:S(2)}) async-start(bf16[16,5,16,256]{3,2,1,0:T(8,128)(2,1)} %all_to_all.21), calls=%async_computation.3 | async-start | bytes 1310720 | tf_op jit(solution)/shard_map/all_to_all | solution.py:353
  101.3 0.0 copy-done.10
  101.4 20.1 %all-to-all-done.3.refs_4_ = bf16[16,5,16,256]{3,2,1,0:T(8,128)(2,1)} async-done(((bf16[16,5,16,256]{3,2,1,0:T(8,128)(2,1)}), bf16[16,5,16,256]{3,2,1,0:T(8,128)(2,1)}, u32[]{:S(2)}, u32[]{:S(2)}) %all-to-all-start.3) | async-done | bytes 655392 | tf_op jit(solution)/shard_map/all_to_all | solution.py:353
  121.5 0.0 copy-done.1
  121.5 5.2 %legendre_return.1 = f32[20,2,16,641]{3,2,1,0:T(8,128)S(1)} custom-call(s32[1]{0:T(128)} %bitcast.refs_0_, s32[320]{0:T(512)S(1)} %copy-done.5, s32[1,256]{1,0:T(1,128)S(1)} %reshape.47.refs_2_, f32[1,256]{1,0:T(1,128)S(1)} %bitcast.28, bf16[16,5,16,256]{3,2,1,0:T(8,128)(2,1)} %all-to-all-done.3.refs_4_, bf16[20,641,128]{2,1,0:T(8,128)(2,1)S(1)} %bitcast.23), custom_call_target="tpu_custom_call" | custom-call | flops 503316480 | bytes 6000000 | tf_op jit(solution)/shard_map/legendre_return/pallas_call | solution.py:355
  126.7 2.8 %copy.33 = f32[16,2,20,641]{3,1,2,0:T(2,128)} copy(f32[16,2,20,641]{3,0,1,2:T(8,128)S(1)} %bitcast.24) | data formatting | bytes 3281920
  (3 shorter events, 0.0 us)
Async XLA Ops:
  0.6 2.3 %copy-start.5 = (s32[320]{0:T(512)S(1)}, s32[320]{0:T(512)}, u32[]{:S(2)}) copy-start(s32[320]{0:T(512)} %refs_1_.7) | copy-start | bytes 3844
  3.0 1.9 %copy-start = (bf16[20,128,641]{1,2,0:T(8,128)(2,1)S(1)}, bf16[20,128,641]{1,2,0:T(8,128)(2,1)}, u32[]{:S(2)}) copy-start(bf16[20,128,641]{1,2,0:T(8,128)(2,1)} %param.10) | copy-start | bytes 9845764
  10.5 11.4 %copy-start.9 = (bf16[16,2688]{1,0:T(8,128)(2,1)S(1)}, bf16[16,2688]{1,0:T(8,128)(2,1)}, u32[]{:S(2)}) copy-start(bf16[16,2688]{1,0:T(8,128)(2,1)} %param.13) | copy-start | bytes 258052
  10.5 11.5 %copy-start.6 = (s32[256]{0:T(256)S(1)}, s32[256]{0:T(256)}, u32[]{:S(2)}) copy-start(s32[256]{0:T(256)} %refs_1_.6) | copy-start | bytes 3076
  10.5 11.5 %copy-start.7 = (s32[128]{0:T(128)S(1)}, s32[128]{0:T(128)}, u32[]{:S(2)}) copy-start(s32[128]{0:T(128)} %refs_2_.3) | copy-start | bytes 1540
  10.5 30.2 %copy-start.8 = (s32[128]{0:T(128)S(1)}, s32[128]{0:T(128)}, u32[]{:S(2)}) copy-start(s32[128]{0:T(128)} %refs_3_.1) | copy-start | bytes 1540
  10.5 30.1 %all-to-all-start = ((bf16[16,5,16,256]{3,2,1,0:T(8,128)(2,1)}), bf16[16,5,16,256]{3,2,1,0:T(8,128)(2,1)S(1)}, u32[]{:S(2)}, u32[]{:S(2)}) async-start(bf16[16,5,16,256]{3,2,1,0:T(8,128)(2,1)} %legendre_send.1), calls=%async_computation | async-start | bytes 1310720 | tf_op jit(solution)/shard_map/all_to_all | solution.py:284
  30.5 4.0 %copy-start.2 = (bf16[16,256,1280]{2,1,0:T(8,128)(2,1)}, bf16[16,256,1280]{2,1,0:T(8,128)(2,1)S(1)}, u32[]{:S(2)}) copy-start(bf16[16,256,1280]{2,1,0:T(8,128)(2,1)S(1)} %get-tuple-element.7.refs_6_) | copy-start | bytes 31457284
  40.6 4.0 %copy-start.3 = (bf16[16,256,1280]{2,1,0:T(8,128)(2,1)S(1)}, bf16[16,256,1280]{2,1,0:T(8,128)(2,1)}, u32[]{:S(2)}) copy-start(bf16[16,256,1280]{2,1,0:T(8,128)(2,1)} %copy-done.2) | copy-start | bytes 31457284
  44.6 35.1 %copy-start.4 = (bf16[256,256]{1,0:T(8,128)(2,1)S(1)}, bf16[256,256]{1,0:T(8,128)(2,1)}, u32[]{:S(2)}) copy-start(bf16[256,256]{1,0:T(8,128)(2,1)} %vertical.1) | copy-start | bytes 393220
  79.7 21.7 %copy-start.10 = (f32[128]{0:T(128)S(1)}, f32[128]{0:T(128)}, u32[]{:S(2)}) copy-start(f32[128]{0:T(128)} %param.11) | copy-start | bytes 1540
  79.7 41.8 %copy-start.1 = (bf16[20,128,641]{1,2,0:T(8,128)(2,1)S(1)}, bf16[20,128,641]{1,2,0:T(8,128)(2,1)}, u32[]{:S(2)}) copy-start(bf16[20,128,641]{1,2,0:T(8,128)(2,1)} %param.10) | copy-start | bytes 9845764
  96.4 25.1 %all-to-all-start.3 = ((bf16[16,5,16,256]{3,2,1,0:T(8,128)(2,1)}), bf16[16,5,16,256]{3,2,1,0:T(8,128)(2,1)}, u32[]{:S(2)}, u32[]{:S(2)}) async-start(bf16[16,5,16,256]{3,2,1,0:T(8,128)(2,1)} %all_to_all.21), calls=%async_computation.3 | async-start | bytes 1310720 | tf_op jit(solution)/shard_map/all_to_all | solution.py:353

commit v2 on v1

v2 whole, which is shorter than its diff:
```python
import math

import jax
import jax.numpy as jnp
from jax import lax
from jax.experimental import pallas as pl
from jax.experimental.pallas import tpu as pltpu
from jax.sharding import PartitionSpec as P

F32, BF16 = jnp.float32, jnp.bfloat16
NB = 16
GROUPS = 5
WAVES = 1280
ROWS = 2560
COS = (1.0, -19.739208221435547, 64.93938446044922, -85.45658111572266,
       60.241241455078125, -26.39919662475586, 7.783571243286133, -1.4335278272628784)
SIN = (6.2831854820251465, -41.34170150756836, 81.6052474975586, -76.70577239990234,
       42.05741882324219, -15.084507942199707, 3.775092124938965, -0.6134149432182312)
NT = (((1,), (1,)), ((), ()))
FINE, COARSE = 64, 42


def params(limit=24):
    return pltpu.CompilerParams(vmem_limit_bytes=limit * 1024 * 1024)


def dot(a, b, dims=(((1,), (0,)), ((), ()))):
    return lax.dot_general(a, b, dims, preferred_element_type=F32)


def identity():
    same = lax.broadcasted_iota(jnp.int32, (256, 256), 0) == lax.broadcasted_iota(
        jnp.int32, (256, 256), 1
    )
    return same.astype(F32).astype(BF16)


def exchange_chunks(items):
    items = list(items)
    lane = lax.broadcasted_iota(jnp.int32, items[0].shape, 1)
    for level in range(4):
        step = 1 << level
        keep = (lane & step) == 0
        for low in range(16):
            if low & step:
                continue
            a, b = items[low], items[low + step]
            items[low] = jnp.where(keep, a, pltpu.roll(b, step, 1))
            items[low + step] = jnp.where(keep, pltpu.roll(a, 128 - step, 1), b)
    return items


def slot_columns(pair, width, truncation):
    column = lax.broadcasted_iota(jnp.int32, (1, width), 1)
    split = truncation + 1 - pair
    first = column < split
    odd = jnp.where(first, column, column - split) & 1
    return first, odd


def table_kernel(own, row_latitude, points, waves, table, fine, coarse):
    lat = row_latitude[own[0]] & (points.shape[0] - 1)
    for t in range(10):
        lanes = slice(128 * t, 128 * (t + 1))
        wave = waves[:, lanes]
        count = jnp.full((1, 128), points[lat].astype(F32))
        inverse = 1.0 / count

        def circle(rows, stride):
            index = lax.broadcasted_iota(jnp.int32, (rows, 128), 0).astype(F32)
            product = (wave * stride) * index
            turns = jnp.floor(product * inverse + 0.5)
            y = (product - turns * count) * inverse
            z = y * y
            c = jnp.full_like(z, COS[-1])
            s = jnp.full_like(z, SIN[-1])
            for k in range(6, -1, -1):
                c = c * z + COS[k]
                s = s * z + SIN[k]
            return c, s * y

        imag = (lax.broadcasted_iota(jnp.int32, (1, 128), 1) & 16) == 16
        fine[0], fine[1] = circle(FINE, 1.0)
        c2, s2 = circle(48, float(FINE))
        coarse[0] = jnp.where(imag, s2, c2)
        coarse[1] = jnp.where(imag, -c2, s2)
        for a in range(COARSE):
            value = coarse[0, a : a + 1, :] * fine[0] - coarse[1, a : a + 1, :] * fine[1]
            table[FINE * a : FINE * (a + 1), lanes] = value.astype(BF16)


def send_kernel(truncation, band, slot_pair, lane_latitude, spectral, legendre, out, sums, place, rows):
    group = pl.program_id(0)
    width = spectral.shape[-1]

    @pl.when(group == 0)
    def _():
        hit = lax.broadcasted_iota(jnp.int32, (256, 256), 0) == lane_latitude[...]
        place[...] = dot(identity(), hit.astype(F32).astype(BF16), NT).astype(BF16)

    for s in range(4):
        first, odd = slot_columns(slot_pair[band[0] * 20 + group * 4 + s], width, truncation)
        one = first.astype(F32)
        sign = 1.0 - 2.0 * odd.astype(F32)
        x = spectral[s].reshape(32, width)
        picks = [one, 1.0 - one, one * sign, (1.0 - one) * sign]
        left = jnp.concatenate([x * p.astype(BF16) for p in picks], 0)
        values = dot(left, legendre[s]).astype(BF16)
        sums[64 * s : 64 * (s + 1), :128] = values[:64]
        sums[64 * s : 64 * (s + 1), 128:] = values[64:]
    placed = dot(place[...], sums[...], NT)
    rows[pl.ds(2 * group, 256, stride=10), :] = placed[:, :128]
    rows[pl.ds(2 * group + 1, 256, stride=10), :] = placed[:, 128:]

    @pl.when(group == GROUPS - 1)
    def _():
        out[...] = rows[...].astype(BF16)


def row_kernel(
    own, row_latitude, points, cutoffs, received, waves, table, vertical, factor, grid_field, out,
    rows, fourier, left, samples
):
    lat = row_latitude[own[0]] & (points.shape[0] - 1)
    count = points[lat]
    wave = waves[...]
    imag = (lax.broadcasted_iota(jnp.int32, (1, WAVES), 1) & 16) == 16
    sign = jnp.where(imag, F32(-1.0), F32(1.0))
    kept = sign * (wave <= cutoffs[lat].astype(F32)).astype(F32)
    weight = kept * jnp.where(wave == 0.0, F32(1.0), F32(2.0))
    scale = kept / jnp.full((1, WAVES), count.astype(F32))
    rows[...] = received[...].astype(F32)
    for c in range(10):
        items = [rows[pl.ds(160 * b + c, 16, stride=10), :] for b in range(16)]
        lanes = slice(128 * c, 128 * (c + 1))
        for l, item in enumerate(exchange_chunks(items)):
            fourier[pl.ds(256 * c + l, 16, stride=16), :] = item * weight[:, lanes]
        left[:, lanes] = fourier[256 * c : 256 * (c + 1), :].astype(BF16)
    lane = lax.broadcasted_iota(jnp.int32, (1, 256), 1)
    width = grid_field.shape[1]
    for start in range(0, width, 256):
        size = min(256, width - start)
        cut = slice(start, start + size)
        field = dot(left[...], table[cut, :], NT)
        field = jnp.where(lane[:, :size] + start < count, field, 0.0).astype(BF16)
        grid_field[:, cut] = field
        samples[:, cut] = (dot(vertical[...], field) * factor[:, cut]).astype(BF16)
    for t in range(5):
        lanes = slice(256 * t, 256 * (t + 1))
        value = dot(samples[...], table[:, lanes]) * scale[:, lanes]
        fourier[512 * t : 512 * t + 256, :] = value[:, :128]
        fourier[512 * t + 256 : 512 * (t + 1), :] = value[:, 128:]
    for c in range(10):
        items = [fourier[pl.ds(256 * c + l, 16, stride=16), :] for l in range(16)]
        for b, item in enumerate(exchange_chunks(items)):
            rows[pl.ds(160 * b + c, 16, stride=10), :] = item
    out[...] = rows[...].astype(BF16)


def final_kernel(truncation, band, slot_pair, lane_latitude, weights, received, legendre, out, rows):
    group = pl.program_id(0)
    width = legendre.shape[1]

    @pl.when(group == 0)
    def _():
        rows[...] = received[...].astype(F32)

    values = jnp.concatenate(
        [rows[pl.ds(2 * group + h, 256, stride=10), :].astype(BF16) for h in (0, 1)], 1
    )
    turned = dot(identity(), values, NT).astype(BF16)
    target = lax.broadcasted_iota(jnp.int32, (256, 256), 0)
    source = lane_latitude[...]
    value = jnp.where((target >= 128) & (source >= 128), F32(-1.0), F32(1.0))
    fold = jnp.where((target & 127) == (source & 127), value, 0.0).astype(BF16)
    parts = (dot(turned, fold, NT) * weights[...]).astype(BF16)
    for s in range(4):
        first, odd = slot_columns(slot_pair[band[0] * 20 + group * 4 + s], width, truncation)
        own = parts[64 * s : 64 * (s + 1)]
        left = jnp.concatenate([own[:, :128], own[:, 128:]], 0)
        full = dot(left, legendre[s], NT)
        even_part = jnp.where(first, full[0:32], full[32:64])
        odd_part = jnp.where(first, full[64:96], full[96:128])
        chosen = jnp.where(odd == 0, even_part, odd_part)
        out[s, 0] = chosen[:16]
        out[s, 1] = chosen[16:]


def whole(shape):
    return pl.BlockSpec(shape, lambda i: (0,) * len(shape))


SMEM = pl.BlockSpec(memory_space=pltpu.SMEM)
VMEM = pl.BlockSpec(memory_space=pltpu.VMEM)


def cost(flops, size):
    return pl.CostEstimate(flops=flops, bytes_accessed=size, transcendentals=0)


def everywhere(message):
    pieces = message.reshape(ROWS // 2, 2, 128)
    pieces = lax.all_to_all(pieces, ("band", "lev"), split_axis=0, concat_axis=0, tiled=True)
    return pieces.reshape(ROWS, 128)


def per_device(
    spectral, legendre, weights, vertical, grid_factor, points, cutoffs, row_latitude, slot_pair
):
    band_index = lax.axis_index("band").astype(jnp.int32)
    lev_index = lax.axis_index("lev").astype(jnp.int32)
    band = band_index.reshape(1)
    own = (band_index * NB + lev_index).reshape(1)
    truncation = 2 * slot_pair.shape[0] - 1
    width = spectral.shape[3]
    row_width = grid_factor.shape[1]
    by_slot = spectral.transpose(2, 1, 0, 3)
    legendre = legendre.transpose(0, 2, 1)
    lane_latitude = row_latitude.reshape(1, 256)
    pairs = slot_pair.reshape(NB, GROUPS, 4).transpose(1, 2, 0)
    waves = jnp.stack([pairs, pairs, truncation - pairs, truncation - pairs], 2)
    waves = waves.reshape(1, WAVES).astype(F32)
    factor = lax.dynamic_slice_in_dim(grid_factor, lev_index, 1, 0).astype(F32)

    message = pl.pallas_call(
        lambda *refs: send_kernel(truncation, *refs),
        grid=(GROUPS,),
        in_specs=[
            SMEM, SMEM, whole((1, 256)),
            pl.BlockSpec((4, 2, 16, width), lambda i: (i, 0, 0, 0)),
            pl.BlockSpec((4, width, 128), lambda i: (i, 0, 0)),
        ],
        out_specs=whole((ROWS, 128)),
        out_shape=jax.ShapeDtypeStruct((ROWS, 128), BF16),
        scratch_shapes=[
            pltpu.VMEM((256, 256), BF16),
            pltpu.VMEM((256, 256), BF16),
            pltpu.VMEM((ROWS, 128), F32),
        ],
        compiler_params=params(),
        cost_estimate=cost(2 * 20 * 128 * 768 * 128, 5_000_000),
        name="legendre_send",
    )(band, slot_pair, lane_latitude, by_slot, legendre)
    received = everywhere(message)

    table = pl.pallas_call(
        table_kernel,
        in_specs=[SMEM, SMEM, SMEM, VMEM],
        out_specs=VMEM,
        out_shape=jax.ShapeDtypeStruct((row_width, WAVES), BF16),
        scratch_shapes=[pltpu.VMEM((2, FINE, 128), F32), pltpu.VMEM((2, 48, 128), F32)],
        compiler_params=params(),
        cost_estimate=cost(2688 * 1280 * 10, 7_000_000),
        name="phase_table",
    )(own, row_latitude, points, waves)

    grid_row, outgoing = pl.pallas_call(
        row_kernel,
        in_specs=[SMEM, SMEM, SMEM, SMEM, VMEM, VMEM, VMEM, VMEM, VMEM],
        out_specs=[VMEM, VMEM],
        out_shape=[
            jax.ShapeDtypeStruct((256, row_width), BF16),
            jax.ShapeDtypeStruct((ROWS, 128), BF16),
        ],
        scratch_shapes=[
            pltpu.VMEM((ROWS, 128), F32),
            pltpu.VMEM((ROWS, 128), F32),
            pltpu.VMEM((256, WAVES), BF16),
            pltpu.VMEM((256, row_width), BF16),
        ],
        compiler_params=params(),
        cost_estimate=cost(4 * 256 * 2688 * 1280, 10_000_000),
        name="grid_row",
    )(own, row_latitude, points, cutoffs, received, waves, table, vertical, factor)

    returned = everywhere(outgoing)
    grid_row, returned = lax.optimization_barrier((grid_row, returned))
    grid_field = lax.all_to_all(
        grid_row.reshape(NB, NB, row_width), "lev", split_axis=0, concat_axis=0, tiled=True
    )

    round_trip = pl.pallas_call(
        lambda *refs: final_kernel(truncation, *refs),
        grid=(GROUPS,),
        in_specs=[
            SMEM, SMEM, whole((1, 256)), whole((1, 256)), whole((ROWS, 128)),
            pl.BlockSpec((4, width, 128), lambda i: (i, 0, 0)),
        ],
        out_specs=pl.BlockSpec((4, 2, 16, width), lambda i: (i, 0, 0, 0)),
        out_shape=jax.ShapeDtypeStruct((20, 2, 16, width), F32),
        scratch_shapes=[pltpu.VMEM((ROWS, 128), F32)],
        compiler_params=params(),
        cost_estimate=cost(2 * 20 * 128 * 768 * 128, 6_000_000),
        name="legendre_return",
    )(
        band, slot_pair, lane_latitude, jnp.concatenate([weights, weights]).reshape(1, 256),
        returned, legendre,
    )
    return (grid_field, round_trip.transpose(2, 1, 0, 3))


def solution(mesh):
    in_specs = (
        P("lev", None, "band", None),
        P("band", None, None),
        P(),
        P(),
        P("band", None),
        P(),
        P(),
        P(),
        P(),
    )
    out_specs = (P("band", "lev", None), P("lev", None, "band", None))
    return jax.shard_map(
        per_device, mesh=mesh, in_specs=in_specs, out_specs=out_specs, check_vma=False
    )
```

time: 130 us -> 120 us (0.923); the launches traced: 129 us -> 118 us
  Pallas kernels: 35.7 us -> 22.2 us
  blocking collectives: 35.3 us -> 29.1 us
  starting transfers between devices: 15.1 us -> 20.1 us
  waiting for transfers between devices: 26.3 us -> 27.8 us
    pallas_call x3 -> x2, Pallas kernels: 24.9 us -> 13.2 us  [the longest x1 9.9 us: per_device(): pl.pallas_call(row_kernel, in_specs=[SMEM, SMEM, SMEM, SMEM, VMEM, VMEM,...]
    all_to_all x2 -> x1, blocking collectives: 35.3 us -> 29.1 us  [everywhere(): lax.all_to_all(pieces, ('band', 'lev'), split_axis=0, concat_axis=0, tile...]
    all_to_all x2, starting transfers between devices: 15.1 us -> 20.1 us  [the longest x1 15.7 us: everywhere(): lax.all_to_all(pieces, ('band', 'lev'), split_axis=0, concat_axis=0, tile...]
    unnamed x24 -> x27, local copies, waits for them, and re-layouts: 14.1 us -> 16.6 us
    all_to_all x2, waiting for transfers between devices: 26.3 us -> 27.8 us  [the longest x1 15.1 us: everywhere(): lax.all_to_all(pieces, ('band', 'lev'), split_axis=0, concat_axis=0, tile...]
  transfers between devices with their start and end apart: 2 -> 2, of which waited for: 2 -> 2; matrix products, arithmetic and copies ran while one was open for 1% -> 3% of each run, Pallas kernels for 7% -> 6%
where the time goes in v2:
time: 120 us; the launch traced here: 118 us
  blocking collectives  29.1 us (24%)
  waiting for transfers between devices  27.8 us (23%)
  Pallas kernels  22.2 us (18%)
  starting transfers between devices  20.1 us (17%)
  local copies, waits for them, and re-layouts  17 us (14%)
    all_to_all x1, blocking collectives, everywhere(): lax.all_to_all(pieces, ('band', 'lev'), split_axis=0, concat_axis=0, tile...  29.1 us
    unnamed x27, local copies, waits for them, and re-layouts  16.6 us
    all_to_all x1, starting transfers between devices, everywhere(): lax.all_to_all(pieces, ('band', 'lev'), split_axis=0, concat_axis=0, tile...  15.7 us
    all_to_all x1, waiting for transfers between devices, everywhere(): lax.all_to_all(pieces, ('band', 'lev'), split_axis=0, concat_axis=0, tile...  15.1 us
    all_to_all x1, waiting for transfers between devices, per_device(): lax.all_to_all(grid_row.reshape(NB, NB, row_width), 'lev', split_axis=0,...  12.7 us
    pallas_call x1, Pallas kernels, per_device(): pl.pallas_call(row_kernel, in_specs=[SMEM, SMEM, SMEM, SMEM, VMEM, VMEM,...  9.9 us
    pallas_call x1, Pallas kernels, per_device(): pl.pallas_call(lambda *refs: send_kernel(truncation, *refs), grid=(GROUPS...  4.92 us
    all_to_all x1, starting transfers between devices, per_device(): lax.all_to_all(grid_row.reshape(NB, NB, row_width), 'lev', split_axis=0,...  4.4 us
  transfers between devices with their start and end apart: 2, of which 2 were waited for; matrix products, arithmetic and copies ran while one was open for 3% of the time, Pallas kernels for 6%

profile of v2, /device:TPU:1, one launch (start us, length us, event | category | flops | bytes accessed | tf_op | source)
XLA Modules:
  0.0 117.8 jit_solution(13776691822901407260)
XLA Ops:
  0.6 0.0 copy-start.6
  0.6 0.0 copy-start.7
  0.7 1.4 %copy.25 = bf16[16,2,20,641]{3,0,1,2:T(8,128)(2,1)S(1)} copy(bf16[16,2,20,641]{3,1,2,0:T(2,128)(2,1)} %param.9) | data formatting | bytes 1640960 | tf_op args[0]
  2.0 0.0 copy-done.6
  2.1 0.0 copy-done.7
  2.1 0.0 copy-start
  2.1 1.9 %copy-done = bf16[20,128,641]{1,2,0:T(8,128)(2,1)S(1)} copy-done((bf16[20,128,641]{1,2,0:T(8,128)(2,1)S(1)}, bf16[20,128,641]{1,2,0:T(8,128)(2,1)}, u32[]{:S(2)}) %copy-start) | copy-done | bytes 3281944
  4.0 0.0 copy-start.8
  4.0 4.9 %legendre_send.1 = bf16[2560,128]{1,0:T(8,128)(2,1)} custom-call(s32[1]{0:T(128)} %bitcast.1.refs_0_, s32[320]{0:T(512)S(1)} %copy-done.6, s32[1,256]{1,0:T(1,128)S(1)} %bitcast.30, bf16[20,2,16,641]{3,2,1,0:T(8,128)(2,1)S(1)} %bitcast.25, bf16[20,641,128]{2,1,0:T(8,128)(2,1)S(1)} %bitcast.22), custom_call_target="tpu_custom_call" | custom-call | flops 503316480 | bytes 5000000 | tf_op jit(solution)/shard_map/legendre_send/pallas_call | solution.py:225
  8.9 15.7 %all-to-all-start = ((bf16[1280,2,128]{2,1,0:T(2,128)(2,1)}), bf16[1280,2,128]{2,1,0:T(2,128)(2,1)S(1)}, u32[]{:S(2)}, u32[]{:S(2)}) async-start(bf16[1280,2,128]{2,1,0:T(2,128)(2,1)} %bitcast.5), calls=%async_computation | async-start | bytes 1310720 | tf_op jit(solution)/shard_map/all_to_all | solution.py:203
  24.6 0.1 reshape.53
  24.7 0.1 copy.21
  24.8 0.1 copy.19
  24.9 0.1 add_convert_fusion
  25.0 0.1 convert_element_type.9.waves
  25.1 0.0 copy-done.8
  25.1 0.0 copy-start.9
  25.1 0.0 copy-start.10
  25.1 3.3 %phase_table.1.table = bf16[2688,1280]{1,0:T(8,128)(2,1)S(1)} custom-call(s32[1]{0:T(128)} %bitcast.own, s32[256]{0:T(256)S(1)} %copy-done.7, s32[128]{0:T(128)S(1)} %copy-done.8, f32[1,1280]{1,0:T(1,128)S(1)} %convert_element_type.9.waves), custom_call_target="tpu_custom_call" | custom-call | flops 34406400 | bytes 7000000 | tf_op jit(solution)/shard_map/phase_table/pallas_call | solution.py:246
  28.5 0.0 copy-start.2
  28.5 2.8 %copy-done.2 = bf16[2688,1280]{1,0:T(8,128)(2,1)} copy-done((bf16[2688,1280]{1,0:T(8,128)(2,1)}, bf16[2688,1280]{1,0:T(8,128)(2,1)S(1)}, u32[]{:S(2)}) %copy-start.2) | copy-done | bytes 6881304
  31.3 0.8 dynamic-slice_convert_fusion.factor
  32.1 15.1 %all-to-all-done = bf16[1280,2,128]{2,1,0:T(2,128)(2,1)S(1)} async-done(((bf16[1280,2,128]{2,1,0:T(2,128)(2,1)}), bf16[1280,2,128]{2,1,0:T(2,128)(2,1)S(1)}, u32[]{:S(2)}, u32[]{:S(2)}) %all-to-all-start) | async-done | bytes 655392 | tf_op jit(solution)/shard_map/all_to_all | solution.py:203
  47.2 0.0 copy-done.9
  47.2 0.0 copy-done.10
  47.2 0.0 copy-start.3
  47.2 3.0 %copy-done.3 = bf16[2688,1280]{1,0:T(8,128)(2,1)S(1)} copy-done((bf16[2688,1280]{1,0:T(8,128)(2,1)S(1)}, bf16[2688,1280]{1,0:T(8,128)(2,1)}, u32[]{:S(2)}) %copy-start.3) | copy-done | bytes 6881304
  50.2 9.9 %grid_row.1 = (bf16[256,2688]{1,0:T(8,128)(2,1)S(1)}, bf16[2560,128]{1,0:T(8,128)(2,1)S(1)}) custom-call(s32[1]{0:T(128)} %bitcast.own, s32[256]{0:T(256)S(1)} %copy-done.7, s32[128]{0:T(128)S(1)} %copy-done.8, s32[128]{0:T(128)S(1)} %copy-done.10, bf16[2560,128]{1,0:T(8,128)(2,1)S(1)} %bitcast.28, f32[1,1280]{1,0:T(1,128)S(1)} %convert_element_type.9.waves, ...), custom_call_target="tpu_custom_call" | custom-call | flops 3523215360 | bytes 10000000 | tf_op jit(solution)/shard_map/grid_row/pallas_call | solution.py:257
  60.1 0.0 copy-start.5
  60.1 1.1 copy-done.5
  61.2 0.0 copy-start.11
  61.2 0.0 copy-start.1
  61.2 29.1 %all_to_all.15 = bf16[1280,2,128]{2,1,0:T(2,128)(2,1)} all-to-all(bf16[1280,2,128]{2,1,0:T(2,128)(2,1)S(1)} %bitcast.29), channel_id=1, replica_groups=mesh['band'=16,'lev'=16] {'band','lev'}, dimensions={0} | all-to-all | bytes 1310720 | tf_op jit(solution)/shard_map/all_to_all | solution.py:203
  90.2 4.4 %all-to-all-start.2 = ((bf16[16,16,2688]{2,1,0:T(8,128)(2,1)}), bf16[16,16,2688]{2,1,0:T(8,128)(2,1)}, u32[]{:S(2)}, u32[]{:S(2)}) async-start(bf16[16,16,2688]{2,1,0:T(8,128)(2,1)} %bitcast.27), calls=%async_computation.2 | async-start | bytes 2752512 | tf_op jit(solution)/shard_map/all_to_all | solution.py:278
  94.6 0.0 copy-done.11
  94.7 0.0 copy-done.1
  94.7 0.0 copy-start.4
  94.7 1.1 copy-done.4
  95.8 4.0 %legendre_return.1 = f32[20,2,16,641]{3,2,1,0:T(8,128)S(1)} custom-call(s32[1]{0:T(128)} %bitcast.1.refs_0_, s32[320]{0:T(512)S(1)} %copy-done.6, s32[1,256]{1,0:T(1,128)S(1)} %bitcast.31, f32[1,256]{1,0:T(1,128)S(1)} %bitcast.32, bf16[2560,128]{1,0:T(8,128)(2,1)S(1)} %bitcast.26, bf16[20,641,128]{2,1,0:T(8,128)(2,1)S(1)} %bitcast.23), custom_call_target="tpu_custom_call" | custom-call | flops 503316480 | bytes 6000000 | tf_op jit(solution)/shard_map/legendre_return/pallas_call | solution.py:282
  99.8 2.8 %copy.23 = f32[16,2,20,641]{3,1,2,0:T(2,128)} copy(f32[16,2,20,641]{3,0,1,2:T(8,128)S(1)} %bitcast.24) | data formatting | bytes 3281920
  102.6 12.7 %all-to-all-done.2 = bf16[16,16,2688]{2,1,0:T(8,128)(2,1)} async-done(((bf16[16,16,2688]{2,1,0:T(8,128)(2,1)}), bf16[16,16,2688]{2,1,0:T(8,128)(2,1)}, u32[]{:S(2)}, u32[]{:S(2)}) %all-to-all-start.2) | async-done | bytes 1376288 | tf_op jit(solution)/shard_map/all_to_all | solution.py:278
  115.3 2.5 %copy.27 = bf16[16,16,2688]{2,1,0:T(8,128)(2,1)} copy(bf16[16,16,2688]{2,1,0:T(8,128)(2,1)} %all-to-all-done.2) | data formatting | bytes 2752512
  (2 shorter events, 0.0 us)
Async XLA Ops:
  0.6 1.4 %copy-start.6 = (s32[320]{0:T(512)S(1)}, s32[320]{0:T(512)}, u32[]{:S(2)}) copy-start(s32[320]{0:T(512)} %refs_1_.3) | copy-start | bytes 3844
  0.6 1.4 %copy-start.7 = (s32[256]{0:T(256)S(1)}, s32[256]{0:T(256)}, u32[]{:S(2)}) copy-start(s32[256]{0:T(256)} %row_latitude.3) | copy-start | bytes 3076
  2.1 1.9 %copy-start = (bf16[20,128,641]{1,2,0:T(8,128)(2,1)S(1)}, bf16[20,128,641]{1,2,0:T(8,128)(2,1)}, u32[]{:S(2)}) copy-start(bf16[20,128,641]{1,2,0:T(8,128)(2,1)} %param.10) | copy-start | bytes 9845764
  4.0 21.1 %copy-start.8 = (s32[128]{0:T(128)S(1)}, s32[128]{0:T(128)}, u32[]{:S(2)}) copy-start(s32[128]{0:T(128)} %points.3) | copy-start | bytes 1540
  8.9 38.3 %all-to-all-start = ((bf16[1280,2,128]{2,1,0:T(2,128)(2,1)}), bf16[1280,2,128]{2,1,0:T(2,128)(2,1)S(1)}, u32[]{:S(2)}, u32[]{:S(2)}) async-start(bf16[1280,2,128]{2,1,0:T(2,128)(2,1)} %bitcast.5), calls=%async_computation | async-start | bytes 1310720 | tf_op jit(solution)/shard_map/all_to_all | solution.py:203
  25.1 22.1 %copy-start.9 = (bf16[256,256]{1,0:T(8,128)(2,1)S(1)}, bf16[256,256]{1,0:T(8,128)(2,1)}, u32[]{:S(2)}) copy-start(bf16[256,256]{1,0:T(8,128)(2,1)} %vertical.1) | copy-start | bytes 393220
  25.1 22.1 %copy-start.10 = (s32[128]{0:T(128)S(1)}, s32[128]{0:T(128)}, u32[]{:S(2)}) copy-start(s32[128]{0:T(128)} %cutoffs.1) | copy-start | bytes 1540
  28.5 2.9 %copy-start.2 = (bf16[2688,1280]{1,0:T(8,128)(2,1)}, bf16[2688,1280]{1,0:T(8,128)(2,1)S(1)}, u32[]{:S(2)}) copy-start(bf16[2688,1280]{1,0:T(8,128)(2,1)S(1)} %phase_table.1.table) | copy-start | bytes 20643844
  47.2 3.0 %copy-start.3 = (bf16[2688,1280]{1,0:T(8,128)(2,1)S(1)}, bf16[2688,1280]{1,0:T(8,128)(2,1)}, u32[]{:S(2)}) copy-start(bf16[2688,1280]{1,0:T(8,128)(2,1)} %copy-done.2) | copy-start | bytes 20643844
  60.1 1.1 copy-start.5
  61.2 33.5 %copy-start.11 = (f32[128]{0:T(128)S(1)}, f32[128]{0:T(128)}, u32[]{:S(2)}) copy-start(f32[128]{0:T(128)} %param.11) | copy-start | bytes 1540
  61.2 33.5 %copy-start.1 = (bf16[20,128,641]{1,2,0:T(8,128)(2,1)S(1)}, bf16[20,128,641]{1,2,0:T(8,128)(2,1)}, u32[]{:S(2)}) copy-start(bf16[20,128,641]{1,2,0:T(8,128)(2,1)} %param.10) | copy-start | bytes 9845764
  90.2 25.1 %all-to-all-start.2 = ((bf16[16,16,2688]{2,1,0:T(8,128)(2,1)}), bf16[16,16,2688]{2,1,0:T(8,128)(2,1)}, u32[]{:S(2)}, u32[]{:S(2)}) async-start(bf16[16,16,2688]{2,1,0:T(8,128)(2,1)} %bitcast.27), calls=%async_computation.2 | async-start | bytes 2752512 | tf_op jit(solution)/shard_map/all_to_all | solution.py:278
  94.7 1.1 copy-start.4

commit v3 on v1

--- a/solution.py
+++ b/solution.py
@@ -10,6 +10,7 @@
 F32, BF16 = jnp.float32, jnp.bfloat16
 NB = 16
 GROUPS = 5
+ROWS = 2560
 WAVES = 1280
 COS = (1.0, -19.739208221435547, 64.93938446044922, -85.45658111572266,
        60.241241455078125, -26.39919662475586, 7.783571243286133, -1.4335278272628784)
@@ -18,7 +19,7 @@
 NT = (((1,), (1,)), ((), ()))
 
 
-def params(limit=40):
+def params(limit=24):
     return pltpu.CompilerParams(vmem_limit_bytes=limit * 1024 * 1024)
 
 
@@ -44,6 +45,23 @@
             items[low + step] = tuple(
                 jnp.where(keep, pltpu.roll(a[h], 128 - shift, 1), b[h]) for h in (0, 1)
             )
+    return items
+
+
+def exchange_lanes(items, width):
+    items = list(items)
+    lane = lax.broadcasted_iota(jnp.int32, items[0].shape, 1)
+    count = len(items)
+    for level in range(count.bit_length() - 1):
+        step = 1 << level
+        shift = width * step
+        keep = (lane & shift) == 0
+        for low in range(count):
+            if low & step:
+                continue
+            a, b = items[low], items[low + step]
+            items[low] = jnp.where(keep, a, pltpu.roll(b, shift, 1))
+            items[low + step] = jnp.where(keep, pltpu.roll(a, 128 - shift, 1), b)
     return items
 
 
@@ -188,46 +206,42 @@
                 total_cos = total_cos + block * outer_cos[r, b : b + 1, lanes]
                 total_sin = total_sin + block * outer_sin[r, b : b + 1, lanes]
             value = sign[:, lanes] * total_cos - swap_parts(total_sin)
-            fourier[row, :, lanes] = value * scale[:, lanes]
-
-    @pl.when(step == pl.num_programs(0) - 1)
-    def _():
-        for g in range(GROUPS):
-            items = [
-                (fourier[row, :, 256 * g : 256 * g + 128],
-                 fourier[row, :, 256 * g + 128 : 256 * g + 256])
-                for row in range(NB)
-            ]
-            for b, (lo, hi) in enumerate(exchange_chunks(items, 16)):
-                out[b, g, :, :128] = lo.astype(BF16)
-                out[b, g, :, 128:] = hi.astype(BF16)
-
-
-def mix_kernel(vertical, received, out):
-    matrix = vertical[...]
-    devices, chunks = received.shape[:2]
-    for chunk in range(chunks):
-        for g in range(GROUPS):
-            block = received[:, chunk, g].reshape(devices * 16, 256)
-            value = dot(matrix, block).astype(BF16)
-            out[:, chunk, g] = value.reshape(devices, 16, 256)
-
-
-def final_kernel(truncation, band, slot_pair, lane_latitude, weights, received, legendre, out, sums):
+            out[r, :, lanes] = (value * scale[:, lanes]).astype(BF16)
+
+
+def mix_kernel(vertical, received, out, levels, rows):
+    block = received[...].reshape(256, WAVES)
+    for t in range(10):
+        levels[256 * t : 256 * (t + 1), :] = dot(vertical[...], block[:, 128 * t : 128 * (t + 1)])
+    for t in range(10):
+        for high in range(2):
+            first = 256 * t + 8 * high
+            items = [levels[pl.ds(first + l, 16, stride=16), :] for l in range(8)]
+            for b, item in enumerate(exchange_lanes(items, 16)):
+                start = 160 * (8 * (t % 2) + b) + 2 * (t // 2) + high
+                rows[pl.ds(start, 16, stride=10), :] = item
+    out[...] = rows[...].astype(BF16)
+
+
+def final_kernel(truncation, band, slot_pair, lane_latitude, weights, received, legendre, out, rows):
     group = pl.program_id(0)
     width = legendre.shape[1]
-    items = []
-    for src in range(NB):
-        block = received[src, 0].astype(F32)
-        items.append((block[:, :128], block[:, 128:]))
-    for u, (lo, hi) in enumerate(exchange_chunks(items, 1)):
-        sums[16 * u : 16 * (u + 1), :128] = lo.astype(BF16)
-        sums[16 * u : 16 * (u + 1), 128:] = hi.astype(BF16)
+
+    @pl.when(group == 0)
+    def _():
+        rows[...] = received[...].astype(F32)
+
+    values = jnp.concatenate(
+        [rows[pl.ds(2 * group + h, 256, stride=10), :].astype(BF16) for h in (0, 1)], 1
+    )
     target = lax.broadcasted_iota(jnp.int32, (256, 256), 0)
+    lane = lax.broadcasted_iota(jnp.int32, (256, 256), 1)
+    swap = (lane >> 4 == (target & 15)) & ((lane & 15) == target >> 4)
+    turned = dot(swap.astype(F32).astype(BF16), values, NT).astype(BF16)
     source = lane_latitude[...]
     value = jnp.where((target >= 128) & (source >= 128), F32(-1.0), F32(1.0))
     fold = jnp.where((target & 127) == (source & 127), value, 0.0).astype(BF16)
-    parts = (dot(sums[...], fold, NT) * weights[...]).astype(BF16)
+    parts = (dot(turned, fold, NT) * weights[...]).astype(BF16)
     for s in range(4):
         first, odd = slot_columns(slot_pair[band[0] * 20 + group * 4 + s], width, truncation)
         own = parts[64 * s : 64 * (s + 1)]
@@ -245,17 +259,23 @@
 
 
 SMEM = pl.BlockSpec(memory_space=pltpu.SMEM)
+VMEM = pl.BlockSpec(memory_space=pltpu.VMEM)
 
 
 def cost(flops, size):
     return pl.CostEstimate(flops=flops, bytes_accessed=size, transcendentals=0)
+
+
+def everywhere(message):
+    pieces = message.reshape(ROWS // 2, 2, 128)
+    pieces = lax.all_to_all(pieces, ("band", "lev"), split_axis=0, concat_axis=0, tiled=True)
+    return pieces.reshape(ROWS, 128)
 
 
 def per_device(
     spectral, legendre, weights, vertical, grid_factor, points, cutoffs, row_latitude, slot_pair
 ):
     band = lax.axis_index("band").astype(jnp.int32).reshape(1)
-    lev_count = lax.axis_size("lev")
     truncation = 2 * slot_pair.shape[0] - 1
     width = spectral.shape[3]
     row_width = grid_factor.shape[1]
@@ -319,11 +339,11 @@
         ],
         out_specs=[
             pl.BlockSpec((per_step, 16, row_width), lambda i: (i, 0, 0)),
-            whole((NB, GROUPS, 16, 256)),
+            pl.BlockSpec((per_step, 16, WAVES), lambda i: (i, 0, 0)),
         ],
         out_shape=[
             jax.ShapeDtypeStruct((NB, 16, row_width), BF16),
-            jax.ShapeDtypeStruct((NB, GROUPS, 16, 256), BF16),
+            jax.ShapeDtypeStruct((NB, 16, WAVES), BF16),
         ],
         scratch_shapes=[
             pltpu.VMEM((NB, 16, WAVES), F32),
@@ -336,38 +356,33 @@
     )(band, row_latitude, points, cutoffs, received, waves, table, outer_cos, outer_sin, factor)
 
     levels_in = lax.all_to_all(harmonic, "lev", split_axis=0, concat_axis=0, tiled=True)
-    shape = (lev_count, NB // lev_count, GROUPS, 16, 256)
-    mixed = pl.pallas_call(
+    outgoing = pl.pallas_call(
         mix_kernel,
-        grid=(1,),
-        in_specs=[whole(vertical.shape), whole(shape)],
-        out_specs=whole(shape),
-        out_shape=jax.ShapeDtypeStruct(shape, BF16),
+        in_specs=[VMEM, VMEM],
+        out_specs=VMEM,
+        out_shape=jax.ShapeDtypeStruct((ROWS, 128), BF16),
+        scratch_shapes=[pltpu.VMEM((ROWS, 128), F32), pltpu.VMEM((ROWS, 128), F32)],
         compiler_params=params(),
         cost_estimate=cost(2 * 256 * 256 * 1280, 1_400_000),
         name="vertical_mix",
-    )(vertical, levels_in.reshape(shape))
-    outgoing = lax.all_to_all(
-        mixed.reshape(NB, GROUPS, 16, 256), "lev", split_axis=0, concat_axis=0, tiled=True
-    )
-    returned = lax.all_to_all(outgoing, "band", split_axis=0, concat_axis=0, tiled=True)
+    )(vertical, levels_in)
+    returned = everywhere(outgoing)
 
     round_trip = pl.pallas_call(
         lambda *refs: final_kernel(truncation, *refs),
         grid=(GROUPS,),
         in_specs=[
-            SMEM, SMEM, whole((1, 256)), whole((1, 256)),
-            pl.BlockSpec((NB, 1, 16, 256), lambda i: (0, i, 0, 0)),
+            SMEM, SMEM, whole((1, 256)), whole((1, 256)), whole((ROWS, 128)),
             pl.BlockSpec((4, width, 128), lambda i: (i, 0, 0)),
         ],
         out_specs=pl.BlockSpec((4, 2, 16, width), lambda i: (i, 0, 0, 0)),
         out_shape=jax.ShapeDtypeStruct((20, 2, 16, width), F32),
-        scratch_shapes=[pltpu.VMEM((256, 256), BF16)],
+        scratch_shapes=[pltpu.VMEM((ROWS, 128), F32)],
         compiler_params=params(),
         cost_estimate=cost(2 * 20 * 128 * 768 * 128, 6_000_000),
         name="legendre_return",
     )(
-        band, slot_pair, lane_latitude, jnp.concatenate([weights, weights]).reshape(1, 256),
+        band, slot_pair, row_latitude.reshape(1, 256), jnp.concatenate([weights, weights]).reshape(1, 256),
         returned, legendre,
     )
     return (grid_field, round_trip.transpose(2, 1, 0, 3))

time: 130 us -> 118 us (0.908)
  blocking collectives: 35.3 us -> 19.2 us
  starting transfers between devices: 15.1 us -> 17.1 us
  waiting for transfers between devices: 26.3 us -> 28 us
    all_to_all x1 -> x0, blocking collectives: 16.4 us -> none  [per_device(): lax.all_to_all(mixed.reshape(NB, GROUPS, 16, 256), 'lev', split_axis=0, c...]
    pallas_call x1, Pallas kernels: 0.34 us -> 2.67 us  [per_device(): pl.pallas_call(mix_kernel, in_specs=[VMEM, VMEM], out_specs=VMEM, out_sha...]
    all_to_all x1, starting transfers between devices: 4.94 us -> 6.95 us  [everywhere(): lax.all_to_all(pieces, ('band', 'lev'), split_axis=0, concat_axis=0, tile...]
    all_to_all x1, waiting for transfers between devices: 20.1 us -> 21.8 us  [everywhere(): lax.all_to_all(pieces, ('band', 'lev'), split_axis=0, concat_axis=0, tile...]
    unnamed x24 -> x26, local copies, waits for them, and re-layouts: 14.1 us -> 14.9 us
where the time goes in v3:
time: 118 us
  Pallas kernels  36.2 us (31%)
  waiting for transfers between devices  28 us (24%)
  blocking collectives  19.2 us (16%)
  starting transfers between devices  17.1 us (14%)
  local copies, waits for them, and re-layouts  16.5 us (14%)
    all_to_all x1, waiting for transfers between devices, everywhere(): lax.all_to_all(pieces, ('band', 'lev'), split_axis=0, concat_axis=0, tile...  21.8 us
    all_to_all x1, blocking collectives, per_device(): lax.all_to_all(harmonic, 'lev', split_axis=0, concat_axis=0, tiled=True)  19.2 us
    pallas_call x1, Pallas kernels, per_device(): pl.pallas_call(lambda *refs: rows_kernel(per_step, *refs), grid=(NB // pe...  15 us
    unnamed x26, local copies, waits for them, and re-layouts  14.9 us
    all_to_all x1, starting transfers between devices, per_device(): lax.all_to_all(message, 'band', split_axis=0, concat_axis=0, tiled=True)  10.1 us
    pallas_call x1, Pallas kernels, per_device(): pl.pallas_call(lambda *refs: table_kernel(per_step, *refs), grid=(NB // p...  8.43 us
    all_to_all x1, starting transfers between devices, everywhere(): lax.all_to_all(pieces, ('band', 'lev'), split_axis=0, concat_axis=0, tile...  6.95 us
    all_to_all x1, waiting for transfers between devices, per_device(): lax.all_to_all(message, 'band', split_axis=0, concat_axis=0, tiled=True)  6.21 us
  transfers between devices with their start and end apart: 2, of which 2 were waited for; matrix products, arithmetic and copies ran while one was open for 1% of the time, Pallas kernels for 7%

profile of v3, /device:TPU:1, one launch (start us, length us, event | category | flops | bytes accessed | tf_op | source)
XLA Modules:
  0.0 117.8 jit_solution(66571386011203384)
XLA Ops:
  0.6 0.0 copy-start.7
  0.6 0.0 copy-start.6
  0.7 1.4 %copy.35 = bf16[16,2,20,641]{3,0,1,2:T(8,128)(2,1)S(1)} copy(bf16[16,2,20,641]{3,1,2,0:T(2,128)(2,1)} %param.9) | data formatting | bytes 1640960 | tf_op args[0]
  2.0 0.0 copy-done.7
  2.1 0.1 reshape.49
  2.1 0.1 copy.27
  2.2 0.1 reshape.50.refs_2_
  2.3 0.0 copy-done.6
  2.3 0.0 copy-start
  2.3 1.9 %copy-done = bf16[20,128,641]{1,2,0:T(8,128)(2,1)S(1)} copy-done((bf16[20,128,641]{1,2,0:T(8,128)(2,1)S(1)}, bf16[20,128,641]{1,2,0:T(8,128)(2,1)}, u32[]{:S(2)}) %copy-start) | copy-done | bytes 3281944
  4.2 5.6 %legendre_send.1 = bf16[16,5,16,256]{3,2,1,0:T(8,128)(2,1)} custom-call(s32[1]{0:T(128)} %bitcast.refs_0_, s32[320]{0:T(512)S(1)} %copy-done.6, s32[1,256]{1,0:T(1,128)S(1)} %reshape.50.refs_2_, bf16[20,2,16,641]{3,2,1,0:T(8,128)(2,1)S(1)} %bitcast.26, bf16[20,641,128]{2,1,0:T(8,128)(2,1)S(1)} %bitcast.23), custom_call_target="tpu_custom_call" | custom-call | flops 503316480 | bytes 5000000 | tf_op jit(solution)/shard_map/legendre_send/pallas_call | solution.py:289
  9.8 0.0 copy-start.10
  9.8 0.0 copy-start.8
  9.8 0.0 copy-start.9
  9.8 10.1 %all-to-all-start = ((bf16[16,5,16,256]{3,2,1,0:T(8,128)(2,1)}), bf16[16,5,16,256]{3,2,1,0:T(8,128)(2,1)S(1)}, u32[]{:S(2)}, u32[]{:S(2)}) async-start(bf16[16,5,16,256]{3,2,1,0:T(8,128)(2,1)} %legendre_send.1), calls=%async_computation | async-start | bytes 1310720 | tf_op jit(solution)/shard_map/all_to_all | solution.py:304
  19.9 0.1 reshape.51
  20.0 0.1 copy.29
  20.2 0.2 copy.32
  20.4 0.4 broadcast_in_dim.2
  20.8 0.4 convert_element_type.7.refs_3_.refs_5_
  21.2 0.0 copy-done.10
  21.2 0.1 reshape.59.refs_9_
  21.3 0.0 copy-done.8
  21.3 8.4 %phase_tables.1 = (bf16[16,256,1280]{2,1,0:T(8,128)(2,1)S(1)}, f32[16,16,1280]{2,1,0:T(8,128)S(1)}, f32[16,16,1280]{2,1,0:T(8,128)S(1)}) custom-call(s32[1]{0:T(128)} %bitcast.refs_0_, s32[256]{0:T(256)S(1)} %copy-done.7, s32[128]{0:T(128)S(1)} %copy-done.8, f32[1,1280]{1,0:T(1,128)S(1)} %convert_element_type.7.refs_3_.refs_5_), custom_call_target="tpu_custom_call" | custom-call | flops 104857600 | bytes 14000000 | tf_op jit(solution)/shard_map/phase_tables/pallas_call | solution.py:307
  29.8 0.0 copy-start.2
  29.8 4.0 %copy-done.2 = bf16[16,256,1280]{2,1,0:T(8,128)(2,1)} copy-done((bf16[16,256,1280]{2,1,0:T(8,128)(2,1)}, bf16[16,256,1280]{2,1,0:T(8,128)(2,1)S(1)}, u32[]{:S(2)}) %copy-start.2) | copy-done | bytes 10485784
  33.7 6.2 %all-to-all-done.refs_4_ = bf16[16,5,16,256]{3,2,1,0:T(8,128)(2,1)S(1)} async-done(((bf16[16,5,16,256]{3,2,1,0:T(8,128)(2,1)}), bf16[16,5,16,256]{3,2,1,0:T(8,128)(2,1)S(1)}, u32[]{:S(2)}, u32[]{:S(2)}) %all-to-all-start) | async-done | bytes 655392 | tf_op jit(solution)/shard_map/all_to_all | solution.py:304
  40.0 0.0 copy-done.9
  40.0 0.0 copy-start.3
  40.0 4.0 %copy-done.3 = bf16[16,256,1280]{2,1,0:T(8,128)(2,1)S(1)} copy-done((bf16[16,256,1280]{2,1,0:T(8,128)(2,1)S(1)}, bf16[16,256,1280]{2,1,0:T(8,128)(2,1)}, u32[]{:S(2)}) %copy-start.3) | copy-done | bytes 10485784
  43.9 0.0 copy-start.5
  43.9 15.0 %grid_rows.1 = (bf16[16,16,2688]{2,1,0:T(8,128)(2,1)}, bf16[16,16,1280]{2,1,0:T(8,128)(2,1)S(1)}) custom-call(s32[1]{0:T(128)} %bitcast.refs_0_, s32[256]{0:T(256)S(1)} %copy-done.7, s32[128]{0:T(128)S(1)} %copy-done.8, s32[128]{0:T(128)S(1)} %copy-done.9, bf16[16,5,16,256]{3,2,1,0:T(8,128)(2,1)S(1)} %all-to-all-done.refs_4_, ...), custom_call_target="tpu_custom_call" | custom-call | flops 3690987520 | bytes 17000000 | tf_op jit(solution)/shard_map/grid_rows/pallas_call | solution.py:328
  58.9 0.0 copy-start.11
  58.9 0.0 copy-start.1
  58.9 19.2 %all_to_all.15.received = bf16[16,16,1280]{2,1,0:T(8,128)(2,1)S(1)} all-to-all(bf16[16,16,1280]{2,1,0:T(8,128)(2,1)S(1)} %get-tuple-element.11), channel_id=1, replica_groups=mesh['band'=16,'lev'=16] {'lev'}, dimensions={0} | all-to-all | bytes 1310720 | tf_op jit(solution)/shard_map/all_to_all | solution.py:358
  78.1 0.0 copy-done.5
  78.1 2.7 %vertical_mix.1 = bf16[2560,128]{1,0:T(8,128)(2,1)S(1)} custom-call(bf16[256,256]{1,0:T(8,128)(2,1)S(1)} %copy-done.5, bf16[16,16,1280]{2,1,0:T(8,128)(2,1)S(1)} %all_to_all.15.received), custom_call_target="tpu_custom_call" | custom-call | flops 167772160 | bytes 1400000 | tf_op jit(solution)/shard_map/vertical_mix/pallas_call | solution.py:359
  80.8 0.0 copy-start.4
  80.8 0.8 copy-done.4
  81.6 6.9 %all-to-all-start.2 = ((bf16[1280,2,128]{2,1,0:T(2,128)(2,1)}), bf16[1280,2,128]{2,1,0:T(2,128)(2,1)}, u32[]{:S(2)}, u32[]{:S(2)}) async-start(bf16[1280,2,128]{2,1,0:T(2,128)(2,1)} %bitcast.27), calls=%async_computation.2 | async-start | bytes 1310720 | tf_op jit(solution)/shard_map/all_to_all | solution.py:271
  88.5 0.0 copy-done.11
  88.6 21.8 %all-to-all-done.2 = bf16[1280,2,128]{2,1,0:T(2,128)(2,1)} async-done(((bf16[1280,2,128]{2,1,0:T(2,128)(2,1)}), bf16[1280,2,128]{2,1,0:T(2,128)(2,1)}, u32[]{:S(2)}, u32[]{:S(2)}) %all-to-all-start.2) | async-done | bytes 655392 | tf_op jit(solution)/shard_map/all_to_all | solution.py:271
  110.4 0.0 copy-done.1
  110.4 4.6 %legendre_return.1 = f32[20,2,16,641]{3,2,1,0:T(8,128)S(1)} custom-call(s32[1]{0:T(128)} %bitcast.refs_0_, s32[320]{0:T(512)S(1)} %copy-done.6, s32[1,256]{1,0:T(1,128)S(1)} %bitcast.28, f32[1,256]{1,0:T(1,128)S(1)} %bitcast.29, bf16[2560,128]{1,0:T(8,128)(2,1)} %bitcast.12.refs_4_, bf16[20,641,128]{2,1,0:T(8,128)(2,1)S(1)} %bitcast.24), custom_call_target="tpu_custom_call" | custom-call | flops 503316480 | bytes 6000000 | tf_op jit(solution)/shard_map/legendre_return/pallas_call | solution.py:371
  115.0 2.8 %copy.33 = f32[16,2,20,641]{3,1,2,0:T(2,128)} copy(f32[16,2,20,641]{3,0,1,2:T(8,128)S(1)} %bitcast.25) | data formatting | bytes 3281920
  (3 shorter events, 0.0 us)
Async XLA Ops:
  0.6 1.4 %copy-start.7 = (s32[256]{0:T(256)S(1)}, s32[256]{0:T(256)}, u32[]{:S(2)}) copy-start(s32[256]{0:T(256)} %refs_1_.6) | copy-start | bytes 3076
  0.6 1.7 %copy-start.6 = (s32[320]{0:T(512)S(1)}, s32[320]{0:T(512)}, u32[]{:S(2)}) copy-start(s32[320]{0:T(512)} %refs_1_.7) | copy-start | bytes 3844
  2.3 1.9 %copy-start = (bf16[20,128,641]{1,2,0:T(8,128)(2,1)S(1)}, bf16[20,128,641]{1,2,0:T(8,128)(2,1)}, u32[]{:S(2)}) copy-start(bf16[20,128,641]{1,2,0:T(8,128)(2,1)} %param.10) | copy-start | bytes 9845764
  9.8 11.4 %copy-start.10 = (bf16[16,2688]{1,0:T(8,128)(2,1)S(1)}, bf16[16,2688]{1,0:T(8,128)(2,1)}, u32[]{:S(2)}) copy-start(bf16[16,2688]{1,0:T(8,128)(2,1)} %param.13) | copy-start | bytes 258052
  9.8 11.5 %copy-start.8 = (s32[128]{0:T(128)S(1)}, s32[128]{0:T(128)}, u32[]{:S(2)}) copy-start(s32[128]{0:T(128)} %refs_2_.3) | copy-start | bytes 1540
  9.8 30.1 %copy-start.9 = (s32[128]{0:T(128)S(1)}, s32[128]{0:T(128)}, u32[]{:S(2)}) copy-start(s32[128]{0:T(128)} %refs_3_.1) | copy-start | bytes 1540
  9.8 30.1 %all-to-all-start = ((bf16[16,5,16,256]{3,2,1,0:T(8,128)(2,1)}), bf16[16,5,16,256]{3,2,1,0:T(8,128)(2,1)S(1)}, u32[]{:S(2)}, u32[]{:S(2)}) async-start(bf16[16,5,16,256]{3,2,1,0:T(8,128)(2,1)} %legendre_send.1), calls=%async_computation | async-start | bytes 1310720 | tf_op jit(solution)/shard_map/all_to_all | solution.py:304
  29.8 4.0 %copy-start.2 = (bf16[16,256,1280]{2,1,0:T(8,128)(2,1)}, bf16[16,256,1280]{2,1,0:T(8,128)(2,1)S(1)}, u32[]{:S(2)}) copy-start(bf16[16,256,1280]{2,1,0:T(8,128)(2,1)S(1)} %get-tuple-element.7.refs_6_) | copy-start | bytes 31457284
  40.0 4.0 %copy-start.3 = (bf16[16,256,1280]{2,1,0:T(8,128)(2,1)S(1)}, bf16[16,256,1280]{2,1,0:T(8,128)(2,1)}, u32[]{:S(2)}) copy-start(bf16[16,256,1280]{2,1,0:T(8,128)(2,1)} %copy-done.2) | copy-start | bytes 31457284
  43.9 34.1 %copy-start.5 = (bf16[256,256]{1,0:T(8,128)(2,1)S(1)}, bf16[256,256]{1,0:T(8,128)(2,1)}, u32[]{:S(2)}) copy-start(bf16[256,256]{1,0:T(8,128)(2,1)} %vertical.1) | copy-start | bytes 393220
  58.9 29.6 %copy-start.11 = (f32[128]{0:T(128)S(1)}, f32[128]{0:T(128)}, u32[]{:S(2)}) copy-start(f32[128]{0:T(128)} %param.11) | copy-start | bytes 1540
  58.9 51.5 %copy-start.1 = (bf16[20,128,641]{1,2,0:T(8,128)(2,1)S(1)}, bf16[20,128,641]{1,2,0:T(8,128)(2,1)}, u32[]{:S(2)}) copy-start(bf16[20,128,641]{1,2,0:T(8,128)(2,1)} %param.10) | copy-start | bytes 9845764
  80.8 0.8 copy-start.4
  81.6 28.8 %all-to-all-start.2 = ((bf16[1280,2,128]{2,1,0:T(2,128)(2,1)}), bf16[1280,2,128]{2,1,0:T(2,128)(2,1)}, u32[]{:S(2)}, u32[]{:S(2)}) async-start(bf16[1280,2,128]{2,1,0:T(2,128)(2,1)} %bitcast.27), calls=%async_computation.2 | async-start | bytes 1310720 | tf_op jit(solution)/shard_map/all_to_all | solution.py:271

commit v4 on v3

--- a/solution.py
+++ b/solution.py
@@ -122,40 +122,67 @@
                 table[r, 16 * a : 16 * (a + 1), lanes] = value.astype(BF16)
 
 
-def send_kernel(truncation, band, slot_pair, lane_latitude, spectral, legendre, out, sums):
-    group = pl.program_id(0)
+def send_kernel(
+    truncation, band, slot_pair, lane_latitude, spectral, legendre, out, sums, spread, spectral_in,
+    legendre_in, messages, ready, sent
+):
     width = spectral.shape[-1]
+    whole_spectral = pltpu.make_async_copy(spectral, spectral_in, ready.at[GROUPS])
+    whole_spectral.start()
+    copies = []
+    for g in range(GROUPS):
+        cut = pl.ds(4 * g, 4)
+        copies.append(pltpu.make_async_copy(legendre.at[cut], legendre_in.at[cut], ready.at[g]))
+        copies[g].start()
     place = (
         lax.broadcasted_iota(jnp.int32, (256, 256), 0) == lane_latitude[...]
     ).astype(F32).astype(BF16)
-    for s in range(4):
-        first, odd = slot_columns(slot_pair[band[0] * 20 + group * 4 + s], width, truncation)
-        one = first.astype(F32)
-        sign = 1.0 - 2.0 * odd.astype(F32)
-        x = spectral[s].reshape(32, width)
-        picks = [one, 1.0 - one, one * sign, (1.0 - one) * sign]
-        left = jnp.concatenate([x * p.astype(BF16) for p in picks], 0)
-        values = dot(left, legendre[s]).astype(BF16)
-        sums[64 * s : 64 * (s + 1), :128] = values[:64]
-        sums[64 * s : 64 * (s + 1), 128:] = values[64:]
-    placed = dot(sums[...], place)
-    items = [
-        (placed[16 * u : 16 * (u + 1), :128], placed[16 * u : 16 * (u + 1), 128:])
-        for u in range(16)
-    ]
-    for b, (lo, hi) in enumerate(exchange_chunks(items, 1)):
-        out[b, 0, :, :128] = lo.astype(BF16)
-        out[b, 0, :, 128:] = hi.astype(BF16)
+    whole_spectral.wait()
+    for g in range(GROUPS):
+        copies[g].wait()
+        values = []
+        for s in range(4 * g, 4 * g + 4):
+            first, odd = slot_columns(slot_pair[band[0] * 20 + s], width, truncation)
+            one = first.astype(F32)
+            sign = 1.0 - 2.0 * odd.astype(F32)
+            x = spectral_in[:, s].reshape(32, width)
+            picks = [one, 1.0 - one, one * sign, (1.0 - one) * sign]
+            left = jnp.concatenate([x * p.astype(BF16) for p in picks], 0)
+            values.append(dot(left, legendre_in[s]).astype(BF16))
+        for s in range(4):
+            sums[g, 64 * s : 64 * (s + 1), :128] = values[s][:64]
+            sums[g, 64 * s : 64 * (s + 1), 128:] = values[s][64:]
+    for g in range(GROUPS):
+        placed = dot(sums[g], place)
+        spread[g, 0] = placed[:, :128]
+        spread[g, 1] = placed[:, 128:]
+        items = []
+        for u in range(16):
+            at = pl.ds(32 * (u >> 1) + (u & 1), 16, stride=2)
+            items.append((spread[g, 0, at, :], spread[g, 1, at, :]))
+        for b, (lo, hi) in enumerate(exchange_chunks(items, 1)):
+            messages[b, g, :, :128] = lo.astype(BF16)
+            messages[b, g, :, 128:] = hi.astype(BF16)
+        cut = pl.ds(g, 1)
+        copies[g] = pltpu.make_async_copy(messages.at[:, cut], out.at[:, cut], sent.at[g])
+        copies[g].start()
+    for copy in copies:
+        copy.wait()
 
 
 def rows_kernel(
     rows_per_step, band, row_latitude, points, cutoffs, received, waves, table, outer_cos,
-    outer_sin, factor, grid_field, out, fourier, twisted, samples
+    outer_sin, factor, grid_field, out, fourier, twisted, samples, tables, ready
 ):
     step = pl.program_id(0)
 
+    def fetch(row):
+        return pltpu.make_async_copy(table.at[row], tables.at[row], ready.at[row])
+
     @pl.when(step == 0)
     def _():
+        for row in range(NB):
+            fetch(row).start()
         for g in range(GROUPS):
             items = []
             for src in range(NB):
@@ -165,48 +192,68 @@
                 fourier[row, :, 256 * g : 256 * g + 128] = lo
                 fourier[row, :, 256 * g + 128 : 256 * g + 256] = hi
 
-    wave = waves[...]
-    imag = (lax.broadcasted_iota(jnp.int32, (1, WAVES), 1) & 1) == 1
-    sign = jnp.where(imag, F32(-1.0), F32(1.0))
     lane = lax.broadcasted_iota(jnp.int32, (1, 256), 1)
-    for r in range(rows_per_step):
-        row = step * rows_per_step + r
-        lat = row_latitude[band[0] * NB + row] & (points.shape[0] - 1)
-        count = points[lat]
-        kept = (wave <= cutoffs[lat].astype(F32)).astype(F32)
-        weight = kept * jnp.where(wave == 0.0, F32(1.0), F32(2.0))
-        x = fourier[row]
-        crossed = swap_parts(x) * -weight
-        x = x * (weight * sign)
-        for b in range(11):
-            value = x * outer_cos[r, b : b + 1, :] + crossed * outer_sin[r, b : b + 1, :]
-            twisted[r, 16 * b : 16 * (b + 1), :] = value.astype(BF16)
-        field = dot(twisted[r], table[r], NT)
-        for b in range(11):
-            value = jnp.where(lane + 256 * b < count, field[16 * b : 16 * (b + 1), :], 0.0)
-            value = value.astype(BF16)
-            if b < 10:
-                grid_field[r, :, 256 * b : 256 * (b + 1)] = value
-                scaled = value.astype(F32) * factor[r, :, 256 * b : 256 * (b + 1)]
-                samples[r, 16 * b : 16 * (b + 1), :] = scaled.astype(BF16)
-            else:
-                value = value[:, :128]
-                grid_field[r, :, 2560:2688] = value
-                scaled = value.astype(F32) * factor[r, :, 2560:2688]
-                samples[r, 160:176, :128] = scaled.astype(BF16)
-                samples[r, 160:176, 128:] = jnp.zeros((16, 128), BF16)
-        scale = kept / jnp.full((1, WAVES), count.astype(F32))
+    sign = jnp.where((lane & 1) == 1, F32(-1.0), F32(1.0))
+
+    def limits(r):
+        lat = row_latitude[band[0] * NB + step * rows_per_step + r] & (points.shape[0] - 1)
+        return points[lat], cutoffs[lat].astype(F32)
+
+    def twist(r):
+        cutoff = limits(r)[1]
         for t in range(5):
             lanes = slice(256 * t, 256 * (t + 1))
-            part = dot(samples[r], table[r, :, lanes])
+            wave = waves[:, lanes]
+            kept = (wave <= cutoff).astype(F32)
+            weight = kept * jnp.where(wave == 0.0, F32(1.0), F32(2.0))
+            x = fourier[step * rows_per_step + r, :, lanes]
+            crossed = swap_parts(x) * -weight
+            x = x * (weight * sign)
+            for b in range(11):
+                cosine, sine = outer_cos[r, b : b + 1, lanes], outer_sin[r, b : b + 1, lanes]
+                value = x * cosine + crossed * sine
+                twisted[r, 16 * b : 16 * (b + 1), lanes] = value.astype(BF16)
+
+    def inverse(r):
+        count = limits(r)[0]
+        row = step * rows_per_step + r
+        fetch(row).wait()
+        field = dot(twisted[r], tables[row], NT)
+        for b in range(11):
+            size = 256 if b < 10 else 128
+            cut = slice(256 * b, 256 * b + size)
+            value = jnp.where(lane + 256 * b < count, field[16 * b : 16 * (b + 1), :], 0.0)
+            value = value.astype(BF16)[:, :size]
+            grid_field[r, :, cut] = value
+            scaled = value.astype(F32) * factor[r, :, cut]
+            samples[r, 16 * b : 16 * (b + 1), :size] = scaled.astype(BF16)
+        samples[r, 160:176, 128:] = jnp.zeros((16, 128), BF16)
+
+    def direct(r):
+        count, cutoff = limits(r)
+        row = step * rows_per_step + r
+        for t in range(5):
+            lanes = slice(256 * t, 256 * (t + 1))
+            kept = (waves[:, lanes] <= cutoff).astype(F32)
+            scale = kept / jnp.full((1, 256), count.astype(F32))
+            part = dot(samples[r], tables[row, :, lanes])
             total_cos = jnp.zeros((16, 256), F32)
             total_sin = jnp.zeros((16, 256), F32)
             for b in range(11):
                 block = part[16 * b : 16 * (b + 1), :]
                 total_cos = total_cos + block * outer_cos[r, b : b + 1, lanes]
                 total_sin = total_sin + block * outer_sin[r, b : b + 1, lanes]
-            value = sign[:, lanes] * total_cos - swap_parts(total_sin)
-            out[r, :, lanes] = (value * scale[:, lanes]).astype(BF16)
+            value = sign * total_cos - swap_parts(total_sin)
+            out[r, :, lanes] = (value * scale).astype(BF16)
+
+    twist(0)
+    for r in range(rows_per_step):
+        if r + 1 < rows_per_step:
+            twist(r + 1)
+        inverse(r)
+        if r > 0:
+            direct(r - 1)
+    direct(rows_per_step - 1)
 
 
 def mix_kernel(vertical, received, out, levels, rows):
@@ -223,35 +270,40 @@
     out[...] = rows[...].astype(BF16)
 
 
-def final_kernel(truncation, band, slot_pair, lane_latitude, weights, received, legendre, out, rows):
-    group = pl.program_id(0)
+def final_kernel(
+    truncation, band, slot_pair, lane_latitude, weights, received, legendre, out, rows, full_out, sent
+):
     width = legendre.shape[1]
-
-    @pl.when(group == 0)
-    def _():
-        rows[...] = received[...].astype(F32)
-
-    values = jnp.concatenate(
-        [rows[pl.ds(2 * group + h, 256, stride=10), :].astype(BF16) for h in (0, 1)], 1
-    )
+    rows[...] = received[...].astype(F32)
     target = lax.broadcasted_iota(jnp.int32, (256, 256), 0)
     lane = lax.broadcasted_iota(jnp.int32, (256, 256), 1)
-    swap = (lane >> 4 == (target & 15)) & ((lane & 15) == target >> 4)
-    turned = dot(swap.astype(F32).astype(BF16), values, NT).astype(BF16)
     source = lane_latitude[...]
+    wave = ((target >> 5) << 1) | (target & 1)
+    turn = ((lane >> 4 == ((target >> 1) & 15)) & ((lane & 15) == wave)).astype(F32).astype(BF16)
     value = jnp.where((target >= 128) & (source >= 128), F32(-1.0), F32(1.0))
     fold = jnp.where((target & 127) == (source & 127), value, 0.0).astype(BF16)
-    parts = (dot(turned, fold, NT) * weights[...]).astype(BF16)
-    for s in range(4):
-        first, odd = slot_columns(slot_pair[band[0] * 20 + group * 4 + s], width, truncation)
-        own = parts[64 * s : 64 * (s + 1)]
-        left = jnp.concatenate([own[:, :128], own[:, 128:]], 0)
-        full = dot(left, legendre[s], NT)
-        even_part = jnp.where(first, full[0:32], full[32:64])
-        odd_part = jnp.where(first, full[64:96], full[96:128])
-        chosen = jnp.where(odd == 0, even_part, odd_part)
-        out[s, 0] = chosen[:16]
-        out[s, 1] = chosen[16:]
+    parts = []
+    for g in range(GROUPS):
+        halves = [rows[pl.ds(2 * g + h, 256, stride=10), :].astype(BF16) for h in (0, 1)]
+        turned = dot(turn, jnp.concatenate(halves, 1), NT).astype(BF16)
+        parts.append((dot(turned, fold, NT) * weights[...]).astype(BF16))
+    copies = []
+    for g in range(GROUPS):
+        for s in range(4):
+            slot = 4 * g + s
+            own = parts[g][64 * s : 64 * (s + 1)]
+            left = jnp.concatenate([own[:, :128], own[:, 128:]], 0)
+            full = dot(left, legendre[slot], NT)
+            first, odd = slot_columns(slot_pair[band[0] * 20 + slot], width, truncation)
+            even_part = jnp.where(first, full[0:32], full[32:64])
+            odd_part = jnp.where(first, full[64:96], full[96:128])
+            chosen = jnp.where(odd == 0, even_part, odd_part)
+            full_out[:, slot] = chosen.reshape(16, 2, width)
+        cut = pl.ds(4 * g, 4)
+        copies.append(pltpu.make_async_copy(full_out.at[:, cut], out.at[:, cut], sent.at[g]))
+        copies[g].start()
+    for copy in copies:
+        copy.wait()
 
 
 def whole(shape):
@@ -260,10 +312,15 @@
 
 SMEM = pl.BlockSpec(memory_space=pltpu.SMEM)
 VMEM = pl.BlockSpec(memory_space=pltpu.VMEM)
+HBM = pl.BlockSpec(memory_space=pltpu.HBM)
 
 
 def cost(flops, size):
     return pl.CostEstimate(flops=flops, bytes_accessed=size, transcendentals=0)
+
+
+def in_hbm(array):
+    return pltpu.with_memory_space_constraint(array, pltpu.HBM)
 
 
 def everywhere(message):
@@ -279,7 +336,7 @@
     truncation = 2 * slot_pair.shape[0] - 1
     width = spectral.shape[3]
     row_width = grid_factor.shape[1]
-    by_slot = spectral.transpose(2, 1, 0, 3)
+    by_slot = spectral.transpose(0, 2, 1, 3)
     legendre = legendre.transpose(0, 2, 1)
     lane_latitude = row_latitude.reshape(NB, NB).T.reshape(1, 256)
     pairs = slot_pair.reshape(NB, GROUPS, 4).transpose(1, 0, 2)
@@ -288,19 +345,22 @@
 
     message = pl.pallas_call(
         lambda *refs: send_kernel(truncation, *refs),
-        grid=(GROUPS,),
-        in_specs=[
-            SMEM, SMEM, whole((1, 256)),
-            pl.BlockSpec((4, 2, 16, width), lambda i: (i, 0, 0, 0)),
-            pl.BlockSpec((4, width, 128), lambda i: (i, 0, 0)),
-        ],
-        out_specs=pl.BlockSpec((NB, 1, 16, 256), lambda i: (0, i, 0, 0)),
-        out_shape=jax.ShapeDtypeStruct((NB, GROUPS, 16, 256), BF16),
-        scratch_shapes=[pltpu.VMEM((256, 256), BF16)],
+        in_specs=[SMEM, SMEM, VMEM, HBM, HBM],
+        out_specs=HBM,
+        out_shape=pltpu.HBM((NB, GROUPS, 16, 256), BF16),
+        scratch_shapes=[
+            pltpu.VMEM((GROUPS, 256, 256), BF16),
+            pltpu.VMEM((GROUPS, 2, 256, 128), F32),
+            pltpu.VMEM(by_slot.shape, BF16),
+            pltpu.VMEM(legendre.shape, BF16),
+            pltpu.VMEM((NB, GROUPS, 16, 256), BF16),
+            pltpu.SemaphoreType.DMA((GROUPS + 1,)),
+            pltpu.SemaphoreType.DMA((GROUPS,)),
+        ],
         compiler_params=params(),
         cost_estimate=cost(2 * 20 * 128 * 768 * 128, 5_000_000),
         name="legendre_send",
-    )(band, slot_pair, lane_latitude, by_slot, legendre)
+    )(band, slot_pair, lane_latitude, in_hbm(by_slot), in_hbm(legendre))
     received = lax.all_to_all(message, "band", split_axis=0, concat_axis=0, tiled=True)
 
     per_step = 2
@@ -314,7 +374,7 @@
             pl.BlockSpec((per_step, 16, WAVES), lambda i: (i, 0, 0)),
         ],
         out_shape=[
-            jax.ShapeDtypeStruct((NB, 256, WAVES), BF16),
+            pltpu.HBM((NB, 256, WAVES), BF16),
             jax.ShapeDtypeStruct((NB, 16, WAVES), F32),
             jax.ShapeDtypeStruct((NB, 16, WAVES), F32),
         ],
@@ -324,6 +384,7 @@
         name="phase_tables",
     )(band, row_latitude, points, waves)
 
+    per_step = 4
     factor = grid_factor.astype(F32).reshape(NB, 1, row_width)
     grid_field, harmonic = pl.pallas_call(
         lambda *refs: rows_kernel(per_step, *refs),
@@ -332,7 +393,7 @@
             SMEM, SMEM, SMEM, SMEM,
             whole((NB, GROUPS, 16, 256)),
             whole((1, WAVES)),
-            pl.BlockSpec((per_step, 256, WAVES), lambda i: (i, 0, 0)),
+            HBM,
             pl.BlockSpec((per_step, 16, WAVES), lambda i: (i, 0, 0)),
             pl.BlockSpec((per_step, 16, WAVES), lambda i: (i, 0, 0)),
             pl.BlockSpec((per_step, 1, row_width), lambda i: (i, 0, 0)),
@@ -349,11 +410,14 @@
             pltpu.VMEM((NB, 16, WAVES), F32),
             pltpu.VMEM((per_step, 176, WAVES), BF16),
             pltpu.VMEM((per_step, 176, 256), BF16),
-        ],
-        compiler_params=params(),
+            pltpu.VMEM((NB, 256, WAVES), BF16),
+            pltpu.SemaphoreType.DMA((NB,)),
+        ],
+        compiler_params=params(32),
         cost_estimate=cost(4 * 16 * 176 * 1280 * 256, 17_000_000),
         name="grid_rows",
-    )(band, row_latitude, points, cutoffs, received, waves, table, outer_cos, outer_sin, factor)
+    )(band, row_latitude, points, cutoffs, received, waves, in_hbm(table), outer_cos, outer_sin,
+      factor)
 
     levels_in = lax.all_to_all(harmonic, "lev", split_axis=0, concat_axis=0, tiled=True)
     outgoing = pl.pallas_call(
@@ -370,22 +434,22 @@
 
     round_trip = pl.pallas_call(
         lambda *refs: final_kernel(truncation, *refs),
-        grid=(GROUPS,),
-        in_specs=[
-            SMEM, SMEM, whole((1, 256)), whole((1, 256)), whole((ROWS, 128)),
-            pl.BlockSpec((4, width, 128), lambda i: (i, 0, 0)),
-        ],
-        out_specs=pl.BlockSpec((4, 2, 16, width), lambda i: (i, 0, 0, 0)),
-        out_shape=jax.ShapeDtypeStruct((20, 2, 16, width), F32),
-        scratch_shapes=[pltpu.VMEM((ROWS, 128), F32)],
+        in_specs=[SMEM, SMEM, VMEM, VMEM, VMEM, VMEM],
+        out_specs=HBM,
+        out_shape=jax.ShapeDtypeStruct((16, 20, 2, width), F32),
+        scratch_shapes=[
+            pltpu.VMEM((ROWS, 128), F32),
+            pltpu.VMEM((16, 20, 2, width), F32),
+            pltpu.SemaphoreType.DMA((GROUPS,)),
+        ],
         compiler_params=params(),
         cost_estimate=cost(2 * 20 * 128 * 768 * 128, 6_000_000),
         name="legendre_return",
     )(
-        band, slot_pair, row_latitude.reshape(1, 256), jnp.concatenate([weights, weights]).reshape(1, 256),
-        returned, legendre,
+        band, slot_pair, row_latitude.reshape(1, 256),
+        jnp.concatenate([weights, weights]).reshape(1, 256), returned, legendre,
     )
-    return (grid_field, round_trip.transpose(2, 1, 0, 3))
+    return (grid_field, round_trip.transpose(0, 2, 1, 3))
 
 
 def solution(mesh):

time: 118 us -> 109 us (0.924)
  local copies, waits for them, and re-layouts: 16.5 us -> 3.81 us
  waiting for transfers between devices: 28 us -> 30.7 us
    unnamed x26 -> x20, local copies, waits for them, and re-layouts: 14.9 us -> 1.57 us
    all_to_all x1, waiting for transfers between devices: 6.21 us -> 8.89 us  [per_device(): lax.all_to_all(message, 'band', split_axis=0, concat_axis=0, tiled=True)]
    pallas_call x1, Pallas kernels: 8.43 us -> 9.73 us  [per_device(): pl.pallas_call(lambda *refs: table_kernel(per_step, *refs), grid=(NB // p...]
  transfers between devices with their start and end apart: 2 -> 2, of which waited for: 2 -> 2; matrix products, arithmetic and copies ran while one was open for 1% -> 1% of each run, Pallas kernels for 7% -> 9%
where the time goes in v4:
time: 109 us
  Pallas kernels  37.2 us (34%)
  waiting for transfers between devices  30.7 us (28%)
  blocking collectives  19.2 us (18%)
  starting transfers between devices  17.1 us (16%)
  local copies, waits for them, and re-layouts  3.81 us (3%)
    all_to_all x1, waiting for transfers between devices, everywhere(): lax.all_to_all(pieces, ('band', 'lev'), split_axis=0, concat_axis=0, tile...  21.8 us
    all_to_all x1, blocking collectives, per_device(): lax.all_to_all(harmonic, 'lev', split_axis=0, concat_axis=0, tiled=True)  19.2 us
    pallas_call x1, Pallas kernels, per_device(): pl.pallas_call(lambda *refs: rows_kernel(per_step, *refs), grid=(NB // pe...  15.1 us
    all_to_all x1, starting transfers between devices, per_device(): lax.all_to_all(message, 'band', split_axis=0, concat_axis=0, tiled=True)  10.1 us
    pallas_call x1, Pallas kernels, per_device(): pl.pallas_call(lambda *refs: table_kernel(per_step, *refs), grid=(NB // p...  9.73 us
    all_to_all x1, waiting for transfers between devices, per_device(): lax.all_to_all(message, 'band', split_axis=0, concat_axis=0, tiled=True)  8.89 us
    all_to_all x1, starting transfers between devices, everywhere(): lax.all_to_all(pieces, ('band', 'lev'), split_axis=0, concat_axis=0, tile...  6.94 us
    pallas_call x1, Pallas kernels, per_device(): pl.pallas_call(lambda *refs: send_kernel(truncation, *refs), in_specs=[SM...  5.99 us
  transfers between devices with their start and end apart: 2, of which 2 were waited for; matrix products, arithmetic and copies ran while one was open for 1% of the time, Pallas kernels for 9%

profile of v4, /device:TPU:1, one launch (start us, length us, event | category | flops | bytes accessed | tf_op | source)
XLA Modules:
  0.0 108.8 jit_solution(2806759866037010575)
XLA Ops:
  0.6 0.8 reshape.49
  1.4 0.1 copy.21
  1.5 0.1 reshape.50.refs_2_
  1.5 0.0 copy-start.3
  1.5 0.7 copy-done.3
  2.2 0.0 copy-start.4
  2.2 6.0 %legendre_send.1 = bf16[16,5,16,256]{3,2,1,0:T(8,128)(2,1)} custom-call(s32[1]{0:T(128)} %bitcast.refs_0_, s32[320]{0:T(512)S(1)} %copy-done.3, s32[1,256]{1,0:T(1,128)S(1)} %reshape.50.refs_2_, bf16[16,20,2,641]{3,2,1,0:T(2,128)(2,1)} %bitcast.27, bf16[20,641,128]{2,1,0:T(8,128)(2,1)} %bitcast.21), custom_call_target="tpu_custom_call" | custom-call | flops 503316480 | bytes 5000000 | tf_op jit(solution)/shard_map/legendre_send/pallas_call | solution.py:346
  8.2 0.0 copy-start.8
  8.2 0.0 copy-start.5
  8.3 0.0 copy-start.6
  8.3 0.0 copy-start.7
  8.3 10.1 %all-to-all-start = ((bf16[16,5,16,256]{3,2,1,0:T(8,128)(2,1)}), bf16[16,5,16,256]{3,2,1,0:T(8,128)(2,1)S(1)}, u32[]{:S(2)}, u32[]{:S(2)}) async-start(bf16[16,5,16,256]{3,2,1,0:T(8,128)(2,1)} %legendre_send.1), calls=%async_computation | async-start | bytes 1310720 | tf_op jit(solution)/shard_map/all_to_all | solution.py:364
  18.4 0.0 copy-done.4
  18.4 0.1 reshape.51
  18.5 0.1 copy.22
  18.7 0.2 copy.25
  18.9 0.4 broadcast_in_dim.2
  19.3 0.4 convert_element_type.7.refs_3_.refs_5_
  19.7 0.0 copy-done.8
  19.7 0.1 reshape.59.refs_9_
  19.8 0.0 copy-done.5
  19.8 0.0 copy-done.6
  19.8 9.7 %phase_tables.1 = (bf16[16,256,1280]{2,1,0:T(8,128)(2,1)}, f32[16,16,1280]{2,1,0:T(8,128)S(1)}, f32[16,16,1280]{2,1,0:T(8,128)S(1)}) custom-call(s32[1]{0:T(128)} %bitcast.refs_0_, s32[256]{0:T(256)S(1)} %copy-done.5, s32[128]{0:T(128)S(1)} %copy-done.6, f32[1,1280]{1,0:T(1,128)S(1)} %convert_element_type.7.refs_3_.refs_5_), custom_call_target="tpu_custom_call" | custom-call | flops 104857600 | bytes 14000000 | tf_op jit(solution)/shard_map/phase_tables/pallas_call | solution.py:367
  29.5 8.9 %all-to-all-done.refs_4_ = bf16[16,5,16,256]{3,2,1,0:T(8,128)(2,1)S(1)} async-done(((bf16[16,5,16,256]{3,2,1,0:T(8,128)(2,1)}), bf16[16,5,16,256]{3,2,1,0:T(8,128)(2,1)S(1)}, u32[]{:S(2)}, u32[]{:S(2)}) %all-to-all-start) | async-done | bytes 655392 | tf_op jit(solution)/shard_map/all_to_all | solution.py:364
  38.4 0.0 copy-done.7
  38.4 0.0 copy-start.2
  38.4 15.1 %grid_rows.1 = (bf16[16,16,2688]{2,1,0:T(8,128)(2,1)}, bf16[16,16,1280]{2,1,0:T(8,128)(2,1)S(1)}) custom-call(s32[1]{0:T(128)} %bitcast.refs_0_, s32[256]{0:T(256)S(1)} %copy-done.5, s32[128]{0:T(128)S(1)} %copy-done.6, s32[128]{0:T(128)S(1)} %copy-done.7, bf16[16,5,16,256]{3,2,1,0:T(8,128)(2,1)S(1)} %all-to-all-done.refs_4_, ...), custom_call_target="tpu_custom_call" | custom-call | flops 3690987520 | bytes 17000000 | tf_op jit(solution)/shard_map/grid_rows/pallas_call | solution.py:389
  53.5 0.0 copy-start.9
  53.5 0.0 copy-start
  53.5 19.2 %all_to_all.15.received = bf16[16,16,1280]{2,1,0:T(8,128)(2,1)S(1)} all-to-all(bf16[16,16,1280]{2,1,0:T(8,128)(2,1)S(1)} %get-tuple-element.11), channel_id=1, replica_groups=mesh['band'=16,'lev'=16] {'lev'}, dimensions={0} | all-to-all | bytes 1310720 | tf_op jit(solution)/shard_map/all_to_all | solution.py:422
  72.7 0.0 copy-done.2
  72.7 2.7 %vertical_mix.1 = bf16[2560,128]{1,0:T(8,128)(2,1)S(1)} custom-call(bf16[256,256]{1,0:T(8,128)(2,1)S(1)} %copy-done.2, bf16[16,16,1280]{2,1,0:T(8,128)(2,1)S(1)} %all_to_all.15.received), custom_call_target="tpu_custom_call" | custom-call | flops 167772160 | bytes 1400000 | tf_op jit(solution)/shard_map/vertical_mix/pallas_call | solution.py:423
  75.4 0.0 copy-start.1
  75.4 0.8 copy-done.1
  76.2 6.9 %all-to-all-start.2 = ((bf16[1280,2,128]{2,1,0:T(2,128)(2,1)}), bf16[1280,2,128]{2,1,0:T(2,128)(2,1)}, u32[]{:S(2)}, u32[]{:S(2)}) async-start(bf16[1280,2,128]{2,1,0:T(2,128)(2,1)} %bitcast.23), calls=%async_computation.2 | async-start | bytes 1310720 | tf_op jit(solution)/shard_map/all_to_all | solution.py:328
  83.2 0.0 copy-done.9
  83.2 21.8 %all-to-all-done.2 = bf16[1280,2,128]{2,1,0:T(2,128)(2,1)} async-done(((bf16[1280,2,128]{2,1,0:T(2,128)(2,1)}), bf16[1280,2,128]{2,1,0:T(2,128)(2,1)}, u32[]{:S(2)}, u32[]{:S(2)}) %all-to-all-start.2) | async-done | bytes 655392 | tf_op jit(solution)/shard_map/all_to_all | solution.py:328
  105.0 0.0 copy-done
  105.0 3.7 %legendre_return.1 = f32[16,20,2,641]{3,2,1,0:T(2,128)} custom-call(s32[1]{0:T(128)} %bitcast.refs_0_, s32[320]{0:T(512)S(1)} %copy-done.4, s32[1,256]{1,0:T(1,128)S(1)} %bitcast.24, f32[1,256]{1,0:T(1,128)S(1)} %bitcast.25, bf16[2560,128]{1,0:T(8,128)(2,1)} %bitcast.12.refs_4_, bf16[20,641,128]{2,1,0:T(8,128)(2,1)S(1)} %bitcast.22), custom_call_target="tpu_custom_call" | custom-call | flops 503316480 | bytes 6000000 | tf_op jit(solution)/shard_map/legendre_return/pallas_call | solution.py:435
  (3 shorter events, 0.0 us)
Async XLA Ops:
  1.5 0.7 copy-start.3
  2.2 16.2 %copy-start.4 = (s32[320]{0:T(512)S(1)}, s32[320]{0:T(512)}, u32[]{:S(2)}) copy-start(s32[320]{0:T(512)} %refs_1_.7) | copy-start | bytes 3844
  8.2 11.5 %copy-start.8 = (bf16[16,2688]{1,0:T(8,128)(2,1)S(1)}, bf16[16,2688]{1,0:T(8,128)(2,1)}, u32[]{:S(2)}) copy-start(bf16[16,2688]{1,0:T(8,128)(2,1)} %param.13) | copy-start | bytes 258052
  8.2 11.6 %copy-start.5 = (s32[256]{0:T(256)S(1)}, s32[256]{0:T(256)}, u32[]{:S(2)}) copy-start(s32[256]{0:T(256)} %refs_1_.6) | copy-start | bytes 3076
  8.3 11.6 %copy-start.6 = (s32[128]{0:T(128)S(1)}, s32[128]{0:T(128)}, u32[]{:S(2)}) copy-start(s32[128]{0:T(128)} %refs_2_.3) | copy-start | bytes 1540
  8.3 30.2 %copy-start.7 = (s32[128]{0:T(128)S(1)}, s32[128]{0:T(128)}, u32[]{:S(2)}) copy-start(s32[128]{0:T(128)} %refs_3_.1) | copy-start | bytes 1540
  8.3 30.1 %all-to-all-start = ((bf16[16,5,16,256]{3,2,1,0:T(8,128)(2,1)}), bf16[16,5,16,256]{3,2,1,0:T(8,128)(2,1)S(1)}, u32[]{:S(2)}, u32[]{:S(2)}) async-start(bf16[16,5,16,256]{3,2,1,0:T(8,128)(2,1)} %legendre_send.1), calls=%async_computation | async-start | bytes 1310720 | tf_op jit(solution)/shard_map/all_to_all | solution.py:364
  38.4 34.3 %copy-start.2 = (bf16[256,256]{1,0:T(8,128)(2,1)S(1)}, bf16[256,256]{1,0:T(8,128)(2,1)}, u32[]{:S(2)}) copy-start(bf16[256,256]{1,0:T(8,128)(2,1)} %vertical.1) | copy-start | bytes 393220
  53.5 29.7 %copy-start.9 = (f32[128]{0:T(128)S(1)}, f32[128]{0:T(128)}, u32[]{:S(2)}) copy-start(f32[128]{0:T(128)} %param.11) | copy-start | bytes 1540
  53.5 51.5 %copy-start = (bf16[20,128,641]{1,2,0:T(8,128)(2,1)S(1)}, bf16[20,128,641]{1,2,0:T(8,128)(2,1)}, u32[]{:S(2)}) copy-start(bf16[20,128,641]{1,2,0:T(8,128)(2,1)} %param.10) | copy-start | bytes 9845764
  75.4 0.8 copy-start.1
  76.2 28.8 %all-to-all-start.2 = ((bf16[1280,2,128]{2,1,0:T(2,128)(2,1)}), bf16[1280,2,128]{2,1,0:T(2,128)(2,1)}, u32[]{:S(2)}, u32[]{:S(2)}) async-start(bf16[1280,2,128]{2,1,0:T(2,128)(2,1)} %bitcast.23), calls=%async_computation.2 | async-start | bytes 1310720 | tf_op jit(solution)/shard_map/all_to_all | solution.py:328

commit v5 on v4

--- a/solution.py
+++ b/solution.py
@@ -123,10 +123,12 @@
 
 
 def send_kernel(
-    truncation, band, slot_pair, lane_latitude, spectral, legendre, out, sums, spread, spectral_in,
-    legendre_in, messages, ready, sent
+    truncation, band, all_pairs, lane_latitude, spectral, legendre, out, sums, spread, spectral_in,
+    legendre_in, messages, slot_pair, ready, sent
 ):
     width = spectral.shape[-1]
+    slots = pltpu.make_async_copy(all_pairs, slot_pair, ready.at[GROUPS + 1])
+    slots.start()
     whole_spectral = pltpu.make_async_copy(spectral, spectral_in, ready.at[GROUPS])
     whole_spectral.start()
     copies = []
@@ -134,9 +136,12 @@
         cut = pl.ds(4 * g, 4)
         copies.append(pltpu.make_async_copy(legendre.at[cut], legendre_in.at[cut], ready.at[g]))
         copies[g].start()
-    place = (
-        lax.broadcasted_iota(jnp.int32, (256, 256), 0) == lane_latitude[...]
-    ).astype(F32).astype(BF16)
+    index = lax.broadcasted_iota(jnp.int32, (256, 256), 0)
+    lane = lax.broadcasted_iota(jnp.int32, (256, 256), 1)
+    place = (index == lane_latitude[...]).astype(F32).astype(BF16)
+    by_row = (index == ((lane & 15) << 4 | lane >> 4)).astype(F32).astype(BF16)
+    place = dot(place, by_row).astype(BF16)
+    slots.wait()
     whole_spectral.wait()
     for g in range(GROUPS):
         copies[g].wait()
@@ -181,7 +186,7 @@
 
     @pl.when(step == 0)
     def _():
-        for row in range(NB):
+        for row in range(rows_per_step):
             fetch(row).start()
         for g in range(GROUPS):
             items = []
@@ -191,6 +196,11 @@
             for row, (lo, hi) in enumerate(exchange_chunks(items, 16)):
                 fourier[row, :, 256 * g : 256 * g + 128] = lo
                 fourier[row, :, 256 * g + 128 : 256 * g + 256] = hi
+
+    @pl.when(step + 1 < pl.num_programs(0))
+    def _():
+        for r in range(rows_per_step):
+            fetch((step + 1) * rows_per_step + r).start()
 
     lane = lax.broadcasted_iota(jnp.int32, (1, 256), 1)
     sign = jnp.where((lane & 1) == 1, F32(-1.0), F32(1.0))
@@ -282,11 +292,12 @@
     turn = ((lane >> 4 == ((target >> 1) & 15)) & ((lane & 15) == wave)).astype(F32).astype(BF16)
     value = jnp.where((target >= 128) & (source >= 128), F32(-1.0), F32(1.0))
     fold = jnp.where((target & 127) == (source & 127), value, 0.0).astype(BF16)
+    doubled = jnp.concatenate([weights[...], weights[...]], 1)
     parts = []
     for g in range(GROUPS):
         halves = [rows[pl.ds(2 * g + h, 256, stride=10), :].astype(BF16) for h in (0, 1)]
         turned = dot(turn, jnp.concatenate(halves, 1), NT).astype(BF16)
-        parts.append((dot(turned, fold, NT) * weights[...]).astype(BF16))
+        parts.append((dot(turned, fold, NT) * doubled).astype(BF16))
     copies = []
     for g in range(GROUPS):
         for s in range(4):
@@ -338,14 +349,14 @@
     row_width = grid_factor.shape[1]
     by_slot = spectral.transpose(0, 2, 1, 3)
     legendre = legendre.transpose(0, 2, 1)
-    lane_latitude = row_latitude.reshape(NB, NB).T.reshape(1, 256)
+    lane_latitude = row_latitude.reshape(1, 256)
     pairs = slot_pair.reshape(NB, GROUPS, 4).transpose(1, 0, 2)
     waves = jnp.stack([pairs, truncation - pairs], -1)
     waves = jnp.broadcast_to(waves[..., None], waves.shape + (2,)).reshape(1, WAVES).astype(F32)
 
     message = pl.pallas_call(
         lambda *refs: send_kernel(truncation, *refs),
-        in_specs=[SMEM, SMEM, VMEM, HBM, HBM],
+        in_specs=[SMEM, HBM, VMEM, HBM, HBM],
         out_specs=HBM,
         out_shape=pltpu.HBM((NB, GROUPS, 16, 256), BF16),
         scratch_shapes=[
@@ -354,13 +365,14 @@
             pltpu.VMEM(by_slot.shape, BF16),
             pltpu.VMEM(legendre.shape, BF16),
             pltpu.VMEM((NB, GROUPS, 16, 256), BF16),
-            pltpu.SemaphoreType.DMA((GROUPS + 1,)),
+            pltpu.SMEM(slot_pair.shape, jnp.int32),
+            pltpu.SemaphoreType.DMA((GROUPS + 2,)),
             pltpu.SemaphoreType.DMA((GROUPS,)),
         ],
         compiler_params=params(),
         cost_estimate=cost(2 * 20 * 128 * 768 * 128, 5_000_000),
         name="legendre_send",
-    )(band, slot_pair, lane_latitude, in_hbm(by_slot), in_hbm(legendre))
+    )(band, in_hbm(slot_pair), lane_latitude, in_hbm(by_slot), in_hbm(legendre))
     received = lax.all_to_all(message, "band", split_axis=0, concat_axis=0, tiled=True)
 
     per_step = 2
@@ -446,8 +458,7 @@
         cost_estimate=cost(2 * 20 * 128 * 768 * 128, 6_000_000),
         name="legendre_return",
     )(
-        band, slot_pair, row_latitude.reshape(1, 256),
-        jnp.concatenate([weights, weights]).reshape(1, 256), returned, legendre,
+        band, slot_pair, lane_latitude, weights.reshape(1, 128), returned, legendre,
     )
     return (grid_field, round_trip.transpose(0, 2, 1, 3))
 

time: 109 us -> 106 us (0.972)
  blocking collectives: 19.2 us -> 47.7 us
  waiting for transfers between devices: 30.7 us -> 8.88 us
  starting transfers between devices: 17.1 us -> 10.1 us
  local copies, waits for them, and re-layouts: 3.81 us -> 2.05 us
  Pallas kernels: 37.2 us -> 36 us
    all_to_all x0 -> x1, blocking collectives: none -> 28.5 us  [everywhere(): lax.all_to_all(pieces, ('band', 'lev'), split_axis=0, concat_axis=0, tile...]
    all_to_all x1 -> x0, waiting for transfers between devices: 21.8 us -> none  [everywhere(): lax.all_to_all(pieces, ('band', 'lev'), split_axis=0, concat_axis=0, tile...]
    all_to_all x1 -> x0, starting transfers between devices: 6.94 us -> none  [everywhere(): lax.all_to_all(pieces, ('band', 'lev'), split_axis=0, concat_axis=0, tile...]
  transfers between devices with their start and end apart: 2 -> 1, of which waited for: 2 -> 1; matrix products, arithmetic and copies ran while one was open for 1% -> 1% of each run, Pallas kernels for 9% -> 9%
where the time goes in v5:
time: 106 us
  blocking collectives  47.7 us (45%)
  Pallas kernels  36 us (34%)
  starting transfers between devices  10.1 us (10%)
  waiting for transfers between devices  8.88 us (8%)
  local copies, waits for them, and re-layouts  2.05 us (2%)
    all_to_all x1, blocking collectives, everywhere(): lax.all_to_all(pieces, ('band', 'lev'), split_axis=0, concat_axis=0, tile...  28.5 us
    all_to_all x1, blocking collectives, per_device(): lax.all_to_all(harmonic, 'lev', split_axis=0, concat_axis=0, tiled=True)  19.2 us
    pallas_call x1, Pallas kernels, per_device(): pl.pallas_call(lambda *refs: rows_kernel(per_step, *refs), grid=(NB // pe...  15 us
    all_to_all x1, starting transfers between devices, per_device(): lax.all_to_all(message, 'band', split_axis=0, concat_axis=0, tiled=True)  10.1 us
    pallas_call x1, Pallas kernels, per_device(): pl.pallas_call(lambda *refs: table_kernel(per_step, *refs), grid=(NB // p...  9.73 us
    all_to_all x1, waiting for transfers between devices, per_device(): lax.all_to_all(message, 'band', split_axis=0, concat_axis=0, tiled=True)  8.88 us
    pallas_call x1, Pallas kernels, per_device(): pl.pallas_call(lambda *refs: send_kernel(truncation, *refs), in_specs=[SM...  5.41 us
    pallas_call x1, Pallas kernels, per_device(): pl.pallas_call(lambda *refs: final_kernel(truncation, *refs), in_specs=[S...  3.18 us
  transfers between devices with their start and end apart: 1, of which 1 were waited for; matrix products, arithmetic and copies ran while one was open for 1% of the time, Pallas kernels for 9%

profile of v5, /device:TPU:1, one launch (start us, length us, event | category | flops | bytes accessed | tf_op | source)
XLA Modules:
  0.0 105.7 jit_solution(14386894786009436538)
XLA Ops:
  0.6 0.0 copy-start.3
  0.6 0.7 copy-done.3
  1.3 0.0 copy-start.2
  1.3 5.4 %legendre_send.1 = bf16[16,5,16,256]{3,2,1,0:T(8,128)(2,1)} custom-call(s32[1]{0:T(128)} %bitcast.refs_0_, s32[320]{0:T(512)} %refs_1_.7, s32[1,256]{1,0:T(1,128)S(1)} %bitcast.24, bf16[16,20,2,641]{3,2,1,0:T(2,128)(2,1)} %bitcast.28, bf16[20,641,128]{2,1,0:T(8,128)(2,1)} %bitcast.20), custom_call_target="tpu_custom_call" | custom-call | flops 503316480 | bytes 5000000 | tf_op jit(solution)/shard_map/legendre_send/pallas_call | solution.py:357
  6.7 0.0 copy-start.8
  6.7 0.0 copy-start.4
  6.8 0.0 copy-start.6
  6.8 0.0 copy-start.7
  6.8 10.1 %all-to-all-start = ((bf16[16,5,16,256]{3,2,1,0:T(8,128)(2,1)}), bf16[16,5,16,256]{3,2,1,0:T(8,128)(2,1)S(1)}, u32[]{:S(2)}, u32[]{:S(2)}) async-start(bf16[16,5,16,256]{3,2,1,0:T(8,128)(2,1)} %legendre_send.1), calls=%async_computation | async-start | bytes 1310720 | tf_op jit(solution)/shard_map/all_to_all | solution.py:376
  16.9 0.0 copy-done.2
  16.9 0.1 reshape.44
  17.0 0.1 copy.19
  17.1 0.2 copy.22
  17.4 0.4 broadcast_in_dim.2
  17.8 0.4 convert_element_type.7.refs_3_.refs_5_
  18.2 0.0 copy-done.8
  18.2 0.1 reshape.51.refs_9_
  18.3 0.0 copy-done.4
  18.3 0.0 copy-done.6
  18.3 9.7 %phase_tables.1 = (bf16[16,256,1280]{2,1,0:T(8,128)(2,1)}, f32[16,16,1280]{2,1,0:T(8,128)S(1)}, f32[16,16,1280]{2,1,0:T(8,128)S(1)}) custom-call(s32[1]{0:T(128)} %bitcast.refs_0_, s32[256]{0:T(256)S(1)} %copy-done.4, s32[128]{0:T(128)S(1)} %copy-done.6, f32[1,1280]{1,0:T(1,128)S(1)} %convert_element_type.7.refs_3_.refs_5_), custom_call_target="tpu_custom_call" | custom-call | flops 104857600 | bytes 14000000 | tf_op jit(solution)/shard_map/phase_tables/pallas_call | solution.py:379
  28.1 8.9 %all-to-all-done.refs_4_ = bf16[16,5,16,256]{3,2,1,0:T(8,128)(2,1)S(1)} async-done(((bf16[16,5,16,256]{3,2,1,0:T(8,128)(2,1)}), bf16[16,5,16,256]{3,2,1,0:T(8,128)(2,1)S(1)}, u32[]{:S(2)}, u32[]{:S(2)}) %all-to-all-start) | async-done | bytes 655392 | tf_op jit(solution)/shard_map/all_to_all | solution.py:376
  36.9 0.0 copy-done.7
  36.9 0.0 copy-start.1
  36.9 15.0 %grid_rows.1 = (bf16[16,16,2688]{2,1,0:T(8,128)(2,1)}, bf16[16,16,1280]{2,1,0:T(8,128)(2,1)S(1)}) custom-call(s32[1]{0:T(128)} %bitcast.refs_0_, s32[256]{0:T(256)S(1)} %copy-done.4, s32[128]{0:T(128)S(1)} %copy-done.6, s32[128]{0:T(128)S(1)} %copy-done.7, bf16[16,5,16,256]{3,2,1,0:T(8,128)(2,1)S(1)} %all-to-all-done.refs_4_, ...), custom_call_target="tpu_custom_call" | custom-call | flops 3690987520 | bytes 17000000 | tf_op jit(solution)/shard_map/grid_rows/pallas_call | solution.py:401
  52.0 0.0 copy-start
  52.0 0.0 copy-start.5
  52.0 19.2 %all_to_all.15.received = bf16[16,16,1280]{2,1,0:T(8,128)(2,1)S(1)} all-to-all(bf16[16,16,1280]{2,1,0:T(8,128)(2,1)S(1)} %get-tuple-element.11), channel_id=1, replica_groups=mesh['band'=16,'lev'=16] {'lev'}, dimensions={0} | all-to-all | bytes 1310720 | tf_op jit(solution)/shard_map/all_to_all | solution.py:434
  71.2 0.0 copy-done.1
  71.2 2.7 %vertical_mix.1 = bf16[2560,128]{1,0:T(8,128)(2,1)S(1)} custom-call(bf16[256,256]{1,0:T(8,128)(2,1)S(1)} %copy-done.1, bf16[16,16,1280]{2,1,0:T(8,128)(2,1)S(1)} %all_to_all.15.received), custom_call_target="tpu_custom_call" | custom-call | flops 167772160 | bytes 1400000 | tf_op jit(solution)/shard_map/vertical_mix/pallas_call | solution.py:435
  73.9 28.5 %all_to_all.16 = bf16[1280,2,128]{2,1,0:T(2,128)(2,1)S(1)} all-to-all(bf16[1280,2,128]{2,1,0:T(2,128)(2,1)S(1)} %bitcast.23), channel_id=1, replica_groups=mesh['band'=16,'lev'=16] {'band','lev'}, dimensions={0} | all-to-all | bytes 1310720 | tf_op jit(solution)/shard_map/all_to_all | solution.py:339
  102.4 0.0 copy-done
  102.4 0.0 copy-done.5
  102.4 3.2 %legendre_return.1 = f32[16,20,2,641]{3,2,1,0:T(2,128)} custom-call(s32[1]{0:T(128)} %bitcast.refs_0_, s32[320]{0:T(512)S(1)} %copy-done.2, s32[1,256]{1,0:T(1,128)S(1)} %bitcast.25, f32[1,128]{1,0:T(1,128)S(1)} %bitcast.26, bf16[2560,128]{1,0:T(8,128)(2,1)S(1)} %bitcast.22, bf16[20,641,128]{2,1,0:T(8,128)(2,1)S(1)} %bitcast.21), custom_call_target="tpu_custom_call" | custom-call | flops 503316480 | bytes 6000000 | tf_op jit(solution)/shard_map/legendre_return/pallas_call | solution.py:447
  (2 shorter events, 0.0 us)
Async XLA Ops:
  0.6 0.7 copy-start.3
  1.3 15.6 %copy-start.2 = (s32[320]{0:T(512)S(1)}, s32[320]{0:T(512)}, u32[]{:S(2)}) copy-start(s32[320]{0:T(512)} %refs_1_.7) | copy-start | bytes 3844
  6.7 11.5 %copy-start.8 = (bf16[16,2688]{1,0:T(8,128)(2,1)S(1)}, bf16[16,2688]{1,0:T(8,128)(2,1)}, u32[]{:S(2)}) copy-start(bf16[16,2688]{1,0:T(8,128)(2,1)} %param.13) | copy-start | bytes 258052
  6.7 11.6 %copy-start.4 = (s32[256]{0:T(256)S(1)}, s32[256]{0:T(256)}, u32[]{:S(2)}) copy-start(s32[256]{0:T(256)} %refs_1_.6) | copy-start | bytes 3076
  6.8 11.6 %copy-start.6 = (s32[128]{0:T(128)S(1)}, s32[128]{0:T(128)}, u32[]{:S(2)}) copy-start(s32[128]{0:T(128)} %refs_2_.3) | copy-start | bytes 1540
  6.8 30.2 %copy-start.7 = (s32[128]{0:T(128)S(1)}, s32[128]{0:T(128)}, u32[]{:S(2)}) copy-start(s32[128]{0:T(128)} %refs_3_.1) | copy-start | bytes 1540
  6.8 30.1 %all-to-all-start = ((bf16[16,5,16,256]{3,2,1,0:T(8,128)(2,1)}), bf16[16,5,16,256]{3,2,1,0:T(8,128)(2,1)S(1)}, u32[]{:S(2)}, u32[]{:S(2)}) async-start(bf16[16,5,16,256]{3,2,1,0:T(8,128)(2,1)} %legendre_send.1), calls=%async_computation | async-start | bytes 1310720 | tf_op jit(solution)/shard_map/all_to_all | solution.py:376
  36.9 34.2 %copy-start.1 = (bf16[256,256]{1,0:T(8,128)(2,1)S(1)}, bf16[256,256]{1,0:T(8,128)(2,1)}, u32[]{:S(2)}) copy-start(bf16[256,256]{1,0:T(8,128)(2,1)} %vertical.1) | copy-start | bytes 393220
  52.0 50.4 %copy-start = (bf16[20,128,641]{1,2,0:T(8,128)(2,1)S(1)}, bf16[20,128,641]{1,2,0:T(8,128)(2,1)}, u32[]{:S(2)}) copy-start(bf16[20,128,641]{1,2,0:T(8,128)(2,1)} %param.10) | copy-start | bytes 9845764
  52.0 50.4 %copy-start.5 = (f32[128]{0:T(128)S(1)}, f32[128]{0:T(128)}, u32[]{:S(2)}) copy-start(f32[128]{0:T(128)} %param.11) | copy-start | bytes 1540

commit v6 on v5

--- a/solution.py
+++ b/solution.py
@@ -123,12 +123,14 @@
 
 
 def send_kernel(
-    truncation, band, all_pairs, lane_latitude, spectral, legendre, out, sums, spread, spectral_in,
-    legendre_in, messages, slot_pair, ready, sent
+    truncation, band, all_pairs, latitudes, spectral, legendre, out, sums, spread, spectral_in,
+    legendre_in, messages, slot_pair, lane_latitude, ready, sent
 ):
     width = spectral.shape[-1]
     slots = pltpu.make_async_copy(all_pairs, slot_pair, ready.at[GROUPS + 1])
     slots.start()
+    rows = pltpu.make_async_copy(latitudes, lane_latitude, ready.at[GROUPS + 2])
+    rows.start()
     whole_spectral = pltpu.make_async_copy(spectral, spectral_in, ready.at[GROUPS])
     whole_spectral.start()
     copies = []
@@ -138,6 +140,7 @@
         copies[g].start()
     index = lax.broadcasted_iota(jnp.int32, (256, 256), 0)
     lane = lax.broadcasted_iota(jnp.int32, (256, 256), 1)
+    rows.wait()
     place = (index == lane_latitude[...]).astype(F32).astype(BF16)
     by_row = (index == ((lane & 15) << 4 | lane >> 4)).astype(F32).astype(BF16)
     place = dot(place, by_row).astype(BF16)
@@ -177,17 +180,12 @@
 
 def rows_kernel(
     rows_per_step, band, row_latitude, points, cutoffs, received, waves, table, outer_cos,
-    outer_sin, factor, grid_field, out, fourier, twisted, samples, tables, ready
+    outer_sin, factor, grid_field, out, fourier, twisted, samples
 ):
     step = pl.program_id(0)
 
-    def fetch(row):
-        return pltpu.make_async_copy(table.at[row], tables.at[row], ready.at[row])
-
     @pl.when(step == 0)
     def _():
-        for row in range(rows_per_step):
-            fetch(row).start()
         for g in range(GROUPS):
             items = []
             for src in range(NB):
@@ -196,11 +194,6 @@
             for row, (lo, hi) in enumerate(exchange_chunks(items, 16)):
                 fourier[row, :, 256 * g : 256 * g + 128] = lo
                 fourier[row, :, 256 * g + 128 : 256 * g + 256] = hi
-
-    @pl.when(step + 1 < pl.num_programs(0))
-    def _():
-        for r in range(rows_per_step):
-            fetch((step + 1) * rows_per_step + r).start()
 
     lane = lax.broadcasted_iota(jnp.int32, (1, 256), 1)
     sign = jnp.where((lane & 1) == 1, F32(-1.0), F32(1.0))
@@ -226,9 +219,7 @@
 
     def inverse(r):
         count = limits(r)[0]
-        row = step * rows_per_step + r
-        fetch(row).wait()
-        field = dot(twisted[r], tables[row], NT)
+        field = dot(twisted[r], table[r], NT)
         for b in range(11):
             size = 256 if b < 10 else 128
             cut = slice(256 * b, 256 * b + size)
@@ -241,12 +232,11 @@
 
     def direct(r):
         count, cutoff = limits(r)
-        row = step * rows_per_step + r
         for t in range(5):
             lanes = slice(256 * t, 256 * (t + 1))
             kept = (waves[:, lanes] <= cutoff).astype(F32)
             scale = kept / jnp.full((1, 256), count.astype(F32))
-            part = dot(samples[r], tables[row, :, lanes])
+            part = dot(samples[r], table[r, :, lanes])
             total_cos = jnp.zeros((16, 256), F32)
             total_sin = jnp.zeros((16, 256), F32)
             for b in range(11):
@@ -266,14 +256,20 @@
     direct(rows_per_step - 1)
 
 
-def mix_kernel(vertical, received, out, levels, rows):
+def mix_kernel(vertical, received, out, rows):
+    index = lax.broadcasted_iota(jnp.int32, (256, 256), 0)
+    lane = lax.broadcasted_iota(jnp.int32, (256, 256), 1)
+    by_level = (((lane & 15) == index >> 4) & (lane >> 4 == (index & 15))).astype(F32).astype(BF16)
+    matrix = dot(by_level, vertical[...]).astype(BF16)
     block = received[...].reshape(256, WAVES)
-    for t in range(10):
-        levels[256 * t : 256 * (t + 1), :] = dot(vertical[...], block[:, 128 * t : 128 * (t + 1)])
+    values = []
+    for t in range(5):
+        value = dot(matrix, block[:, 256 * t : 256 * (t + 1)])
+        values += [value[:, :128], value[:, 128:]]
     for t in range(10):
         for high in range(2):
-            first = 256 * t + 8 * high
-            items = [levels[pl.ds(first + l, 16, stride=16), :] for l in range(8)]
+            levels = range(128 * high, 128 * (high + 1), 16)
+            items = [values[t][l : l + 16, :] for l in levels]
             for b, item in enumerate(exchange_lanes(items, 16)):
                 start = 160 * (8 * (t % 2) + b) + 2 * (t // 2) + high
                 rows[pl.ds(start, 16, stride=10), :] = item
@@ -356,7 +352,7 @@
 
     message = pl.pallas_call(
         lambda *refs: send_kernel(truncation, *refs),
-        in_specs=[SMEM, HBM, VMEM, HBM, HBM],
+        in_specs=[SMEM, HBM, HBM, HBM, HBM],
         out_specs=HBM,
         out_shape=pltpu.HBM((NB, GROUPS, 16, 256), BF16),
         scratch_shapes=[
@@ -366,13 +362,14 @@
             pltpu.VMEM(legendre.shape, BF16),
             pltpu.VMEM((NB, GROUPS, 16, 256), BF16),
             pltpu.SMEM(slot_pair.shape, jnp.int32),
-            pltpu.SemaphoreType.DMA((GROUPS + 2,)),
+            pltpu.VMEM((1, 256), jnp.int32),
+            pltpu.SemaphoreType.DMA((GROUPS + 3,)),
             pltpu.SemaphoreType.DMA((GROUPS,)),
         ],
         compiler_params=params(),
         cost_estimate=cost(2 * 20 * 128 * 768 * 128, 5_000_000),
         name="legendre_send",
-    )(band, in_hbm(slot_pair), lane_latitude, in_hbm(by_slot), in_hbm(legendre))
+    )(band, in_hbm(slot_pair), in_hbm(lane_latitude), in_hbm(by_slot), in_hbm(legendre))
     received = lax.all_to_all(message, "band", split_axis=0, concat_axis=0, tiled=True)
 
     per_step = 2
@@ -405,7 +402,7 @@
             SMEM, SMEM, SMEM, SMEM,
             whole((NB, GROUPS, 16, 256)),
             whole((1, WAVES)),
-            HBM,
+            pl.BlockSpec((per_step, 256, WAVES), lambda i: (i, 0, 0)),
             pl.BlockSpec((per_step, 16, WAVES), lambda i: (i, 0, 0)),
             pl.BlockSpec((per_step, 16, WAVES), lambda i: (i, 0, 0)),
             pl.BlockSpec((per_step, 1, row_width), lambda i: (i, 0, 0)),
@@ -422,8 +419,6 @@
             pltpu.VMEM((NB, 16, WAVES), F32),
             pltpu.VMEM((per_step, 176, WAVES), BF16),
             pltpu.VMEM((per_step, 176, 256), BF16),
-            pltpu.VMEM((NB, 256, WAVES), BF16),
-            pltpu.SemaphoreType.DMA((NB,)),
         ],
         compiler_params=params(32),
         cost_estimate=cost(4 * 16 * 176 * 1280 * 256, 17_000_000),
@@ -437,7 +432,7 @@
         in_specs=[VMEM, VMEM],
         out_specs=VMEM,
         out_shape=jax.ShapeDtypeStruct((ROWS, 128), BF16),
-        scratch_shapes=[pltpu.VMEM((ROWS, 128), F32), pltpu.VMEM((ROWS, 128), F32)],
+        scratch_shapes=[pltpu.VMEM((ROWS, 128), F32)],
         compiler_params=params(),
         cost_estimate=cost(2 * 256 * 256 * 1280, 1_400_000),
         name="vertical_mix",

time: 106 us -> 100 us (0.943)
  Pallas kernels: 36 us -> 31.3 us
    pallas_call x1, Pallas kernels: 15 us -> 10.6 us  [per_device(): pl.pallas_call(lambda *refs: rows_kernel(per_step, *refs), grid=(NB // pe...]
  transfers between devices with their start and end apart: 1 -> 1, of which waited for: 1 -> 1; matrix products, arithmetic and copies ran while one was open for 1% -> 1% of each run, Pallas kernels for 9% -> 10%
where the time goes in v6:
time: 100 us
  blocking collectives  47.6 us (48%)
  Pallas kernels  31.3 us (31%)
  starting transfers between devices  10.1 us (10%)
  waiting for transfers between devices  8.89 us (9%)
  local copies, waits for them, and re-layouts  1.37 us (1%)
    all_to_all x1, blocking collectives, everywhere(): lax.all_to_all(pieces, ('band', 'lev'), split_axis=0, concat_axis=0, tile...  28.5 us
    all_to_all x1, blocking collectives, per_device(): lax.all_to_all(harmonic, 'lev', split_axis=0, concat_axis=0, tiled=True)  19.2 us
    pallas_call x1, Pallas kernels, per_device(): pl.pallas_call(lambda *refs: rows_kernel(per_step, *refs), grid=(NB // pe...  10.6 us
    all_to_all x1, starting transfers between devices, per_device(): lax.all_to_all(message, 'band', split_axis=0, concat_axis=0, tiled=True)  10.1 us
    pallas_call x1, Pallas kernels, per_device(): pl.pallas_call(lambda *refs: table_kernel(per_step, *refs), grid=(NB // p...  9.72 us
    all_to_all x1, waiting for transfers between devices, per_device(): lax.all_to_all(message, 'band', split_axis=0, concat_axis=0, tiled=True)  8.89 us
    pallas_call x1, Pallas kernels, per_device(): pl.pallas_call(lambda *refs: send_kernel(truncation, *refs), in_specs=[SM...  5.43 us
    pallas_call x1, Pallas kernels, per_device(): pl.pallas_call(lambda *refs: final_kernel(truncation, *refs), in_specs=[S...  3.18 us
  transfers between devices with their start and end apart: 1, of which 1 were waited for; matrix products, arithmetic and copies ran while one was open for 1% of the time, Pallas kernels for 10%

profile of v6, /device:TPU:1, one launch (start us, length us, event | category | flops | bytes accessed | tf_op | source)
XLA Modules:
  0.0 100.1 jit_solution(3318886348165506038)
XLA Ops:
  0.6 0.0 copy-start.2
  0.6 5.4 %legendre_send.1 = bf16[16,5,16,256]{3,2,1,0:T(8,128)(2,1)} custom-call(s32[1]{0:T(128)} %bitcast.refs_0_, s32[320]{0:T(512)} %refs_1_.7, s32[1,256]{1,0:T(1,128)} %bitcast.24, bf16[16,20,2,641]{3,2,1,0:T(2,128)(2,1)} %bitcast.28, bf16[20,641,128]{2,1,0:T(8,128)(2,1)} %bitcast.20), custom_call_target="tpu_custom_call" | custom-call | flops 503316480 | bytes 5000000 | tf_op jit(solution)/shard_map/legendre_send/pallas_call | solution.py:353
  6.1 0.0 copy-start.7
  6.1 0.0 copy-start.3
  6.1 0.0 copy-start.5
  6.1 0.0 copy-start.6
  6.1 10.1 %all-to-all-start = ((bf16[16,5,16,256]{3,2,1,0:T(8,128)(2,1)}), bf16[16,5,16,256]{3,2,1,0:T(8,128)(2,1)S(1)}, u32[]{:S(2)}, u32[]{:S(2)}) async-start(bf16[16,5,16,256]{3,2,1,0:T(8,128)(2,1)} %legendre_send.1), calls=%async_computation | async-start | bytes 1310720 | tf_op jit(solution)/shard_map/all_to_all | solution.py:373
  16.3 0.0 copy-done.2
  16.3 0.1 reshape.44
  16.4 0.1 copy.19
  16.5 0.2 copy.22
  16.7 0.4 broadcast_in_dim.2
  17.1 0.4 convert_element_type.7.refs_3_.refs_5_
  17.5 0.0 copy-done.7
  17.5 0.1 reshape.51.refs_9_
  17.6 0.0 copy-done.3
  17.7 0.0 copy-done.5
  17.7 9.7 %phase_tables.1 = (bf16[16,256,1280]{2,1,0:T(8,128)(2,1)}, f32[16,16,1280]{2,1,0:T(8,128)S(1)}, f32[16,16,1280]{2,1,0:T(8,128)S(1)}) custom-call(s32[1]{0:T(128)} %bitcast.refs_0_, s32[256]{0:T(256)S(1)} %copy-done.3, s32[128]{0:T(128)S(1)} %copy-done.5, f32[1,1280]{1,0:T(1,128)S(1)} %convert_element_type.7.refs_3_.refs_5_), custom_call_target="tpu_custom_call" | custom-call | flops 104857600 | bytes 14000000 | tf_op jit(solution)/shard_map/phase_tables/pallas_call | solution.py:376
  27.4 8.9 %all-to-all-done.refs_4_ = bf16[16,5,16,256]{3,2,1,0:T(8,128)(2,1)S(1)} async-done(((bf16[16,5,16,256]{3,2,1,0:T(8,128)(2,1)}), bf16[16,5,16,256]{3,2,1,0:T(8,128)(2,1)S(1)}, u32[]{:S(2)}, u32[]{:S(2)}) %all-to-all-start) | async-done | bytes 655392 | tf_op jit(solution)/shard_map/all_to_all | solution.py:373
  36.3 0.0 copy-done.6
  36.3 0.0 copy-start.1
  36.3 10.6 %grid_rows.1 = (bf16[16,16,2688]{2,1,0:T(8,128)(2,1)}, bf16[16,16,1280]{2,1,0:T(8,128)(2,1)S(1)}) custom-call(s32[1]{0:T(128)} %bitcast.refs_0_, s32[256]{0:T(256)S(1)} %copy-done.3, s32[128]{0:T(128)S(1)} %copy-done.5, s32[128]{0:T(128)S(1)} %copy-done.6, bf16[16,5,16,256]{3,2,1,0:T(8,128)(2,1)S(1)} %all-to-all-done.refs_4_, ...), custom_call_target="tpu_custom_call" | custom-call | flops 3690987520 | bytes 17000000 | tf_op jit(solution)/shard_map/grid_rows/pallas_call | solution.py:398
  46.9 0.0 copy-start
  46.9 0.0 copy-start.4
  46.9 19.2 %all_to_all.15.received = bf16[16,16,1280]{2,1,0:T(8,128)(2,1)S(1)} all-to-all(bf16[16,16,1280]{2,1,0:T(8,128)(2,1)S(1)} %get-tuple-element.11), channel_id=1, replica_groups=mesh['band'=16,'lev'=16] {'lev'}, dimensions={0} | all-to-all | bytes 1310720 | tf_op jit(solution)/shard_map/all_to_all | solution.py:429
  66.1 0.0 copy-done.1
  66.1 2.4 %vertical_mix.1 = bf16[2560,128]{1,0:T(8,128)(2,1)S(1)} custom-call(bf16[256,256]{1,0:T(8,128)(2,1)S(1)} %copy-done.1, bf16[16,16,1280]{2,1,0:T(8,128)(2,1)S(1)} %all_to_all.15.received), custom_call_target="tpu_custom_call" | custom-call | flops 167772160 | bytes 1400000 | tf_op jit(solution)/shard_map/vertical_mix/pallas_call | solution.py:430
  68.5 28.5 %all_to_all.16 = bf16[1280,2,128]{2,1,0:T(2,128)(2,1)S(1)} all-to-all(bf16[1280,2,128]{2,1,0:T(2,128)(2,1)S(1)} %bitcast.23), channel_id=1, replica_groups=mesh['band'=16,'lev'=16] {'band','lev'}, dimensions={0} | all-to-all | bytes 1310720 | tf_op jit(solution)/shard_map/all_to_all | solution.py:335
  96.9 0.0 copy-done
  97.0 0.0 copy-done.4
  97.0 3.2 %legendre_return.1 = f32[16,20,2,641]{3,2,1,0:T(2,128)} custom-call(s32[1]{0:T(128)} %bitcast.refs_0_, s32[320]{0:T(512)S(1)} %copy-done.2, s32[1,256]{1,0:T(1,128)S(1)} %bitcast.25, f32[1,128]{1,0:T(1,128)S(1)} %bitcast.26, bf16[2560,128]{1,0:T(8,128)(2,1)S(1)} %bitcast.22, bf16[20,641,128]{2,1,0:T(8,128)(2,1)S(1)} %bitcast.21), custom_call_target="tpu_custom_call" | custom-call | flops 503316480 | bytes 6000000 | tf_op jit(solution)/shard_map/legendre_return/pallas_call | solution.py:442
  (2 shorter events, 0.0 us)
Async XLA Ops:
  0.6 15.6 %copy-start.2 = (s32[320]{0:T(512)S(1)}, s32[320]{0:T(512)}, u32[]{:S(2)}) copy-start(s32[320]{0:T(512)} %refs_1_.7) | copy-start | bytes 3844
  6.1 11.5 %copy-start.7 = (bf16[16,2688]{1,0:T(8,128)(2,1)S(1)}, bf16[16,2688]{1,0:T(8,128)(2,1)}, u32[]{:S(2)}) copy-start(bf16[16,2688]{1,0:T(8,128)(2,1)} %param.13) | copy-start | bytes 258052
  6.1 11.6 %copy-start.3 = (s32[256]{0:T(256)S(1)}, s32[256]{0:T(256)}, u32[]{:S(2)}) copy-start(s32[256]{0:T(256)} %refs_1_.6) | copy-start | bytes 3076
  6.1 11.6 %copy-start.5 = (s32[128]{0:T(128)S(1)}, s32[128]{0:T(128)}, u32[]{:S(2)}) copy-start(s32[128]{0:T(128)} %refs_2_.3) | copy-start | bytes 1540
  6.1 30.2 %copy-start.6 = (s32[128]{0:T(128)S(1)}, s32[128]{0:T(128)}, u32[]{:S(2)}) copy-start(s32[128]{0:T(128)} %refs_3_.1) | copy-start | bytes 1540
  6.1 30.2 %all-to-all-start = ((bf16[16,5,16,256]{3,2,1,0:T(8,128)(2,1)}), bf16[16,5,16,256]{3,2,1,0:T(8,128)(2,1)S(1)}, u32[]{:S(2)}, u32[]{:S(2)}) async-start(bf16[16,5,16,256]{3,2,1,0:T(8,128)(2,1)} %legendre_send.1), calls=%async_computation | async-start | bytes 1310720 | tf_op jit(solution)/shard_map/all_to_all | solution.py:373
  36.3 29.8 %copy-start.1 = (bf16[256,256]{1,0:T(8,128)(2,1)S(1)}, bf16[256,256]{1,0:T(8,128)(2,1)}, u32[]{:S(2)}) copy-start(bf16[256,256]{1,0:T(8,128)(2,1)} %vertical.1) | copy-start | bytes 393220
  46.9 50.0 %copy-start = (bf16[20,128,641]{1,2,0:T(8,128)(2,1)S(1)}, bf16[20,128,641]{1,2,0:T(8,128)(2,1)}, u32[]{:S(2)}) copy-start(bf16[20,128,641]{1,2,0:T(8,128)(2,1)} %param.10) | copy-start | bytes 9845764
  46.9 50.0 %copy-start.4 = (f32[128]{0:T(128)S(1)}, f32[128]{0:T(128)}, u32[]{:S(2)}) copy-start(f32[128]{0:T(128)} %param.11) | copy-start | bytes 1540

commit v7 on v6

--- a/solution.py
+++ b/solution.py
@@ -12,6 +12,7 @@
 GROUPS = 5
 ROWS = 2560
 WAVES = 1280
+HALF = 640
 COS = (1.0, -19.739208221435547, 64.93938446044922, -85.45658111572266,
        60.241241455078125, -26.39919662475586, 7.783571243286133, -1.4335278272628784)
 SIN = (6.2831854820251465, -41.34170150756836, 81.6052474975586, -76.70577239990234,
@@ -65,16 +66,6 @@
     return items
 
 
-def swap_parts(x):
-    lane = lax.broadcasted_iota(jnp.int32, (x.shape[0], 128), 1)
-    even = (lane & 1) == 0
-    pieces = []
-    for t in range(x.shape[1] // 128):
-        piece = x[:, 128 * t : 128 * (t + 1)]
-        pieces.append(jnp.where(even, pltpu.roll(piece, 127, 1), pltpu.roll(piece, 1, 1)))
-    return jnp.concatenate(pieces, 1)
-
-
 def slot_columns(pair, width, truncation):
     column = lax.broadcasted_iota(jnp.int32, (1, width), 1)
     split = truncation + 1 - pair
@@ -83,18 +74,19 @@
     return first, odd
 
 
-def table_kernel(rows_per_step, band, row_latitude, points, waves, table, outer_cos, outer_sin, seeds):
+def table_kernel(
+    rows_per_step, band, row_latitude, points, waves, table, outer_cos, outer_sin, seeds
+):
     step = pl.program_id(0)
     wave = waves[...]
-    imag = (lax.broadcasted_iota(jnp.int32, (1, WAVES), 1) & 1) == 1
-    index = lax.broadcasted_iota(jnp.int32, (16, WAVES), 0).astype(F32)
     for r in range(rows_per_step):
         lat = row_latitude[band[0] * NB + step * rows_per_step + r] & (points.shape[0] - 1)
-        count = jnp.full((1, WAVES), points[lat].astype(F32))
+        count = jnp.full((1, HALF), 2.0 * points[lat].astype(F32))
         inverse = 1.0 / count
 
-        def circle(stride):
-            product = (wave * stride) * index
+        def circle(rows, stride, offset):
+            index = lax.broadcasted_iota(jnp.int32, (rows, HALF), 0).astype(F32)
+            product = wave * (index * stride + offset)
             turns = jnp.floor(product * inverse + 0.5)
             y = (product - turns * count) * inverse
             z = y * y
@@ -105,21 +97,23 @@
                 s = s * z + SIN[k]
             return c, s * y
 
-        c1, s1 = circle(1.0)
-        c2, s2 = circle(16.0)
-        seeds[0] = jnp.where(imag, s2, c2)
-        seeds[1] = jnp.where(imag, -c2, s2)
-        seeds[2] = c1
-        seeds[3] = s1
-        c3, s3 = circle(256.0)
+        c1, s1 = circle(16, 2.0, 1.0)
+        c2, s2 = circle(16, 32.0, 0.0)
+        seeds[0] = c1
+        seeds[1] = s1
+        seeds[2] = c2
+        seeds[3] = s2
+        c3, s3 = circle(8, 1024.0, 511.0)
         outer_cos[r] = c3
         outer_sin[r] = s3
         for t in range(5):
-            lanes = slice(256 * t, 256 * (t + 1))
-            c1, s1 = seeds[2, :, lanes], seeds[3, :, lanes]
+            lanes = slice(128 * t, 128 * (t + 1))
+            c1, s1 = seeds[0, :, lanes], seeds[1, :, lanes]
             for a in range(16):
-                value = seeds[0, a : a + 1, lanes] * c1 - seeds[1, a : a + 1, lanes] * s1
-                table[r, 16 * a : 16 * (a + 1), lanes] = value.astype(BF16)
+                c2, s2 = seeds[2, a : a + 1, lanes], seeds[3, a : a + 1, lanes]
+                rows = slice(16 * a, 16 * (a + 1))
+                table[r, 0, rows, lanes] = (c2 * c1 - s2 * s1).astype(BF16)
+                table[r, 1, rows, lanes] = (s2 * c1 + c2 * s1).astype(BF16)
 
 
 def send_kernel(
@@ -139,11 +133,8 @@
         copies.append(pltpu.make_async_copy(legendre.at[cut], legendre_in.at[cut], ready.at[g]))
         copies[g].start()
     index = lax.broadcasted_iota(jnp.int32, (256, 256), 0)
-    lane = lax.broadcasted_iota(jnp.int32, (256, 256), 1)
     rows.wait()
     place = (index == lane_latitude[...]).astype(F32).astype(BF16)
-    by_row = (index == ((lane & 15) << 4 | lane >> 4)).astype(F32).astype(BF16)
-    place = dot(place, by_row).astype(BF16)
     slots.wait()
     whole_spectral.wait()
     for g in range(GROUPS):
@@ -166,9 +157,9 @@
         spread[g, 1] = placed[:, 128:]
         items = []
         for u in range(16):
-            at = pl.ds(32 * (u >> 1) + (u & 1), 16, stride=2)
+            at = pl.ds(32 * (u & 7) + (u >> 3), 16, stride=2)
             items.append((spread[g, 0, at, :], spread[g, 1, at, :]))
-        for b, (lo, hi) in enumerate(exchange_chunks(items, 1)):
+        for b, (lo, hi) in enumerate(exchange_chunks(items, 16)):
             messages[b, g, :, :128] = lo.astype(BF16)
             messages[b, g, :, 128:] = hi.astype(BF16)
         cut = pl.ds(g, 1)
@@ -180,7 +171,7 @@
 
 def rows_kernel(
     rows_per_step, band, row_latitude, points, cutoffs, received, waves, table, outer_cos,
-    outer_sin, factor, grid_field, out, fourier, twisted, samples
+    outer_sin, factor_left, factor_right, grid_field, out, fourier, twisted, samples
 ):
     step = pl.program_id(0)
 
@@ -191,12 +182,12 @@
             for src in range(NB):
                 block = received[src, g].astype(F32)
                 items.append((block[:, :128], block[:, 128:]))
-            for row, (lo, hi) in enumerate(exchange_chunks(items, 16)):
-                fourier[row, :, 256 * g : 256 * g + 128] = lo
-                fourier[row, :, 256 * g + 128 : 256 * g + 256] = hi
+            for row, parts in enumerate(exchange_chunks(items, 1)):
+                for h in range(2):
+                    fourier[row, h, :, 128 * g : 128 * (g + 1)] = parts[h]
 
     lane = lax.broadcasted_iota(jnp.int32, (1, 256), 1)
-    sign = jnp.where((lane & 1) == 1, F32(-1.0), F32(1.0))
+    backward = 127 - lax.broadcasted_iota(jnp.int32, (16, 128), 1)
 
     def limits(r):
         lat = row_latitude[band[0] * NB + step * rows_per_step + r] & (points.shape[0] - 1)
@@ -205,46 +196,64 @@
     def twist(r):
         cutoff = limits(r)[1]
         for t in range(5):
-            lanes = slice(256 * t, 256 * (t + 1))
+            lanes = slice(128 * t, 128 * (t + 1))
             wave = waves[:, lanes]
             kept = (wave <= cutoff).astype(F32)
             weight = kept * jnp.where(wave == 0.0, F32(1.0), F32(2.0))
-            x = fourier[step * rows_per_step + r, :, lanes]
-            crossed = swap_parts(x) * -weight
-            x = x * (weight * sign)
-            for b in range(11):
+            real = fourier[step * rows_per_step + r, 0, :, lanes] * weight
+            imag = fourier[step * rows_per_step + r, 1, :, lanes] * weight
+            for b in range(6):
                 cosine, sine = outer_cos[r, b : b + 1, lanes], outer_sin[r, b : b + 1, lanes]
-                value = x * cosine + crossed * sine
-                twisted[r, 16 * b : 16 * (b + 1), lanes] = value.astype(BF16)
+                rows = slice(16 * b, 16 * (b + 1))
+                twisted[r, 0, rows, lanes] = (real * cosine - imag * sine).astype(BF16)
+                twisted[r, 1, rows, lanes] = (real * sine + imag * cosine).astype(BF16)
 
     def inverse(r):
         count = limits(r)[0]
-        field = dot(twisted[r], table[r], NT)
-        for b in range(11):
-            size = 256 if b < 10 else 128
-            cut = slice(256 * b, 256 * b + size)
-            value = jnp.where(lane + 256 * b < count, field[16 * b : 16 * (b + 1), :], 0.0)
-            value = value.astype(BF16)[:, :size]
-            grid_field[r, :, cut] = value
-            scaled = value.astype(F32) * factor[r, :, cut]
-            samples[r, 16 * b : 16 * (b + 1), :size] = scaled.astype(BF16)
-        samples[r, 160:176, 128:] = jnp.zeros((16, 128), BF16)
+        even = dot(twisted[r, 0], table[step * rows_per_step + r, 0], NT)
+        odd = dot(twisted[r, 1], table[step * rows_per_step + r, 1], NT)
+        for b in range(6):
+            rows, lanes = slice(16 * b, 16 * (b + 1)), slice(256 * b, 256 * (b + 1))
+            left = jnp.where(512 * b + 255 - lane < count, even[rows] + odd[rows], 0.0)
+            for k in range(2 if b < 5 else 1):
+                piece = left[:, 128:] if k == 0 else left[:, :128]
+                turned = jnp.take_along_axis(piece, backward, axis=1).astype(BF16)
+                at = 512 * b + 128 * k
+                grid_field[r, :, at : at + 128] = turned
+            left = left.astype(BF16).astype(F32) * factor_left[r, :, lanes]
+            if b < 5:
+                right = jnp.where(512 * b + 256 + lane < count, even[rows] - odd[rows], 0.0)
+                right = right.astype(BF16)
+                grid_field[r, :, 512 * b + 256 : 512 * b + 512] = right
+                right = right.astype(F32) * factor_right[r, :, lanes]
+                samples[r, 0, rows] = (right + left).astype(BF16)
+                samples[r, 1, rows] = (right - left).astype(BF16)
+            else:
+                samples[r, 0, rows] = left.astype(BF16)
+                samples[r, 1, rows] = (-left).astype(BF16)
 
     def direct(r):
         count, cutoff = limits(r)
-        for t in range(5):
-            lanes = slice(256 * t, 256 * (t + 1))
+        for start in range(0, HALF, 256):
+            size = min(256, HALF - start)
+            lanes = slice(start, start + size)
+            even = dot(samples[r, 0], table[step * rows_per_step + r, 0, :, lanes])
+            odd = dot(samples[r, 1], table[step * rows_per_step + r, 1, :, lanes])
+            real = jnp.zeros((16, size), F32)
+            imag = jnp.zeros((16, size), F32)
+            for b in range(6):
+                rows = slice(16 * b, 16 * (b + 1))
+                cosine, sine = outer_cos[r, b : b + 1, lanes], outer_sin[r, b : b + 1, lanes]
+                real = real + (even[rows] * cosine - odd[rows] * sine)
+                imag = imag + (even[rows] * sine + odd[rows] * cosine)
             kept = (waves[:, lanes] <= cutoff).astype(F32)
-            scale = kept / jnp.full((1, 256), count.astype(F32))
-            part = dot(samples[r], table[r, :, lanes])
-            total_cos = jnp.zeros((16, 256), F32)
-            total_sin = jnp.zeros((16, 256), F32)
-            for b in range(11):
-                block = part[16 * b : 16 * (b + 1), :]
-                total_cos = total_cos + block * outer_cos[r, b : b + 1, lanes]
-                total_sin = total_sin + block * outer_sin[r, b : b + 1, lanes]
-            value = sign * total_cos - swap_parts(total_sin)
-            out[r, :, lanes] = (value * scale).astype(BF16)
+            scale = kept / jnp.full((1, size), count.astype(F32))
+            real = (real * scale).astype(BF16)
+            imag = (imag * -scale).astype(BF16)
+            for k in range(size // 128):
+                at, piece = 2 * (start + 128 * k), slice(128 * k, 128 * (k + 1))
+                out[r, :, at : at + 128] = real[:, piece]
+                out[r, :, at + 128 : at + 256] = imag[:, piece]
 
     twist(0)
     for r in range(rows_per_step):
@@ -267,12 +276,9 @@
         value = dot(matrix, block[:, 256 * t : 256 * (t + 1)])
         values += [value[:, :128], value[:, 128:]]
     for t in range(10):
-        for high in range(2):
-            levels = range(128 * high, 128 * (high + 1), 16)
-            items = [values[t][l : l + 16, :] for l in levels]
-            for b, item in enumerate(exchange_lanes(items, 16)):
-                start = 160 * (8 * (t % 2) + b) + 2 * (t // 2) + high
-                rows[pl.ds(start, 16, stride=10), :] = item
+        items = [values[t][l : l + 16, :] for l in range(0, 256, 16)]
+        for b, item in enumerate(exchange_lanes(items, 1)):
+            rows[pl.ds(160 * b + t, 16, stride=10), :] = item
     out[...] = rows[...].astype(BF16)
 
 
@@ -284,8 +290,8 @@
     target = lax.broadcasted_iota(jnp.int32, (256, 256), 0)
     lane = lax.broadcasted_iota(jnp.int32, (256, 256), 1)
     source = lane_latitude[...]
-    wave = ((target >> 5) << 1) | (target & 1)
-    turn = ((lane >> 4 == ((target >> 1) & 15)) & ((lane & 15) == wave)).astype(F32).astype(BF16)
+    wave = ((target & 1) << 3) | (target >> 5)
+    turn = ((lane >> 4 == wave) & ((lane & 15) == ((target >> 1) & 15))).astype(F32).astype(BF16)
     value = jnp.where((target >= 128) & (source >= 128), F32(-1.0), F32(1.0))
     fold = jnp.where((target & 127) == (source & 127), value, 0.0).astype(BF16)
     doubled = jnp.concatenate([weights[...], weights[...]], 1)
@@ -346,9 +352,8 @@
     by_slot = spectral.transpose(0, 2, 1, 3)
     legendre = legendre.transpose(0, 2, 1)
     lane_latitude = row_latitude.reshape(1, 256)
-    pairs = slot_pair.reshape(NB, GROUPS, 4).transpose(1, 0, 2)
-    waves = jnp.stack([pairs, truncation - pairs], -1)
-    waves = jnp.broadcast_to(waves[..., None], waves.shape + (2,)).reshape(1, WAVES).astype(F32)
+    pairs = slot_pair.reshape(NB, GROUPS, 4).transpose(1, 2, 0)
+    waves = jnp.stack([pairs, truncation - pairs], 2).reshape(1, HALF).astype(F32)
 
     message = pl.pallas_call(
         lambda *refs: send_kernel(truncation, *refs),
@@ -376,36 +381,39 @@
     table, outer_cos, outer_sin = pl.pallas_call(
         lambda *refs: table_kernel(per_step, *refs),
         grid=(NB // per_step,),
-        in_specs=[SMEM, SMEM, SMEM, whole((1, WAVES))],
+        in_specs=[SMEM, SMEM, SMEM, whole((1, HALF))],
         out_specs=[
-            pl.BlockSpec((per_step, 256, WAVES), lambda i: (i, 0, 0)),
-            pl.BlockSpec((per_step, 16, WAVES), lambda i: (i, 0, 0)),
-            pl.BlockSpec((per_step, 16, WAVES), lambda i: (i, 0, 0)),
+            pl.BlockSpec((per_step, 2, 256, HALF), lambda i: (i, 0, 0, 0)),
+            pl.BlockSpec((per_step, 8, HALF), lambda i: (i, 0, 0)),
+            pl.BlockSpec((per_step, 8, HALF), lambda i: (i, 0, 0)),
         ],
         out_shape=[
-            pltpu.HBM((NB, 256, WAVES), BF16),
-            jax.ShapeDtypeStruct((NB, 16, WAVES), F32),
-            jax.ShapeDtypeStruct((NB, 16, WAVES), F32),
-        ],
-        scratch_shapes=[pltpu.VMEM((4, 16, WAVES), F32)],
+            pltpu.VMEM((NB, 2, 256, HALF), BF16),
+            jax.ShapeDtypeStruct((NB, 8, HALF), F32),
+            jax.ShapeDtypeStruct((NB, 8, HALF), F32),
+        ],
+        scratch_shapes=[pltpu.VMEM((4, 16, HALF), F32)],
         compiler_params=params(),
-        cost_estimate=cost(16 * 256 * 1280 * 20, 14_000_000),
+        cost_estimate=cost(16 * 256 * 1280 * 20, 7_000_000),
         name="phase_tables",
     )(band, row_latitude, points, waves)
 
-    per_step = 4
-    factor = grid_factor.astype(F32).reshape(NB, 1, row_width)
+    per_step = 8
+    factor = jnp.pad(grid_factor, ((0, 0), (0, 3072 - row_width))).reshape(NB, 6, 2, 256).astype(F32)
+    factor_left = factor[:, :, 0, ::-1].reshape(NB, 1, 1536)
+    factor_right = factor[:, :5, 1].reshape(NB, 1, 1280)
     grid_field, harmonic = pl.pallas_call(
         lambda *refs: rows_kernel(per_step, *refs),
         grid=(NB // per_step,),
         in_specs=[
             SMEM, SMEM, SMEM, SMEM,
             whole((NB, GROUPS, 16, 256)),
-            whole((1, WAVES)),
-            pl.BlockSpec((per_step, 256, WAVES), lambda i: (i, 0, 0)),
-            pl.BlockSpec((per_step, 16, WAVES), lambda i: (i, 0, 0)),
-            pl.BlockSpec((per_step, 16, WAVES), lambda i: (i, 0, 0)),
-            pl.BlockSpec((per_step, 1, row_width), lambda i: (i, 0, 0)),
+            whole((1, HALF)),
+            VMEM,
+            pl.BlockSpec((per_step, 8, HALF), lambda i: (i, 0, 0)),
+            pl.BlockSpec((per_step, 8, HALF), lambda i: (i, 0, 0)),
+            pl.BlockSpec((per_step, 1, 1536), lambda i: (i, 0, 0)),
+            pl.BlockSpec((per_step, 1, 1280), lambda i: (i, 0, 0)),
         ],
         out_specs=[
             pl.BlockSpec((per_step, 16, row_width), lambda i: (i, 0, 0)),
@@ -416,15 +424,15 @@
             jax.ShapeDtypeStruct((NB, 16, WAVES), BF16),
         ],
         scratch_shapes=[
-            pltpu.VMEM((NB, 16, WAVES), F32),
-            pltpu.VMEM((per_step, 176, WAVES), BF16),
-            pltpu.VMEM((per_step, 176, 256), BF16),
-        ],
-        compiler_params=params(32),
+            pltpu.VMEM((NB, 2, 16, HALF), F32),
+            pltpu.VMEM((per_step, 2, 96, HALF), BF16),
+            pltpu.VMEM((per_step, 2, 96, 256), BF16),
+        ],
+        compiler_params=params(),
         cost_estimate=cost(4 * 16 * 176 * 1280 * 256, 17_000_000),
         name="grid_rows",
-    )(band, row_latitude, points, cutoffs, received, waves, in_hbm(table), outer_cos, outer_sin,
-      factor)
+    )(band, row_latitude, points, cutoffs, received, waves, pltpu.with_memory_space_constraint(table, pltpu.VMEM), outer_cos, outer_sin,
+      factor_left, factor_right)
 
     levels_in = lax.all_to_all(harmonic, "lev", split_axis=0, concat_axis=0, tiled=True)
     outgoing = pl.pallas_call(

time: 100 us -> 103 us (1.030)
  local copies, waits for them, and re-layouts: 1.37 us -> 9.05 us
  Pallas kernels: 31.3 us -> 25.6 us
    unnamed x16 -> x21, local copies, waits for them, and re-layouts: 0.04 us -> 7.99 us
    pallas_call x1, Pallas kernels: 9.72 us -> 5.67 us  [per_device(): pl.pallas_call(lambda *refs: table_kernel(per_step, *refs), grid=(NB // p...]
    pallas_call x1, Pallas kernels: 10.6 us -> 8.91 us  [per_device(): pl.pallas_call(lambda *refs: rows_kernel(per_step, *refs), grid=(NB // pe...]
  transfers between devices with their start and end apart: 1 -> 1, of which waited for: 1 -> 1; matrix products, arithmetic and copies ran while one was open for 1% -> 1% of each run, Pallas kernels for 10% -> 6%
where the time goes in v7:
time: 103 us; the launch traced here: 102 us
  blocking collectives  47.7 us (46%)
  Pallas kernels  25.6 us (25%)
  starting transfers between devices  9.99 us (10%)
  waiting for transfers between devices  9.18 us (9%)
  local copies, waits for them, and re-layouts  9.05 us (9%)
    all_to_all x1, blocking collectives, everywhere(): lax.all_to_all(pieces, ('band', 'lev'), split_axis=0, concat_axis=0, tile...  28.5 us
    all_to_all x1, blocking collectives, per_device(): lax.all_to_all(harmonic, 'lev', split_axis=0, concat_axis=0, tiled=True)  19.2 us
    all_to_all x1, starting transfers between devices, per_device(): lax.all_to_all(message, 'band', split_axis=0, concat_axis=0, tiled=True)  9.99 us
    all_to_all x1, waiting for transfers between devices, per_device(): lax.all_to_all(message, 'band', split_axis=0, concat_axis=0, tiled=True)  9.18 us
    pallas_call x1, Pallas kernels, per_device(): pl.pallas_call(lambda *refs: rows_kernel(per_step, *refs), grid=(NB // pe...  8.91 us
    unnamed x21, local copies, waits for them, and re-layouts  7.99 us
    pallas_call x1, Pallas kernels, per_device(): pl.pallas_call(lambda *refs: table_kernel(per_step, *refs), grid=(NB // p...  5.67 us
    pallas_call x1, Pallas kernels, per_device(): pl.pallas_call(lambda *refs: send_kernel(truncation, *refs), in_specs=[SM...  5.35 us
  transfers between devices with their start and end apart: 1, of which 1 were waited for; matrix products, arithmetic and copies ran while one was open for 1% of the time, Pallas kernels for 6%

profile of v7, /device:TPU:1, one launch (start us, length us, event | category | flops | bytes accessed | tf_op | source)
XLA Modules:
  0.0 102.3 jit_solution(16626067363729627511)
XLA Ops:
  0.6 0.0 copy-start.2
  0.6 0.0 copy-start.9
  0.7 0.0 copy-start.3
  0.7 0.0 copy-start.5
  0.7 0.0 copy-start.6
  0.7 5.3 %legendre_send.1 = bf16[16,5,16,256]{3,2,1,0:T(8,128)(2,1)} custom-call(s32[1]{0:T(128)} %bitcast.refs_0_, s32[320]{0:T(512)} %refs_1_.7, s32[1,256]{1,0:T(1,128)} %bitcast.24, bf16[16,20,2,641]{3,2,1,0:T(2,128)(2,1)} %bitcast.28, bf16[20,641,128]{2,1,0:T(8,128)(2,1)} %bitcast.19), custom_call_target="tpu_custom_call" | custom-call | flops 503316480 | bytes 5000000 | tf_op jit(solution)/shard_map/legendre_send/pallas_call | solution.py:358
  6.0 10.0 %all-to-all-start = ((bf16[16,5,16,256]{3,2,1,0:T(8,128)(2,1)}), bf16[16,5,16,256]{3,2,1,0:T(8,128)(2,1)S(1)}, u32[]{:S(2)}, u32[]{:S(2)}) async-start(bf16[16,5,16,256]{3,2,1,0:T(8,128)(2,1)} %legendre_send.1), calls=%async_computation | async-start | bytes 1310720 | tf_op jit(solution)/shard_map/all_to_all | solution.py:378
  16.0 0.0 copy-done.2
  16.0 0.1 reshape.41
  16.1 0.0 copy-done.9
  16.2 0.2 reshape.45
  16.3 0.1 slice.9
  16.4 0.1 slice.8
  16.5 0.1 copy.19
  16.6 0.1 copy.20
  16.8 0.1 convert_element_type.14.refs_3_.refs_5_
  16.9 0.2 rev.3
  17.1 0.1 reshape_squeeze.8.refs_9_
  17.2 0.0 copy-done.3
  17.2 0.0 copy-done.5
  17.2 5.7 %phase_tables.1 = (bf16[16,2,256,640]{3,2,1,0:T(8,128)(2,1)S(1)}, f32[16,8,640]{2,1,0:T(8,128)S(1)}, f32[16,8,640]{2,1,0:T(8,128)S(1)}) custom-call(s32[1]{0:T(128)} %bitcast.refs_0_, s32[256]{0:T(256)S(1)} %copy-done.3, s32[128]{0:T(128)S(1)} %copy-done.5, f32[1,640]{1,0:T(1,128)S(1)} %convert_element_type.14.refs_3_.refs_5_), custom_call_target="tpu_custom_call" | custom-call | flops 104857600 | bytes 7000000 | tf_op jit(solution)/shard_map/phase_tables/pallas_call | solution.py:381
  22.9 0.0 copy-start.7
  22.9 4.0 %copy-done.7 = bf16[16,2,256,640]{3,2,1,0:T(8,128)(2,1)} copy-done((bf16[16,2,256,640]{3,2,1,0:T(8,128)(2,1)}, bf16[16,2,256,640]{3,2,1,0:T(8,128)(2,1)S(1)}, u32[]{:S(2)}) %copy-start.7) | copy-done | bytes 10485784
  26.9 9.2 %all-to-all-done.refs_4_ = bf16[16,5,16,256]{3,2,1,0:T(8,128)(2,1)S(1)} async-done(((bf16[16,5,16,256]{3,2,1,0:T(8,128)(2,1)}), bf16[16,5,16,256]{3,2,1,0:T(8,128)(2,1)S(1)}, u32[]{:S(2)}, u32[]{:S(2)}) %all-to-all-start) | async-done | bytes 655392 | tf_op jit(solution)/shard_map/all_to_all | solution.py:378
  36.1 0.0 copy-done.6
  36.1 0.0 copy-start.8
  36.1 4.0 %copy-done.8 = bf16[16,2,256,640]{3,2,1,0:T(8,128)(2,1)S(1)} copy-done((bf16[16,2,256,640]{3,2,1,0:T(8,128)(2,1)S(1)}, bf16[16,2,256,640]{3,2,1,0:T(8,128)(2,1)}, u32[]{:S(2)}) %copy-start.8) | copy-done | bytes 10485784
  40.0 0.0 copy-start.1
  40.0 8.9 %grid_rows.1 = (bf16[16,16,2688]{2,1,0:T(8,128)(2,1)}, bf16[16,16,1280]{2,1,0:T(8,128)(2,1)S(1)}) custom-call(s32[1]{0:T(128)} %bitcast.refs_0_, s32[256]{0:T(256)S(1)} %copy-done.3, s32[128]{0:T(128)S(1)} %copy-done.5, s32[128]{0:T(128)S(1)} %copy-done.6, bf16[16,5,16,256]{3,2,1,0:T(8,128)(2,1)S(1)} %all-to-all-done.refs_4_, ...), custom_call_target="tpu_custom_call" | custom-call | flops 3690987520 | bytes 17000000 | tf_op jit(solution)/shard_map/grid_rows/pallas_call | solution.py:405
  49.0 0.0 copy-start
  49.0 0.0 copy-start.4
  49.0 19.2 %all_to_all.15.received = bf16[16,16,1280]{2,1,0:T(8,128)(2,1)S(1)} all-to-all(bf16[16,16,1280]{2,1,0:T(8,128)(2,1)S(1)} %get-tuple-element.11), channel_id=1, replica_groups=mesh['band'=16,'lev'=16] {'lev'}, dimensions={0} | all-to-all | bytes 1310720 | tf_op jit(solution)/shard_map/all_to_all | solution.py:437
  68.1 0.0 copy-done.1
  68.1 2.5 %vertical_mix.1 = bf16[2560,128]{1,0:T(8,128)(2,1)S(1)} custom-call(bf16[256,256]{1,0:T(8,128)(2,1)S(1)} %copy-done.1, bf16[16,16,1280]{2,1,0:T(8,128)(2,1)S(1)} %all_to_all.15.received), custom_call_target="tpu_custom_call" | custom-call | flops 167772160 | bytes 1400000 | tf_op jit(solution)/shard_map/vertical_mix/pallas_call | solution.py:438
  70.7 28.5 %all_to_all.16 = bf16[1280,2,128]{2,1,0:T(2,128)(2,1)S(1)} all-to-all(bf16[1280,2,128]{2,1,0:T(2,128)(2,1)S(1)} %bitcast.22), channel_id=1, replica_groups=mesh['band'=16,'lev'=16] {'band','lev'}, dimensions={0} | all-to-all | bytes 1310720 | tf_op jit(solution)/shard_map/all_to_all | solution.py:341
  99.2 0.0 copy-done
  99.2 0.0 copy-done.4
  99.2 3.2 %legendre_return.1 = f32[16,20,2,641]{3,2,1,0:T(2,128)} custom-call(s32[1]{0:T(128)} %bitcast.refs_0_, s32[320]{0:T(512)S(1)} %copy-done.2, s32[1,256]{1,0:T(1,128)S(1)} %bitcast.25, f32[1,128]{1,0:T(1,128)S(1)} %bitcast.26, bf16[2560,128]{1,0:T(8,128)(2,1)S(1)} %bitcast.21, bf16[20,641,128]{2,1,0:T(8,128)(2,1)S(1)} %bitcast.20), custom_call_target="tpu_custom_call" | custom-call | flops 503316480 | bytes 6000000 | tf_op jit(solution)/shard_map/legendre_return/pallas_call | solution.py:450
  (5 shorter events, 0.1 us)
Async XLA Ops:
  0.6 15.4 %copy-start.2 = (s32[320]{0:T(512)S(1)}, s32[320]{0:T(512)}, u32[]{:S(2)}) copy-start(s32[320]{0:T(512)} %refs_1_.7) | copy-start | bytes 3844
  0.6 15.5 %copy-start.9 = (bf16[16,2688]{1,0:T(8,128)(2,1)S(1)}, bf16[16,2688]{1,0:T(8,128)(2,1)}, u32[]{:S(2)}) copy-start(bf16[16,2688]{1,0:T(8,128)(2,1)} %param.13) | copy-start | bytes 258052
  0.7 16.6 %copy-start.3 = (s32[256]{0:T(256)S(1)}, s32[256]{0:T(256)}, u32[]{:S(2)}) copy-start(s32[256]{0:T(256)} %refs_1_.6) | copy-start | bytes 3076
  0.7 16.6 %copy-start.5 = (s32[128]{0:T(128)S(1)}, s32[128]{0:T(128)}, u32[]{:S(2)}) copy-start(s32[128]{0:T(128)} %refs_2_.3) | copy-start | bytes 1540
  0.7 35.4 %copy-start.6 = (s32[128]{0:T(128)S(1)}, s32[128]{0:T(128)}, u32[]{:S(2)}) copy-start(s32[128]{0:T(128)} %refs_3_.1) | copy-start | bytes 1540
  6.0 30.0 %all-to-all-start = ((bf16[16,5,16,256]{3,2,1,0:T(8,128)(2,1)}), bf16[16,5,16,256]{3,2,1,0:T(8,128)(2,1)S(1)}, u32[]{:S(2)}, u32[]{:S(2)}) async-start(bf16[16,5,16,256]{3,2,1,0:T(8,128)(2,1)} %legendre_send.1), calls=%async_computation | async-start | bytes 1310720 | tf_op jit(solution)/shard_map/all_to_all | solution.py:378
  22.9 4.0 %copy-start.7 = (bf16[16,2,256,640]{3,2,1,0:T(8,128)(2,1)}, bf16[16,2,256,640]{3,2,1,0:T(8,128)(2,1)S(1)}, u32[]{:S(2)}) copy-start(bf16[16,2,256,640]{3,2,1,0:T(8,128)(2,1)S(1)} %get-tuple-element.7.refs_6_) | copy-start | bytes 31457284
  36.1 4.0 %copy-start.8 = (bf16[16,2,256,640]{3,2,1,0:T(8,128)(2,1)S(1)}, bf16[16,2,256,640]{3,2,1,0:T(8,128)(2,1)}, u32[]{:S(2)}) copy-start(bf16[16,2,256,640]{3,2,1,0:T(8,128)(2,1)} %copy-done.7) | copy-start | bytes 31457284
  40.0 28.1 %copy-start.1 = (bf16[256,256]{1,0:T(8,128)(2,1)S(1)}, bf16[256,256]{1,0:T(8,128)(2,1)}, u32[]{:S(2)}) copy-start(bf16[256,256]{1,0:T(8,128)(2,1)} %vertical.1) | copy-start | bytes 393220
  49.0 50.2 %copy-start = (bf16[20,128,641]{1,2,0:T(8,128)(2,1)S(1)}, bf16[20,128,641]{1,2,0:T(8,128)(2,1)}, u32[]{:S(2)}) copy-start(bf16[20,128,641]{1,2,0:T(8,128)(2,1)} %param.10) | copy-start | bytes 9845764
  49.0 50.2 %copy-start.4 = (f32[128]{0:T(128)S(1)}, f32[128]{0:T(128)}, u32[]{:S(2)}) copy-start(f32[128]{0:T(128)} %param.11) | copy-start | bytes 1540

commit v8 on v7

--- a/solution.py
+++ b/solution.py
@@ -98,18 +98,18 @@
             return c, s * y
 
         c1, s1 = circle(16, 2.0, 1.0)
-        c2, s2 = circle(16, 32.0, 0.0)
+        c2, s2 = circle(8, 32.0, 0.0)
         seeds[0] = c1
         seeds[1] = s1
-        seeds[2] = c2
-        seeds[3] = s2
-        c3, s3 = circle(8, 1024.0, 511.0)
+        seeds[2, :8] = c2
+        seeds[3, :8] = s2
+        c3, s3 = circle(16, 512.0, 255.0)
         outer_cos[r] = c3
         outer_sin[r] = s3
         for t in range(5):
             lanes = slice(128 * t, 128 * (t + 1))
             c1, s1 = seeds[0, :, lanes], seeds[1, :, lanes]
-            for a in range(16):
+            for a in range(8):
                 c2, s2 = seeds[2, a : a + 1, lanes], seeds[3, a : a + 1, lanes]
                 rows = slice(16 * a, 16 * (a + 1))
                 table[r, 0, rows, lanes] = (c2 * c1 - s2 * s1).astype(BF16)
@@ -186,7 +186,7 @@
                 for h in range(2):
                     fourier[row, h, :, 128 * g : 128 * (g + 1)] = parts[h]
 
-    lane = lax.broadcasted_iota(jnp.int32, (1, 256), 1)
+    lane = lax.broadcasted_iota(jnp.int32, (1, 128), 1)
     backward = 127 - lax.broadcasted_iota(jnp.int32, (16, 128), 1)
 
     def limits(r):
@@ -202,7 +202,7 @@
             weight = kept * jnp.where(wave == 0.0, F32(1.0), F32(2.0))
             real = fourier[step * rows_per_step + r, 0, :, lanes] * weight
             imag = fourier[step * rows_per_step + r, 1, :, lanes] * weight
-            for b in range(6):
+            for b in range(11):
                 cosine, sine = outer_cos[r, b : b + 1, lanes], outer_sin[r, b : b + 1, lanes]
                 rows = slice(16 * b, 16 * (b + 1))
                 twisted[r, 0, rows, lanes] = (real * cosine - imag * sine).astype(BF16)
@@ -210,21 +210,18 @@
 
     def inverse(r):
         count = limits(r)[0]
-        even = dot(twisted[r, 0], table[step * rows_per_step + r, 0], NT)
-        odd = dot(twisted[r, 1], table[step * rows_per_step + r, 1], NT)
-        for b in range(6):
-            rows, lanes = slice(16 * b, 16 * (b + 1)), slice(256 * b, 256 * (b + 1))
-            left = jnp.where(512 * b + 255 - lane < count, even[rows] + odd[rows], 0.0)
-            for k in range(2 if b < 5 else 1):
-                piece = left[:, 128:] if k == 0 else left[:, :128]
-                turned = jnp.take_along_axis(piece, backward, axis=1).astype(BF16)
-                at = 512 * b + 128 * k
-                grid_field[r, :, at : at + 128] = turned
+        even = dot(twisted[r, 0], table[r, 0], NT)
+        odd = dot(twisted[r, 1], table[r, 1], NT)
+        for b in range(11):
+            rows, lanes = slice(16 * b, 16 * (b + 1)), slice(128 * b, 128 * (b + 1))
+            left = jnp.where(256 * b + 127 - lane < count, even[rows] + odd[rows], 0.0)
+            turned = jnp.take_along_axis(left, backward, axis=1)
+            grid_field[r, :, 256 * b : 256 * b + 128] = turned.astype(BF16)
             left = left.astype(BF16).astype(F32) * factor_left[r, :, lanes]
-            if b < 5:
-                right = jnp.where(512 * b + 256 + lane < count, even[rows] - odd[rows], 0.0)
+            if b < 10:
+                right = jnp.where(256 * b + 128 + lane < count, even[rows] - odd[rows], 0.0)
                 right = right.astype(BF16)
-                grid_field[r, :, 512 * b + 256 : 512 * b + 512] = right
+                grid_field[r, :, 256 * b + 128 : 256 * b + 256] = right
                 right = right.astype(F32) * factor_right[r, :, lanes]
                 samples[r, 0, rows] = (right + left).astype(BF16)
                 samples[r, 1, rows] = (right - left).astype(BF16)
@@ -237,11 +234,11 @@
         for start in range(0, HALF, 256):
             size = min(256, HALF - start)
             lanes = slice(start, start + size)
-            even = dot(samples[r, 0], table[step * rows_per_step + r, 0, :, lanes])
-            odd = dot(samples[r, 1], table[step * rows_per_step + r, 1, :, lanes])
+            even = dot(samples[r, 0], table[r, 0, :, lanes])
+            odd = dot(samples[r, 1], table[r, 1, :, lanes])
             real = jnp.zeros((16, size), F32)
             imag = jnp.zeros((16, size), F32)
-            for b in range(6):
+            for b in range(11):
                 rows = slice(16 * b, 16 * (b + 1))
                 cosine, sine = outer_cos[r, b : b + 1, lanes], outer_sin[r, b : b + 1, lanes]
                 real = real + (even[rows] * cosine - odd[rows] * sine)
@@ -383,14 +380,14 @@
         grid=(NB // per_step,),
         in_specs=[SMEM, SMEM, SMEM, whole((1, HALF))],
         out_specs=[
-            pl.BlockSpec((per_step, 2, 256, HALF), lambda i: (i, 0, 0, 0)),
-            pl.BlockSpec((per_step, 8, HALF), lambda i: (i, 0, 0)),
-            pl.BlockSpec((per_step, 8, HALF), lambda i: (i, 0, 0)),
+            pl.BlockSpec((per_step, 2, 128, HALF), lambda i: (i, 0, 0, 0)),
+            pl.BlockSpec((per_step, 16, HALF), lambda i: (i, 0, 0)),
+            pl.BlockSpec((per_step, 16, HALF), lambda i: (i, 0, 0)),
         ],
         out_shape=[
-            pltpu.VMEM((NB, 2, 256, HALF), BF16),
-            jax.ShapeDtypeStruct((NB, 8, HALF), F32),
-            jax.ShapeDtypeStruct((NB, 8, HALF), F32),
+            pltpu.HBM((NB, 2, 128, HALF), BF16),
+            jax.ShapeDtypeStruct((NB, 16, HALF), F32),
+            jax.ShapeDtypeStruct((NB, 16, HALF), F32),
         ],
         scratch_shapes=[pltpu.VMEM((4, 16, HALF), F32)],
         compiler_params=params(),
@@ -399,9 +396,9 @@
     )(band, row_latitude, points, waves)
 
     per_step = 8
-    factor = jnp.pad(grid_factor, ((0, 0), (0, 3072 - row_width))).reshape(NB, 6, 2, 256).astype(F32)
-    factor_left = factor[:, :, 0, ::-1].reshape(NB, 1, 1536)
-    factor_right = factor[:, :5, 1].reshape(NB, 1, 1280)
+    factor = grid_factor.astype(F32).reshape(NB, row_width // 128, 128)
+    factor_left = factor[:, 0::2, ::-1].reshape(NB, 1, 1408)
+    factor_right = factor[:, 1::2].reshape(NB, 1, 1280)
     grid_field, harmonic = pl.pallas_call(
         lambda *refs: rows_kernel(per_step, *refs),
         grid=(NB // per_step,),
@@ -409,10 +406,10 @@
             SMEM, SMEM, SMEM, SMEM,
             whole((NB, GROUPS, 16, 256)),
             whole((1, HALF)),
-            VMEM,
-            pl.BlockSpec((per_step, 8, HALF), lambda i: (i, 0, 0)),
-            pl.BlockSpec((per_step, 8, HALF), lambda i: (i, 0, 0)),
-            pl.BlockSpec((per_step, 1, 1536), lambda i: (i, 0, 0)),
+            pl.BlockSpec((per_step, 2, 128, HALF), lambda i: (i, 0, 0, 0)),
+            pl.BlockSpec((per_step, 16, HALF), lambda i: (i, 0, 0)),
+            pl.BlockSpec((per_step, 16, HALF), lambda i: (i, 0, 0)),
+            pl.BlockSpec((per_step, 1, 1408), lambda i: (i, 0, 0)),
             pl.BlockSpec((per_step, 1, 1280), lambda i: (i, 0, 0)),
         ],
         out_specs=[
@@ -425,13 +422,13 @@
         ],
         scratch_shapes=[
             pltpu.VMEM((NB, 2, 16, HALF), F32),
-            pltpu.VMEM((per_step, 2, 96, HALF), BF16),
-            pltpu.VMEM((per_step, 2, 96, 256), BF16),
-        ],
-        compiler_params=params(),
+            pltpu.VMEM((per_step, 2, 176, HALF), BF16),
+            pltpu.VMEM((per_step, 2, 176, 128), BF16),
+        ],
+        compiler_params=params(32),
         cost_estimate=cost(4 * 16 * 176 * 1280 * 256, 17_000_000),
         name="grid_rows",
-    )(band, row_latitude, points, cutoffs, received, waves, pltpu.with_memory_space_constraint(table, pltpu.VMEM), outer_cos, outer_sin,
+    )(band, row_latitude, points, cutoffs, received, waves, in_hbm(table), outer_cos, outer_sin,
       factor_left, factor_right)
 
     levels_in = lax.all_to_all(harmonic, "lev", split_axis=0, concat_axis=0, tiled=True)

time: 103 us -> 100 us (0.971)
  local copies, waits for them, and re-layouts: 9.05 us -> 0.98 us
  waiting for transfers between devices: 9.18 us -> 12.7 us
  Pallas kernels: 25.6 us -> 28 us
    unnamed x21 -> x16, local copies, waits for them, and re-layouts: 7.99 us -> 0.03 us
    all_to_all x1, waiting for transfers between devices: 9.18 us -> 12.7 us  [per_device(): lax.all_to_all(message, 'band', split_axis=0, concat_axis=0, tiled=True)]
    pallas_call x1, Pallas kernels: 8.91 us -> 10.7 us  [per_device(): pl.pallas_call(lambda *refs: rows_kernel(per_step, *refs), grid=(NB // pe...]
where the time goes in v8:
time: 100 us
  blocking collectives  47.7 us (48%)
  Pallas kernels  28 us (28%)
  waiting for transfers between devices  12.7 us (13%)
  starting transfers between devices  9.99 us (10%)
    all_to_all x1, blocking collectives, everywhere(): lax.all_to_all(pieces, ('band', 'lev'), split_axis=0, concat_axis=0, tile...  28.5 us
    all_to_all x1, blocking collectives, per_device(): lax.all_to_all(harmonic, 'lev', split_axis=0, concat_axis=0, tiled=True)  19.2 us
    all_to_all x1, waiting for transfers between devices, per_device(): lax.all_to_all(message, 'band', split_axis=0, concat_axis=0, tiled=True)  12.7 us
    pallas_call x1, Pallas kernels, per_device(): pl.pallas_call(lambda *refs: rows_kernel(per_step, *refs), grid=(NB // pe...  10.7 us
    all_to_all x1, starting transfers between devices, per_device(): lax.all_to_all(message, 'band', split_axis=0, concat_axis=0, tiled=True)  9.99 us
    pallas_call x1, Pallas kernels, per_device(): pl.pallas_call(lambda *refs: table_kernel(per_step, *refs), grid=(NB // p...  6.26 us
    pallas_call x1, Pallas kernels, per_device(): pl.pallas_call(lambda *refs: send_kernel(truncation, *refs), in_specs=[SM...  5.35 us
    pallas_call x1, Pallas kernels, per_device(): pl.pallas_call(lambda *refs: final_kernel(truncation, *refs), in_specs=[S...  3.17 us
  transfers between devices with their start and end apart: 1, of which 1 were waited for; matrix products, arithmetic and copies ran while one was open for 1% of the time, Pallas kernels for 6%

profile of v8, /device:TPU:1, one launch (start us, length us, event | category | flops | bytes accessed | tf_op | source)
XLA Modules:
  0.0 100.1 jit_solution(4972782017455403127)
XLA Ops:
  0.6 0.0 copy-start.2
  0.6 0.0 copy-start.7
  0.7 0.0 copy-start.3
  0.7 0.0 copy-start.5
  0.7 0.0 copy-start.6
  0.7 5.3 %legendre_send.1 = bf16[16,5,16,256]{3,2,1,0:T(8,128)(2,1)} custom-call(s32[1]{0:T(128)} %bitcast.refs_0_, s32[320]{0:T(512)} %refs_1_.7, s32[1,256]{1,0:T(1,128)} %bitcast.20, bf16[16,20,2,641]{3,2,1,0:T(2,128)(2,1)} %bitcast.24, bf16[20,641,128]{2,1,0:T(8,128)(2,1)} %bitcast.16), custom_call_target="tpu_custom_call" | custom-call | flops 503316480 | bytes 5000000 | tf_op jit(solution)/shard_map/legendre_send/pallas_call | solution.py:355
  6.0 10.0 %all-to-all-start = ((bf16[16,5,16,256]{3,2,1,0:T(8,128)(2,1)}), bf16[16,5,16,256]{3,2,1,0:T(8,128)(2,1)S(1)}, u32[]{:S(2)}, u32[]{:S(2)}) async-start(bf16[16,5,16,256]{3,2,1,0:T(8,128)(2,1)} %legendre_send.1), calls=%async_computation | async-start | bytes 1310720 | tf_op jit(solution)/shard_map/all_to_all | solution.py:375
  16.0 0.0 copy-done.2
  16.0 0.1 reshape.50
  16.1 0.0 copy-done.7
  16.2 0.1 reshape.59
  16.2 0.1 slice.7
  16.3 0.1 slice.6
  16.4 0.1 copy.15
  16.6 0.1 copy.16
  16.7 0.1 convert_element_type.7.refs_3_.refs_5_
  16.8 0.1 reshape.61.refs_10_
  16.9 0.1 rev.3
  17.0 0.1 reshape.60.refs_9_
  17.1 0.0 copy-done.3
  17.1 0.0 copy-done.5
  17.1 6.3 %phase_tables.1 = (bf16[16,2,128,640]{3,2,1,0:T(8,128)(2,1)}, f32[16,16,640]{2,1,0:T(8,128)S(1)}, f32[16,16,640]{2,1,0:T(8,128)S(1)}) custom-call(s32[1]{0:T(128)} %bitcast.refs_0_, s32[256]{0:T(256)S(1)} %copy-done.3, s32[128]{0:T(128)S(1)} %copy-done.5, f32[1,640]{1,0:T(1,128)S(1)} %convert_element_type.7.refs_3_.refs_5_), custom_call_target="tpu_custom_call" | custom-call | flops 104857600 | bytes 7000000 | tf_op jit(solution)/shard_map/phase_tables/pallas_call | solution.py:378
  23.4 12.7 %all-to-all-done.refs_4_ = bf16[16,5,16,256]{3,2,1,0:T(8,128)(2,1)S(1)} async-done(((bf16[16,5,16,256]{3,2,1,0:T(8,128)(2,1)}), bf16[16,5,16,256]{3,2,1,0:T(8,128)(2,1)S(1)}, u32[]{:S(2)}, u32[]{:S(2)}) %all-to-all-start) | async-done | bytes 655392 | tf_op jit(solution)/shard_map/all_to_all | solution.py:375
  36.1 0.0 copy-done.6
  36.1 0.0 copy-start.1
  36.1 10.7 %grid_rows.1 = (bf16[16,16,2688]{2,1,0:T(8,128)(2,1)}, bf16[16,16,1280]{2,1,0:T(8,128)(2,1)S(1)}) custom-call(s32[1]{0:T(128)} %bitcast.refs_0_, s32[256]{0:T(256)S(1)} %copy-done.3, s32[128]{0:T(128)S(1)} %copy-done.5, s32[128]{0:T(128)S(1)} %copy-done.6, bf16[16,5,16,256]{3,2,1,0:T(8,128)(2,1)S(1)} %all-to-all-done.refs_4_, ...), custom_call_target="tpu_custom_call" | custom-call | flops 3690987520 | bytes 17000000 | tf_op jit(solution)/shard_map/grid_rows/pallas_call | solution.py:402
  46.7 0.0 copy-start
  46.7 0.0 copy-start.4
  46.7 19.2 %all_to_all.15.received = bf16[16,16,1280]{2,1,0:T(8,128)(2,1)S(1)} all-to-all(bf16[16,16,1280]{2,1,0:T(8,128)(2,1)S(1)} %get-tuple-element.11), channel_id=1, replica_groups=mesh['band'=16,'lev'=16] {'lev'}, dimensions={0} | all-to-all | bytes 1310720 | tf_op jit(solution)/shard_map/all_to_all | solution.py:434
  65.9 0.0 copy-done.1
  65.9 2.5 %vertical_mix.1 = bf16[2560,128]{1,0:T(8,128)(2,1)S(1)} custom-call(bf16[256,256]{1,0:T(8,128)(2,1)S(1)} %copy-done.1, bf16[16,16,1280]{2,1,0:T(8,128)(2,1)S(1)} %all_to_all.15.received), custom_call_target="tpu_custom_call" | custom-call | flops 167772160 | bytes 1400000 | tf_op jit(solution)/shard_map/vertical_mix/pallas_call | solution.py:435
  68.4 28.5 %all_to_all.16 = bf16[1280,2,128]{2,1,0:T(2,128)(2,1)S(1)} all-to-all(bf16[1280,2,128]{2,1,0:T(2,128)(2,1)S(1)} %bitcast.19), channel_id=1, replica_groups=mesh['band'=16,'lev'=16] {'band','lev'}, dimensions={0} | all-to-all | bytes 1310720 | tf_op jit(solution)/shard_map/all_to_all | solution.py:338
  96.9 0.0 copy-done
  96.9 0.0 copy-done.4
  96.9 3.2 %legendre_return.1 = f32[16,20,2,641]{3,2,1,0:T(2,128)} custom-call(s32[1]{0:T(128)} %bitcast.refs_0_, s32[320]{0:T(512)S(1)} %copy-done.2, s32[1,256]{1,0:T(1,128)S(1)} %bitcast.21, f32[1,128]{1,0:T(1,128)S(1)} %bitcast.22, bf16[2560,128]{1,0:T(8,128)(2,1)S(1)} %bitcast.18, bf16[20,641,128]{2,1,0:T(8,128)(2,1)S(1)} %bitcast.17), custom_call_target="tpu_custom_call" | custom-call | flops 503316480 | bytes 6000000 | tf_op jit(solution)/shard_map/legendre_return/pallas_call | solution.py:447
  (3 shorter events, 0.0 us)
Async XLA Ops:
  0.6 15.4 %copy-start.2 = (s32[320]{0:T(512)S(1)}, s32[320]{0:T(512)}, u32[]{:S(2)}) copy-start(s32[320]{0:T(512)} %refs_1_.7) | copy-start | bytes 3844
  0.6 15.5 %copy-start.7 = (bf16[16,2688]{1,0:T(8,128)(2,1)S(1)}, bf16[16,2688]{1,0:T(8,128)(2,1)}, u32[]{:S(2)}) copy-start(bf16[16,2688]{1,0:T(8,128)(2,1)} %param.13) | copy-start | bytes 258052
  0.7 16.4 %copy-start.3 = (s32[256]{0:T(256)S(1)}, s32[256]{0:T(256)}, u32[]{:S(2)}) copy-start(s32[256]{0:T(256)} %refs_1_.6) | copy-start | bytes 3076
  0.7 16.4 %copy-start.5 = (s32[128]{0:T(128)S(1)}, s32[128]{0:T(128)}, u32[]{:S(2)}) copy-start(s32[128]{0:T(128)} %refs_2_.3) | copy-start | bytes 1540
  0.7 35.4 %copy-start.6 = (s32[128]{0:T(128)S(1)}, s32[128]{0:T(128)}, u32[]{:S(2)}) copy-start(s32[128]{0:T(128)} %refs_3_.1) | copy-start | bytes 1540
  6.0 30.0 %all-to-all-start = ((bf16[16,5,16,256]{3,2,1,0:T(8,128)(2,1)}), bf16[16,5,16,256]{3,2,1,0:T(8,128)(2,1)S(1)}, u32[]{:S(2)}, u32[]{:S(2)}) async-start(bf16[16,5,16,256]{3,2,1,0:T(8,128)(2,1)} %legendre_send.1), calls=%async_computation | async-start | bytes 1310720 | tf_op jit(solution)/shard_map/all_to_all | solution.py:375
  36.1 29.8 %copy-start.1 = (bf16[256,256]{1,0:T(8,128)(2,1)S(1)}, bf16[256,256]{1,0:T(8,128)(2,1)}, u32[]{:S(2)}) copy-start(bf16[256,256]{1,0:T(8,128)(2,1)} %vertical.1) | copy-start | bytes 393220
  46.7 50.2 %copy-start = (bf16[20,128,641]{1,2,0:T(8,128)(2,1)S(1)}, bf16[20,128,641]{1,2,0:T(8,128)(2,1)}, u32[]{:S(2)}) copy-start(bf16[20,128,641]{1,2,0:T(8,128)(2,1)} %param.10) | copy-start | bytes 9845764
  46.7 50.2 %copy-start.4 = (f32[128]{0:T(128)S(1)}, f32[128]{0:T(128)}, u32[]{:S(2)}) copy-start(f32[128]{0:T(128)} %param.11) | copy-start | bytes 1540
